TPU v7x, 32 devices: a whole 2x2x4 slice. The times are simulated.
32 devices in a mesh: mem: 4 (over z), lat: 4 (over y, x), lon: 2 (over core).
Axes of the slice: x: 2, y: 2, z: 4, core: 2. Of those that a mesh axis runs over, the one named last changes fastest.
Arguments:
- perturbation: bfloat16 [16, 64, 128, 256], P('mem', None, 'lat', 'lon'), may hold values from -6 to 6
- control: bfloat16 [16, 16, 128, 256], P('mem', None, 'lat', 'lon'), may hold values from -6 to 6
- filter_length: float32 [16], replicated, may hold values from 20 to 2000
- modes: float32 [64, 16], replicated, may hold values from -1.5 to 1.5
- obs_weights: bfloat16 [4096, 64], P(('lat', 'lon')), may hold values from -1.5 to 1.5
- innovation: float32 [4096], P(('lat', 'lon')), may hold values from -6 to 6
- obs_tile: int32 [4096, 1], P(('lat', 'lon')), may hold values from 0 to 7; in each aligned block of 512 rows (0 to 511, 512 to 1023, ...) at most 128 rows name the same one
- obs_column: int32 [4096], P(('lat', 'lon')), may hold values from 0 to 16383
- obs_count: int32 [8], P(('lat', 'lon')), may hold values from 64 to 512, as said below
Outputs:
- increment: float32 [64, 128, 256], P('mem', 'lat', 'lon')
- departures: float32 [4096], P(('lat', 'lon'))
Inputs may be any that keep to these rules, and one draw needn't show every extreme that they name: obs_tile names each tile for at most 128 of the 512 slots of one tile, a bound that some block reaches of them. `obs_count`: some tile has all 512 slots live.
All inputs are finite; a program needn't handle non-finite values.
Results may differ from a plain program's by a relative error of at most 0.0003.
Values sent between devices are 32-bit elements; how exact they have to be, the bound alone decides.
No kernel may reach another device: no remote copies, remote signals or barrier semaphores. Data moves between devices by JAX's collectives and lax.ppermute only.
A program may use at most 64 MiB of HBM per device.

v0:
```python
import math

import jax
import jax.numpy as jnp
from jax import lax
from jax.sharding import PartitionSpec as P

HIGH = lax.Precision.HIGHEST


def prefix(part, axis, combine, identity, reverse):
    count = lax.axis_size(axis)
    place = lax.axis_index(axis)
    ahead = count - 1 - place if reverse else place
    gathered = jax.tree.map(lambda a: lax.all_gather(a, axis), part)
    state = jax.tree.map(lambda a, e: jnp.zeros_like(a) + jnp.asarray(e, a.dtype), part, identity)

    def one(hop, state):
        source = count - 1 - hop if reverse else hop
        return combine(
            state, jax.tree.map(lambda a: lax.dynamic_index_in_dim(a, source, 0, False), gathered)
        )

    return lax.fori_loop(0, ahead, one, state)


def with_halo(block, sides, width):
    for axis, dim in sides:
        count = lax.axis_size(axis)
        forward = [(i, i + 1) for i in range(count - 1)]
        backward = [(target, source) for source, target in forward]
        low = lax.ppermute(
            lax.slice_in_dim(block, block.shape[dim] - width, None, axis=dim), axis, forward
        )
        high = lax.ppermute(lax.slice_in_dim(block, 0, width, axis=dim), axis, backward)
        block = jnp.concatenate([low, block, high], axis=dim)
    return block


def filter_matrix(rate, length, backward):
    places = jnp.arange(length)
    if backward:
        spacing = places[None, :] - places[:, None]
    else:
        spacing = places[:, None] - places[None, :]
    inside = spacing >= 0
    powers = jnp.exp(
        jnp.where(inside, spacing, 0).astype(jnp.float32)[None] * jnp.log(rate)[:, None, None]
    )
    return jnp.where(inside[None], (1.0 - rate)[:, None, None] * powers, 0.0)


def carry_factor(rate, length, backward):
    places = jnp.arange(length).astype(jnp.float32)
    steps = length - places if backward else places + 1.0
    return jnp.exp(steps[None, :] * jnp.log(rate)[:, None])


def local_pass(field, rate, dim, backward):
    length = field.shape[dim]
    matrix = filter_matrix(rate, length, backward)
    if dim == 2:
        local = jnp.einsum("kij,mkjy->mkiy", matrix, field, precision=HIGH)
        edge = local[:, :, 0, :] if backward else local[:, :, -1, :]
    else:
        local = jnp.einsum("kij,mkxj->mkxi", matrix, field, precision=HIGH)
        edge = local[:, :, :, 0] if backward else local[:, :, :, -1]
    return (local, edge, jnp.exp(length * jnp.log(rate)))


def settle(local, carry, rate, dim, backward):
    factor = carry_factor(rate, local.shape[dim], backward)
    if dim == 2:
        return local + factor[None, :, :, None] * carry[:, :, None, :]
    return local + factor[None, :, None, :] * carry[:, :, :, None]


def combine(earlier, later):
    return (earlier[0] * later[0], later[0][None, :, None] * earlier[1] + later[1])


def per_device(
    perturbation,
    control,
    filter_length,
    modes,
    obs_weights,
    innovation,
    obs_tile,
    obs_column,
    obs_count,
):
    rate = jnp.exp(-1.0 / filter_length)
    boost = (1.0 + rate) / (1.0 - rate)
    field = control.astype(jnp.float32) * boost[None, :, None, None]
    unity = jnp.ones_like(rate)
    local, edge, whole_power = local_pass(field, rate, 2, False)
    carried = prefix((whole_power, edge), "lat", combine, (unity, jnp.zeros_like(edge)), False)
    field = settle(local, carried[1], rate, 2, False)
    local, edge, whole_power = local_pass(field, rate, 2, True)
    carried = prefix((whole_power, edge), "lat", combine, (unity, jnp.zeros_like(edge)), True)
    field = settle(local, carried[1], rate, 2, True)
    local, edge, whole_power = local_pass(field, rate, 3, False)
    carried = prefix((whole_power, edge), "lon", combine, (unity, jnp.zeros_like(edge)), False)
    field = settle(local, carried[1], rate, 3, False)
    local, edge, whole_power = local_pass(field, rate, 3, True)
    carried = prefix((whole_power, edge), "lon", combine, (unity, jnp.zeros_like(edge)), True)
    field = settle(local, carried[1], rate, 3, True)
    member_count, levels, rows_tile, cols_tile = perturbation.shape
    modes_count = control.shape[1]
    flat_field = field.reshape(member_count, modes_count, rows_tile * cols_tile)
    flat_pert = perturbation.reshape(member_count, levels, rows_tile * cols_tile)
    scaling = 1.0 / math.sqrt(member_count * lax.axis_size("mem") - 1)
    share = levels // lax.axis_size("mem")
    first_level = lax.axis_index("mem") * share
    profile = jnp.einsum("zk,mkp->mzp", modes, flat_field, precision=HIGH)
    total = lax.psum(jnp.sum(flat_pert * profile, axis=0) * scaling, "mem")
    owned = lax.dynamic_slice_in_dim(total, first_level, share, 0)
    weights_used = obs_weights.astype(jnp.float32)
    increment = owned.reshape(share, rows_tile, cols_tile)
    depth = total.shape[0]
    padded = with_halo(total.reshape(depth, rows_tile, cols_tile), (("lat", 1), ("lon", 2)), 1)
    flat_padded = padded.reshape(depth, (rows_tile + 2) * (cols_tile + 2))
    slots_dev = innovation.shape[0]
    tiles = lax.axis_size(("lat", "lon"))
    capacity = 2 * slots_dev // tiles
    target = obs_tile[:, 0]
    marks = (target[:, None] == jnp.arange(tiles, dtype=jnp.int32)[None, :]).astype(jnp.int32)
    ranking = jnp.sum(jnp.cumsum(marks, axis=0) * marks, axis=1) - 1
    valid = jnp.arange(slots_dev, dtype=jnp.int32) < obs_count[0]
    weight_send = (
        jnp.zeros((tiles, capacity, depth), jnp.float32)
        .at[target, ranking]
        .set(jnp.where(valid[:, None], weights_used, 0.0))
    )
    column_send = (
        jnp.zeros((tiles, capacity), jnp.float32)
        .at[target, ranking]
        .set(obs_column.astype(jnp.float32))
    )
    weights_in = lax.all_to_all(
        weight_send, ("lat", "lon"), split_axis=0, concat_axis=0, tiled=True
    )
    columns_in = lax.all_to_all(
        column_send, ("lat", "lon"), split_axis=0, concat_axis=0, tiled=True
    )
    column_ids = columns_in.astype(jnp.int32)
    fine_row = column_ids // (2 * cols_tile)
    fine_col = column_ids % (2 * cols_tile)
    near_row = fine_row // 2 + 1
    far_row = near_row + 2 * (fine_row % 2) - 1
    near_col = fine_col // 2 + 1
    far_col = near_col + 2 * (fine_col % 2) - 1
    stride = cols_tile + 2
    blend = (
        0.5625 * flat_padded[:, near_row * stride + near_col]
        + 0.1875 * flat_padded[:, far_row * stride + near_col]
        + 0.1875 * flat_padded[:, near_row * stride + far_col]
        + 0.0625 * flat_padded[:, far_row * stride + far_col]
    )
    values = jnp.einsum("tcz,ztc->tc", weights_in, blend, precision=HIGH)
    returned = lax.all_to_all(values, ("lat", "lon"), split_axis=0, concat_axis=0, tiled=True)
    equivalent = returned[target, ranking]
    departures = jnp.where(valid, innovation - equivalent, 0.0)
    return (increment, departures)


def solution(mesh):
    placed = (
        P("mem", None, "lat", "lon"),
        P("mem", None, "lat", "lon"),
        P(),
        P(),
        P(("lat", "lon"), None),
        P(("lat", "lon")),
        P(("lat", "lon"), None),
        P(("lat", "lon")),
        P(("lat", "lon")),
    )
    return jax.shard_map(
        per_device,
        mesh=mesh,
        in_specs=placed,
        out_specs=(P("mem", "lat", "lon"), P(("lat", "lon"))),
        check_vma=False,
    )
```

profile of v0, /device:TPU:0, one launch (start us, length us, event | category | flops | bytes accessed | tf_op | source)
XLA Modules:
  0.0 240.4 jit_solution(1848255504214207811)
XLA Ops:
  7.4 1.2 dynamic-slice.1
  8.7 1.2 dynamic-slice
  11.2 0.8 exponential_dynamic-update-slice_fusion
  12.1 2.3 convolution_bitcast_fusion.4
  14.4 9.9 %all-gather.1 = f32[16,16,1,128]{3,2,0,1:T(1,128)S(1)} all-gather(f32[4,16,1,128]{3,2,0,1:T(1,128)S(1)} %slice.54), channel_id=3, replica_groups=mesh['mem'=4,'lat'=4,'lon'=2] {'lat'}, dimensions={0}, use_global_device_ids=true | all-gather | bytes 163840 | tf_op jit(solution)/shard_map/all_gather | solution.py:15
  24.3 8.9 %all-reduce = f32[64]{0:T(128)S(1)} all-reduce(f32[64]{0:T(128)S(1)} %get-tuple-element.374), channel_id=2, replica_groups=mesh['mem'=4,'lat'=4,'lon'=2] {'lat'}, use_global_device_ids=true, to_apply=%add | all-reduce | flops 64 | bytes 512
  33.4 1.2 convolution_bitcast_fusion.3
  34.7 8.6 %all-gather.2 = f32[16,16,1,128]{3,2,0,1:T(1,128)S(1)} all-gather(f32[4,16,1,128]{3,2,0,1:T(1,128)S(1)} %slice.55), channel_id=4, replica_groups=mesh['mem'=4,'lat'=4,'lon'=2] {'lat'}, dimensions={0}, use_global_device_ids=true | all-gather | bytes 163840 | tf_op jit(solution)/shard_map/all_gather | solution.py:15
  43.7 2.5 %convolution_bitcast_fusion.2 = f32[4,16,32,128]{3,2,0,1:T(8,128)S(1)} fusion(f32[4,16,32,128]{3,2,0,1:T(8,128)S(1)} %convolution_bitcast_fusion.3, f32[16]{0:T(128)S(1)} %get-tuple-element.375, f32[128,128]{1,0:T(8,128)S(1)} %select_convert_fusion.1, f32[16]{0:T(128)S(1)} %get-tuple-element.376, f32[4,16,128]{2,0,1:T(4,128)S(1)} %copy.60, ...), kind=kOutput, calls=%fused_computation.24 | convolution fusion | flops 403963904 | bytes 2214016 | tf_op jit(solution)/shard_map/kij,mkxj->mkxi/dot_general | solution.py:66
  46.6 3.3 %all-gather.4 = f32[8,16,32,1]{3,2,0,1:T(8,128)S(1)} all-gather(f32[4,16,32,1]{3,2,0,1:T(8,128)S(1)} %slice.56), channel_id=6, replica_groups=mesh['mem'=4,'lat'=4,'lon'=2] {'lon'}, dimensions={0}, use_global_device_ids=true | all-gather | bytes 24576 | tf_op jit(solution)/shard_map/all_gather | solution.py:15
  49.9 0.8 copy.61
  50.7 2.5 %all-reduce.1 = f32[32]{0:T(128)S(1)} all-reduce(f32[32]{0:T(128)S(1)} %get-tuple-element.358), channel_id=5, replica_groups=mesh['mem'=4,'lat'=4,'lon'=2] {'lon'}, use_global_device_ids=true, to_apply=%add.1 | all-reduce | flops 32 | bytes 256
  53.3 2.5 %convolution_bitcast_fusion.1 = f32[4,16,32,128]{3,2,0,1:T(8,128)S(1)} fusion(f32[4,16,32,128]{3,2,0,1:T(8,128)S(1)} %convolution_bitcast_fusion.2, f32[128,128]{1,0:T(8,128)S(1)} %select_convert_fusion, f32[4,16,32]{2,0,1:T(4,128)S(1)} %copy.62, f32[16,128]{1,0:T(8,128)S(1)} %get-tuple-element.371, f32[16]{0:T(128)S(1)} %get-tuple-element.375, ...), kind=kOutput, calls=%fused_computation.23 | convolution fusion | flops 403963904 | bytes 2195584 | tf_op jit(solution)/shard_map/kij,mkxj->mkxi/dot_general | solution.py:66
  55.9 3.3 %all-gather.5 = f32[8,16,32,1]{3,2,0,1:T(8,128)S(1)} all-gather(f32[4,16,32,1]{3,2,0,1:T(8,128)S(1)} %bitcast.141), channel_id=7, replica_groups=mesh['mem'=4,'lat'=4,'lon'=2] {'lon'}, dimensions={0}, use_global_device_ids=true | all-gather | bytes 24576 | tf_op jit(solution)/shard_map/all_gather | solution.py:15
  59.2 0.8 copy.63
  60.6 0.4 reshape.593
  61.0 4.5 %reshape.598 = f32[4,64,4096]{2,1,0:T(8,128)} reshape(bf16[4,64,32,128]{3,2,1,0:T(8,128)(2,1)} %param.17) | data formatting | bytes 6291456 | tf_op jit(solution)/shard_map/convert_element_type | solution.py:117
  65.5 5.5 %fusion.3 = f32[64,4096]{1,0:T(8,128)S(1)} fusion(f32[4,64,4096]{2,1,0:T(8,128)} %reshape.598, f32[4,16,4096]{2,0,1:T(4,128)S(1)} %reshape.593, f32[64,16]{0,1:T(8,128)S(1)} %copy-done), kind=kOutput, calls=%fused_computation.22 | convolution fusion | flops 203161600 | bytes 6295552 | tf_op jit(solution)/shard_map/zk,mkp->mzp/dot_general | solution.py:116
  71.0 1.1 broadcast_multiply_fusion
  72.1 1.1 reduce-window.6
  73.6 0.6 broadcast_in_dim.74
  74.2 76.5 %scatter_fusion.1 = f32[8,128]{1,0:T(8,128)} fusion(f32[8,128]{1,0:T(8,128)} %broadcast_in_dim.74, s32[512]{0:T(512)S(1)} %bitcast.135, f32[512]{0:T(512)S(1)} %convert_element_type.110), kind=kCustom, calls=%fused_computation.6 | custom fusion | bytes 10240 | tf_op jit(solution)/shard_map/scatter | solution.py:139
  150.8 3.3 %all-to-all-start.1 = ((f32[8,1,128]{2,1,0:T(1,128)}), f32[8,1,128]{2,1,0:T(1,128)S(1)}, u32[]{:S(2)}, u32[]{:S(2)}) async-start(f32[8,1,128]{2,1,0:T(1,128)} %bitcast.38), calls=%async_computation.1 | async-start | bytes 8192 | tf_op jit(solution)/shard_map/all_to_all | solution.py:144
  155.0 24.6 %scatter_fusion = f32[8,128,64]{2,1,0:T(8,128)S(1)} fusion(f32[8,128,64]{2,1,0:T(8,128)S(1)} %broadcast_in_dim.71, s32[512]{0:T(512)S(1)} %bitcast.136, f32[512,64]{1,0:T(8,128)S(1)} %copy.66), kind=kCustom, calls=%fused_computation.5 | custom fusion | bytes 397312 | tf_op jit(solution)/shard_map/scatter | solution.py:134
  179.6 0.9 copy.67
  180.5 4.1 %all-to-all-start = ((f32[8,128,64]{1,2,0:T(8,128)}), f32[8,128,64]{1,2,0:T(8,128)S(1)}, u32[]{:S(2)}, u32[]{:S(2)}) async-start(f32[8,128,64]{1,2,0:T(8,128)} %copy.67), calls=%async_computation | async-start | bytes 524288 | tf_op jit(solution)/shard_map/all_to_all | solution.py:141
  184.6 1.8 copy.87
  186.5 3.9 %collective-permute-start = (f32[64,1,128]{0,2,1:T(8,128)S(1)}, f32[64,1,128]{0,2,1:T(8,128)S(1)}, u32[]{:S(2)}, u32[]{:S(2)}) collective-permute-start(f32[64,1,128]{0,2,1:T(8,128)S(1)} %get-tuple-element.362), channel_id=1, source_target_pairs={{0,2},{2,4},{4,6},{1,3},{3,5},{5,7},{8,10},{10,12},{12,14},{9,11},... | collective-permute-start | bytes 98312 | tf_op jit(solution)/shard_map/ppermute | solution.py:32
  190.4 1.3 collective-permute-start.1
  191.8 0.5 collective-permute-done
  192.3 4.3 %collective-permute-done.1 = f32[64,1,128]{0,2,1:T(8,128)S(1)} collective-permute-done((f32[64,1,128]{0,2,1:T(8,128)S(1)}, f32[64,1,128]{0,2,1:T(8,128)S(1)}, u32[]{:S(2)}, u32[]{:S(2)}) %collective-permute-start.1) | collective-permute-done | bytes 32800 | tf_op jit(solution)/shard_map/ppermute | solution.py:35
  196.6 1.3 collective-permute-start.2
  197.9 1.3 collective-permute-start.3
  199.5 1.5 collective-permute-done.3
  201.0 1.7 pad_maximum_fusion
  202.7 2.3 reshape.688
  205.0 2.8 %gather_fusion = f32[1024,64]{1,0:T(8,128)S(1)} fusion(f32[64,4420]{0,1:T(8,128)S(1)} %reshape.688, s32[1024]{0:T(1024)S(1)} %get-tuple-element.365), kind=kCustom, calls=%fused_computation | custom fusion | bytes 528384 | tf_op jit(solution)/shard_map/gather | solution.py:156
  207.9 4.0 %gather_fusion.1 = f32[1024,64]{1,0:T(8,128)} fusion(f32[64,4420]{0,1:T(8,128)S(1)} %reshape.688, s32[1024]{0:T(1024)S(1)} %get-tuple-element.366), kind=kCustom, calls=%fused_computation.1 | custom fusion | bytes 528384 | tf_op jit(solution)/shard_map/gather | solution.py:157
  211.9 4.0 %gather_fusion.2 = f32[1024,64]{1,0:T(8,128)} fusion(f32[64,4420]{0,1:T(8,128)S(1)} %reshape.688, s32[1024]{0:T(1024)S(1)} %get-tuple-element.354), kind=kCustom, calls=%fused_computation.2 | custom fusion | bytes 528384 | tf_op jit(solution)/shard_map/gather | solution.py:158
  215.9 4.0 %gather_fusion.3 = f32[1024,64]{1,0:T(8,128)} fusion(f32[64,4420]{0,1:T(8,128)S(1)} %reshape.688, s32[1024]{0:T(1024)S(1)} %fusion.81), kind=kCustom, calls=%fused_computation.3 | custom fusion | bytes 528384 | tf_op jit(solution)/shard_map/gather | solution.py:159
  219.9 1.5 add_add_fusion
  221.4 0.8 multiply_reduce_fusion
  222.2 3.6 %all-to-all-start.2 = ((f32[8,1,128]{2,1,0:T(1,128)}), f32[8,1,128]{2,1,0:T(1,128)S(1)}, u32[]{:S(2)}, u32[]{:S(2)}) async-start(f32[8,1,128]{2,1,0:T(1,128)} %bitcast.48), calls=%async_computation.2 | async-start | bytes 8192 | tf_op jit(solution)/shard_map/all_to_all | solution.py:162
  225.9 1.0 dynamic-slice_bitcast_fusion.4
  226.8 0.8 copy.90
  227.6 2.9 %all-to-all-done.2 = f32[8,1,128]{2,1,0:T(1,128)S(1)} async-done(((f32[8,1,128]{2,1,0:T(1,128)}), f32[8,1,128]{2,1,0:T(1,128)S(1)}, u32[]{:S(2)}, u32[]{:S(2)}) %all-to-all-start.2) | async-done | bytes 4128 | tf_op jit(solution)/shard_map/all_to_all | solution.py:162
  230.5 2.5 %gather_fusion.4 = f32[512]{0:T(512)S(1)} fusion(f32[8,128]{1,0:T(8,128)S(1)} %bitcast.134, s32[512]{0:T(512)S(1)} %bitcast.137), kind=kCustom, calls=%fused_computation.4 | custom fusion | bytes 8192 | tf_op jit(solution)/shard_map/gather | solution.py:163
  233.0 0.6 subtract_select_fusion
  (78 shorter events, 3.3 us)
Async XLA Ops:
  7.2 58.3 %copy-start = (f32[64,16]{0,1:T(8,128)S(1)}, f32[64,16]{0,1:T(8,128)}, u32[]{:S(2)}) copy-start(f32[64,16]{0,1:T(8,128)} %param.20) | copy-start | bytes 12292
  7.2 177.5 %all-reduce.4.cloned.1.call-start = ((), (), s32[]{:S(2)}) async-start(), calls=%async_computation.3 | async-start | bytes 2097152 | tf_op jit(solution)/shard_map/psum | solution.py:117
  71.0 1.1 copy-start.2
  71.0 2.5 %copy-start.3 = (s32[512]{0:T(512)S(1)}, s32[512]{0:T(512)}, u32[]{:S(2)}) copy-start(s32[512]{0:T(512)} %param.24) | copy-start | bytes 6148
  72.1 82.7 %copy-start.1 = (bf16[512,64]{0,1:T(8,128)(2,1)S(1)}, bf16[512,64]{0,1:T(8,128)(2,1)}, u32[]{:S(2)}) copy-start(bf16[512,64]{0,1:T(8,128)(2,1)} %param.21) | copy-start | bytes 196612
  150.8 29.7 %all-to-all-start.1 = ((f32[8,1,128]{2,1,0:T(1,128)}), f32[8,1,128]{2,1,0:T(1,128)S(1)}, u32[]{:S(2)}, u32[]{:S(2)}) async-start(f32[8,1,128]{2,1,0:T(1,128)} %bitcast.38), calls=%async_computation.1 | async-start | bytes 8192 | tf_op jit(solution)/shard_map/all_to_all | solution.py:144
  180.5 18.8 %all-to-all-start = ((f32[8,128,64]{1,2,0:T(8,128)}), f32[8,128,64]{1,2,0:T(8,128)S(1)}, u32[]{:S(2)}, u32[]{:S(2)}) async-start(f32[8,128,64]{1,2,0:T(8,128)} %copy.67), calls=%async_computation | async-start | bytes 524288 | tf_op jit(solution)/shard_map/all_to_all | solution.py:141
  186.5 5.8 %collective-permute-start = (f32[64,1,128]{0,2,1:T(8,128)S(1)}, f32[64,1,128]{0,2,1:T(8,128)S(1)}, u32[]{:S(2)}, u32[]{:S(2)}) collective-permute-start(f32[64,1,128]{0,2,1:T(8,128)S(1)} %get-tuple-element.362), channel_id=1, source_target_pairs={{0,2},{2,4},{4,6},{1,3},{3,5},{5,7},{8,10},{10,12},{12,14},{9,11},... | collective-permute-start | bytes 98312 | tf_op jit(solution)/shard_map/ppermute | solution.py:32
  190.4 6.2 %collective-permute-start.1 = (f32[64,1,128]{0,2,1:T(8,128)S(1)}, f32[64,1,128]{0,2,1:T(8,128)S(1)}, u32[]{:S(2)}, u32[]{:S(2)}) collective-permute-start(f32[64,1,128]{0,2,1:T(8,128)S(1)} %get-tuple-element.363), channel_id=1, source_target_pairs={{2,0},{4,2},{6,4},{3,1},{5,3},{7,5},{10,8},{12,10},{14,12},{11,9},... | collective-permute-start | bytes 98312 | tf_op jit(solution)/shard_map/ppermute | solution.py:35
  196.6 2.8 %collective-permute-start.2 = (f32[64,34,1]{0,2,1:T(1,128)S(1)}, f32[64,34,1]{0,2,1:T(1,128)S(1)}, u32[]{:S(2)}, u32[]{:S(2)}) collective-permute-start(f32[64,34,1]{0,2,1:T(1,128)S(1)} %get-tuple-element.360), channel_id=1, source_target_pairs={{0,1},{2,3},{4,5},{6,7},{8,9},{10,11},{12,13},{14,15},{16,17},{18,... | collective-permute-start | bytes 26120 | tf_op jit(solution)/shard_map/ppermute | solution.py:32
  197.9 3.1 %collective-permute-start.3 = (f32[64,34,1]{0,2,1:T(1,128)S(1)}, f32[64,34,1]{0,2,1:T(1,128)S(1)}, u32[]{:S(2)}, u32[]{:S(2)}) collective-permute-start(f32[64,34,1]{0,2,1:T(1,128)S(1)} %get-tuple-element.361), channel_id=1, source_target_pairs={{1,0},{3,2},{5,4},{7,6},{9,8},{11,10},{13,12},{15,14},{17,16},{19,... | collective-permute-start | bytes 26120 | tf_op jit(solution)/shard_map/ppermute | solution.py:35
  221.4 11.6 %copy-start.4 = (f32[512]{0:T(512)S(1)}, f32[512]{0:T(512)}, u32[]{:S(2)}) copy-start(f32[512]{0:T(512)} %param.22) | copy-start | bytes 6148
  222.2 8.3 %all-to-all-start.2 = ((f32[8,1,128]{2,1,0:T(1,128)}), f32[8,1,128]{2,1,0:T(1,128)S(1)}, u32[]{:S(2)}, u32[]{:S(2)}) async-start(f32[8,1,128]{2,1,0:T(1,128)} %bitcast.48), calls=%async_computation.2 | async-start | bytes 8192 | tf_op jit(solution)/shard_map/all_to_all | solution.py:162
Sparse Core Ops, SparseCore 0:
  72.2 51.7 all-reduce.3
where the time goes:
time: 243 us; the launch traced here: 240 us
  local copies, waits for them, and re-layouts  136 us (56%)
  blocking collectives  36.5 us (15%)
  starting transfers between devices  18.9 us (8%)
  between operations  16.4 us (7%)
  matrix products  14 us (6%)
  waiting for transfers between devices  9.33 us (4%)
  other arithmetic  8.8 us (4%)
    scatter x1, local copies, waits for them, and re-layouts, per_device(): column_send = jnp.zeros((tiles, capacity), jnp.float32).at[target, rankin...  76.5 us
    scatter x2, local copies, waits for them, and re-layouts, per_device(): weight_send = jnp.zeros((tiles, capacity, depth), jnp.float32).at[target,...  25.5 us
    all_gather x4, blocking collectives, prefix(): gathered = jax.tree.map(lambda a: lax.all_gather(a, axis), part)  25.1 us
    unnamed x2, blocking collectives  11.4 us
    ppermute x2, waiting for transfers between devices, with_halo(): lax.ppermute(lax.slice_in_dim(block, 0, width, axis=dim), axis, backward)  5.81 us
    dot_general x1, matrix products, per_device(): profile = jnp.einsum('zk,mkp->mzp', modes, flat_field, precision=HIGH)  5.49 us
    ppermute x2, starting transfers between devices, with_halo(): lax.ppermute(lax.slice_in_dim(block, block.shape[dim] - width, None, axis...  5.22 us
    dot_general x2, matrix products, local_pass(): local = jnp.einsum('kij,mkxj->mkxi', matrix, field, precision=HIGH)  5.07 us
  transfers between devices with their start and end apart: 8, of which 4 were waited for; matrix products, arithmetic and copies ran while one was open for 45% of the time, Pallas kernels for 0%

commit v1 on v0

v1 whole, which is shorter than its diff:
```python
import functools
import math

import jax
import jax.numpy as jnp
from jax import lax
from jax.experimental import pallas as pl
from jax.experimental.pallas import tpu as pltpu
from jax.sharding import PartitionSpec as P

F32, BF16 = jnp.float32, jnp.bfloat16
VMEM = pl.BlockSpec(memory_space=pltpu.VMEM)
SMEM = pl.BlockSpec(memory_space=pltpu.SMEM)


def params(flops, moved):
    return dict(
        compiler_params=pltpu.CompilerParams(vmem_limit_bytes=48 * 2**20),
        cost_estimate=pl.CostEstimate(flops=flops, bytes_accessed=moved, transcendentals=0),
    )


def paired(count):
    return count & (count - 1) == 0


def toward(place, step, count):
    return place ^ step if paired(count) else (place + step) % count


def source(place, step, count):
    return place ^ step if paired(count) else (place - step) % count


def send(block, axis, step):
    count = lax.axis_size(axis)
    return lax.ppermute(block, axis, [(i, toward(i, step, count)) for i in range(count)])


def collect(block, axis):
    count = lax.axis_size(axis)
    blocks = block[None]
    if not paired(count):
        return jnp.concatenate([blocks] + [send(blocks, axis, s) for s in range(1, count)])
    step = 1
    while step < count:
        blocks = jnp.concatenate([blocks, send(blocks, axis, step)])
        step *= 2
    return blocks


def halve(value):
    high = value.astype(BF16)
    return high, (value - high.astype(F32)).astype(BF16)


def columns_kernel(own_ref, other_ref, matrix_ref, decay_ref, field_ref, edge_ref, first):
    members, modes, rows, cols = own_ref.shape
    sources = matrix_ref.shape[0]
    lines = members * modes
    for k in range(modes):
        pieces = [jnp.concatenate([own_ref[m, k] for m in range(members)])]
        for s in range(1, sources):
            pieces.append(
                jnp.concatenate([other_ref[s - 1, m, k] for m in range(members)]).astype(BF16)
            )
        split = [halve(matrix_ref[s, k]) for s in range(sources)]
        weights = jnp.concatenate(
            [jnp.concatenate([high, low], axis=1) for high, low in split], axis=0
        )
        both = jnp.dot(jnp.concatenate(pieces, axis=1), weights, preferred_element_type=F32)
        made = both[:, :cols] + both[:, cols:]
        for m in range(members):
            field_ref[pl.ds(m * modes + k, rows, stride=lines), :] = made[m * rows : (m + 1) * rows]
    decay = decay_ref[...]
    state = jnp.zeros((lines, cols), F32)
    for x in range(rows):
        state = decay * state + field_ref[x * lines : (x + 1) * lines, :]
        first[x * lines : (x + 1) * lines, :] = state
    edge_ref[0] = state
    state = jnp.zeros((lines, cols), F32)
    for x in reversed(range(rows)):
        state = decay * state + first[x * lines : (x + 1) * lines, :]
    edge_ref[1] = state


def sum_kernel(
    places_ref, chunks_ref, table_ref, edges_ref, field_ref, modes_ref, pert_ref, *rest
):
    chunks = len(rest) - 3
    outs, (first, second, pert) = rest[:chunks], rest[chunks:]
    members, levels, rows, cols = pert_ref.shape
    lines = table_ref.shape[1]
    share = levels // chunks
    count = edges_ref.shape[0]

    for m in range(members):
        for z in range(levels):
            at = (m * levels + z) * rows
            pert[at : at + rows, :] = pert_ref[m, z].astype(F32)

    log, decay, beta = table_ref[0], table_ref[1], table_ref[2]

    def power(ahead):
        exponent = (rows * jnp.maximum(ahead, 0)).astype(F32)
        return jnp.where(ahead >= 0, jnp.exp(log * exponent), 0.0)

    own = places_ref[0]
    state = jnp.zeros((lines, cols), F32)
    after = jnp.zeros((lines, cols), F32)
    for s in range(count):
        there = places_ref[s]
        state = state + power(own - there - 1) * edges_ref[s, 0]
        before = jnp.zeros((lines, cols), F32)
        for t in range(count):
            before = before + power(there - places_ref[t] - 1) * edges_ref[t, 0]
        after = after + power(there - own - 1) * (edges_ref[s, 1] + beta * before)

    for x in range(rows):
        state = decay * state + field_ref[x * lines : (x + 1) * lines, :]
        first[x * lines : (x + 1) * lines, :] = state
    state = after
    for x in reversed(range(rows)):
        state = decay * state + first[x * lines : (x + 1) * lines, :]
        high, low = halve(state)
        second[:, x * cols : (x + 1) * cols] = jnp.concatenate([high, low, high])

    for pair in range(0, rows, 2):
        profile = jnp.dot(
            modes_ref[...],
            second[:, pair * cols : (pair + 2) * cols],
            preferred_element_type=F32,
        )
        for half in range(2):
            x = pair + half
            for r in range(chunks):
                total = None
                for m in range(members):
                    at = (m * levels + chunks_ref[r] * share) * rows + x
                    line = m * levels + r * share
                    term = (
                        profile[line : line + share, half * cols : (half + 1) * cols]
                        * pert[pl.ds(at, share, stride=rows), :]
                    )
                    total = term if total is None else total + term
                outs[r][pl.ds(x, share, stride=rows), :] = total


def observe_kernel(levels, rows, chunks_ref, spots_ref, origin_ref, packed_ref, *rest):
    chunks = len(rest) - 2
    sums, out_ref, split = rest[:chunks], rest[chunks], rest[chunks + 1]
    blocks, _, slots = packed_ref.shape
    step, cols = sums[0].shape
    for r in range(chunks):
        high, low = halve(sums[r][...])
        at = pl.multiple_of(chunks_ref[r] * step, step)
        split[pl.ds(at, step), :] = jnp.concatenate([high, low], axis=1)

    def spread(fine, origin, length):
        near = jnp.floor(fine * 0.5)
        far = near - 1.0 + 2.0 * (fine - 2.0 * near)
        cell = (lax.broadcasted_iota(jnp.int32, (length, slots), 0) + origin).astype(F32)
        return jnp.where(cell == near, 0.75, 0.0) + jnp.where(cell == far, 0.25, 0.0)

    group = math.gcd(levels, 16)

    @pl.loop(0, blocks)
    def _(block):
        fine = packed_ref[block, levels : levels + 8, :]
        across = spread(fine[1:2], origin_ref[1], cols).astype(BF16)
        across = jnp.concatenate([across, across])
        down = spread(fine[0:1], origin_ref[0], rows)
        total = jnp.zeros((rows, slots), F32)
        for g in range(0, levels, group):
            seen = jnp.dot(
                split[g * rows : (g + group) * rows, :], across, preferred_element_type=F32
            )
            weights = packed_ref[block, g : g + group, :]
            for z in range(group):
                total = total + seen[z * rows : (z + 1) * rows] * weights[z : z + 1]
        out_ref[pl.ds(spots_ref[block], 1), :] = jnp.sum(total * down, axis=0, keepdims=True)


def per_device(
    perturbation,
    control,
    filter_length,
    modes,
    obs_weights,
    innovation,
    obs_tile,
    obs_column,
    obs_count,
):
    members, levels, rows, cols = perturbation.shape
    kinds = control.shape[1]
    lines = members * kinds
    n_mem, n_lat, n_lon = (lax.axis_size(a) for a in ("mem", "lat", "lon"))
    mem, lat, lon = (lax.axis_index(a) for a in ("mem", "lat", "lon"))
    slots = innovation.shape[0]
    share = levels // n_mem
    all_cols = cols * n_lon

    rate = jnp.exp(-1.0 / filter_length)
    rest = 1.0 - rate
    log = jnp.log1p(-rest)
    beta = rate * jnp.expm1(2.0 * rows * log) / jnp.expm1(2.0 * log)
    table = jnp.broadcast_to(
        jnp.tile(jnp.stack([log, rate, beta]), (1, members))[:, :, None], (3, lines, cols)
    )
    to_col = (lon * cols + jnp.arange(cols))[None, None, None, :]
    lons = jnp.stack([source(lon, s, n_lon) for s in range(n_lon)])
    from_col = (lons[:, None] * cols + jnp.arange(cols)[None, :])[:, None, :, None]
    log4 = log[None, :, None, None]
    reach = (all_cols - jnp.maximum(to_col, from_col)).astype(F32)
    matrix = (
        (rest * rest)[None, :, None, None]
        * jnp.exp(jnp.abs(to_col - from_col).astype(F32) * log4)
        * -jnp.expm1(2.0 * reach * log4)
    )

    valid = jnp.arange(slots, dtype=jnp.int32) < obs_count[0]
    target = obs_tile[:, 0]
    fine_row = target // n_lon * (2 * rows) + obs_column // (2 * cols)
    fine_col = target % n_lon * (2 * cols) + obs_column % (2 * cols)
    weights = jnp.where(valid[:, None], obs_weights.astype(F32), 0.0).T
    places = jnp.stack([fine_row, fine_col]).astype(F32)
    packed = jnp.concatenate([weights, places, jnp.zeros((6, slots), F32)])

    whole = control.astype(F32)
    others = [send(whole, "lon", s) for s in range(1, n_lon)]
    others = jnp.stack(others) if others else jnp.zeros((1,) + whole.shape, F32)
    field, edge = pl.pallas_call(
        columns_kernel,
        out_shape=(
            jax.ShapeDtypeStruct((rows * lines, cols), F32),
            jax.ShapeDtypeStruct((2, lines, cols), F32),
        ),
        in_specs=[VMEM] * 4,
        out_specs=(VMEM, VMEM),
        scratch_shapes=[pltpu.VMEM((rows * lines, cols), F32)],
        **params(2 * 2 * lines * rows * cols * all_cols, 4 * 2**20),
    )(control, others, matrix, table[1])

    edges = collect(edge, "lat")
    packed = collect(packed, "lat")
    packed = collect(packed, "lon").reshape((n_lat * n_lon,) + packed.shape[1:])
    lats = jnp.stack([source(lat, s, n_lat) for s in range(n_lat)]).astype(jnp.int32)
    chunks = jnp.stack([toward(mem, r, n_mem) for r in range(n_mem)]).astype(jnp.int32)
    scaled = modes * (1.0 / math.sqrt(members * n_mem - 1))
    scaled = jnp.concatenate(
        [lax.dynamic_slice_in_dim(scaled, toward(mem, r, n_mem) * share, share) for r in range(n_mem)]
    )
    spread = (
        jnp.eye(members, dtype=F32)[:, None, :, None] * scaled[None, :, None, :]
    ).reshape(members * levels, lines)
    high = lax.reduce_precision(spread, 8, 7)
    spread = jnp.concatenate([high, high, spread - high], axis=1).astype(BF16)
    chunk_shape = jax.ShapeDtypeStruct((share * rows, cols), F32)
    sums = pl.pallas_call(
        sum_kernel,
        out_shape=(chunk_shape,) * n_mem,
        in_specs=[SMEM, SMEM] + [VMEM] * 5,
        out_specs=(VMEM,) * n_mem,
        scratch_shapes=[
            pltpu.VMEM((rows * lines, cols), F32),
            pltpu.VMEM((3 * lines, rows * cols), BF16),
            pltpu.VMEM((members * levels * rows, cols), F32),
        ],
        **params(6 * members * levels * lines * rows * cols, 6 * 2**20),
    )(lats, chunks, table, edges, field, spread, perturbation)

    held = list(sums)
    if paired(n_mem):
        step = 1
        while step < n_mem:
            for r in reversed(range(step, n_mem, 2 * step)):
                held[r ^ step] = held[r ^ step] + send(held[r], "mem", step)
            step *= 2
    else:
        for r in range(1, n_mem):
            held[0] = held[0] + send(held[r], "mem", r)
    increment = held[0].reshape(share, rows, cols)

    lons = lons.astype(jnp.int32)
    spots = (lats[None, :] * n_lon + lons[:, None]).reshape(-1)
    origin = jnp.stack([lat * rows, lon * cols]).astype(jnp.int32)
    partial = pl.pallas_call(
        functools.partial(observe_kernel, levels, rows),
        out_shape=jax.ShapeDtypeStruct((n_lat * n_lon, slots), F32),
        in_specs=[SMEM] * 3 + [VMEM] * (1 + n_mem),
        out_specs=VMEM,
        scratch_shapes=[pltpu.VMEM((levels * rows, 2 * cols), BF16)],
        **params(4 * levels * rows * cols * n_lat * n_lon * slots, 4 * 2**20),
    )(chunks, spots, origin, packed, *sums)
    spread_out = jnp.broadcast_to(partial[None], (n_mem,) + partial.shape)
    spread_out = spread_out.reshape(n_mem * n_lat * n_lon, slots)
    back = lax.all_to_all(spread_out, ("mem", "lat", "lon"), 0, 0, tiled=True)
    departures = jnp.where(valid, innovation - jnp.sum(back, axis=0), 0.0)
    return (increment, departures)


def solution(mesh):
    placed = (
        P("mem", None, "lat", "lon"),
        P("mem", None, "lat", "lon"),
        P(),
        P(),
        P(("lat", "lon"), None),
        P(("lat", "lon")),
        P(("lat", "lon"), None),
        P(("lat", "lon")),
        P(("lat", "lon")),
    )
    return jax.shard_map(
        per_device,
        mesh=mesh,
        in_specs=placed,
        out_specs=(P("mem", "lat", "lon"), P(("lat", "lon"))),
        check_vma=False,
    )
```

time: 243 us -> 70.2 us (0.29)
  local copies, waits for them, and re-layouts: 136 us -> 1.63 us
  blocking collectives: 36.5 us -> 0 us
  waiting for transfers between devices: 9.33 us -> 24.3 us
  between operations: 16.4 us -> 1.53 us
  matrix products: 14 us -> 0 us
  Pallas kernels: 0 us -> 12.5 us
    scatter x3 -> x0, local copies, waits for them, and re-layouts: 102 us -> none  [the longest x1 76.5 us: per_device(): column_send = jnp.zeros((tiles, capacity), jnp.float32).at[target, rankin...]
    all_gather x4 -> x0, blocking collectives: 25.1 us -> none  [prefix(): gathered = jax.tree.map(lambda a: lax.all_gather(a, axis), part)]
    gather x5 -> x0, local copies, waits for them, and re-layouts: 17.3 us -> none  [the longest x1 4.02 us: per_device(): flat_padded[:, far_row * stride + near_col]]
    ppermute x4 -> x9, waiting for transfers between devices: 6.36 us -> 21 us  [send(): lax.ppermute(block, axis, [(i, toward(i, step, count)) for i in range(cou...]
    dot_general x5 -> x0, matrix products: 14 us -> none  [the longest x1 5.49 us: per_device(): profile = jnp.einsum('zk,mkp->mzp', modes, flat_field, precision=HIGH)]
    pallas_call x0 -> x3, Pallas kernels: none -> 12.5 us  [the longest x1 6.83 us: per_device(): pl.pallas_call(functools.partial(observe_kernel, levels, rows), out_shape...]
    unnamed x2 -> x0, blocking collectives: 11.4 us -> none
    ppermute x4 -> x9, starting transfers between devices: 7.8 us -> 14.2 us  [send(): lax.ppermute(block, axis, [(i, toward(i, step, count)) for i in range(cou...]
  transfers between devices with their start and end apart: 8 -> 10, of which waited for: 4 -> 6; matrix products, arithmetic and copies ran while one was open for 45% -> 14% of each run, Pallas kernels for 0% -> 11%
where the time goes in v1:
time: 70.2 us; the launch traced here: 69.9 us
  waiting for transfers between devices  24.3 us (35%)
  starting transfers between devices  19.1 us (27%)
  Pallas kernels  12.5 us (18%)
  other arithmetic  10.8 us (15%)
  local copies, waits for them, and re-layouts  1.63 us (2%)
  between operations  1.53 us (2%)
    ppermute x9, waiting for transfers between devices, send(): lax.ppermute(block, axis, [(i, toward(i, step, count)) for i in range(cou...  21 us
    ppermute x9, starting transfers between devices, send(): lax.ppermute(block, axis, [(i, toward(i, step, count)) for i in range(cou...  14.2 us
    pallas_call x1, Pallas kernels, per_device(): pl.pallas_call(functools.partial(observe_kernel, levels, rows), out_shape...  6.83 us
    all_to_all x1, starting transfers between devices, per_device(): back = lax.all_to_all(spread_out, ('mem', 'lat', 'lon'), 0, 0, tiled=True)  4.84 us
    pallas_call x1, Pallas kernels, per_device(): pl.pallas_call(sum_kernel, out_shape=(chunk_shape,) * n_mem, in_specs=[SM...  4.53 us
    all_to_all x1, waiting for transfers between devices, per_device(): back = lax.all_to_all(spread_out, ('mem', 'lat', 'lon'), 0, 0, tiled=True)  3.32 us
    mul x1, other arithmetic, per_device(): (rest * rest)[None, :, None, None]  2.05 us
  transfers between devices with their start and end apart: 10, of which 6 were waited for; matrix products, arithmetic and copies ran while one was open for 14% of the time, Pallas kernels for 11%

profile of v1, /device:TPU:0, one launch (start us, length us, event | category | flops | bytes accessed | tf_op | source)
XLA Modules:
  0.0 69.9 jit_solution(12356947127512561558)
XLA Ops:
  0.6 1.2 %convert_element_type.33 = f32[4,16,32,128]{3,2,1,0:T(8,128)S(1)} convert(bf16[4,16,32,128]{3,2,1,0:T(8,128)(2,1)} %own_ref.1) | non-fusion elementwise | flops 262144 | bytes 1572864 | tf_op jit(solution)/shard_map/convert_element_type | solution.py:230
  1.8 0.5 collective-permute-start
  3.0 0.7 %fusion.1 = (s32[512]{0:T(512)S(1)}, s32[512]{0:T(512)S(1)}) fusion(s32[512]{0:T(512)} %bitcast.44, s32[512]{0:T(512)} %param.16), kind=kLoop, calls=%fused_computation.28 | loop fusion | flops 21504 | bytes 8192 | tf_op jit(solution)/shard_map/add | solution.py:224
  3.7 0.9 %select_bitcast_fusion = f32[64,512]{1,0:T(8,128)S(1)} fusion(bf16[512,64]{0,1:T(8,128)(2,1)} %param.13, pred[512]{0:T(512)(128)(4,1)S(1)} %iota_compare_fusion), kind=kLoop, calls=%fused_computation.9 | loop fusion | flops 65536 | bytes 197120 | tf_op jit(solution)/shard_map/transpose | solution.py:226
  4.6 0.1 pad.9.clone
  4.7 0.1 maximum_bitcast_fusion.1
  4.8 2.6 %collective-permute-start.6 = (f32[1,72,512]{2,1,0:T(8,128)S(1)}, f32[1,72,512]{2,1,0:T(8,128)S(1)}, u32[]{:S(2)}, u32[]{:S(2)}) collective-permute-start(f32[1,72,512]{2,1,0:T(8,128)S(1)} %maximum_bitcast_fusion.1), channel_id=1, source_target_pairs={{0,2},{2,0},{4,6},{6,4},{1,3},{3,1},{5,7},{7,5},{8,10},{10,8},{12,... | collective-permute-start | bytes 442376 | tf_op jit(solution)/shard_map/ppermute | solution.py:37
  7.4 0.1 constant_dynamic-slice_fusion.3
  7.4 0.1 pad_maximum_fusion.5
  7.5 0.1 broadcast_multiply_fusion
  7.6 0.1 mul.151
  7.8 0.1 copy.17
  7.9 0.1 broadcast_multiply_fusion.3
  8.0 0.1 iota_add_fusion
  8.0 0.1 copy.16
  8.1 0.8 %abs_convert_fusion = f32[2,128,128]{2,1,0:T(8,128)} fusion(s32[2,128]{1,0:T(2,128)S(1)} %iota_add_fusion, s32[128]{0:T(128)S(1)} %iota_add_fusion.1), kind=kLoop, calls=%fused_computation.12 | loop fusion | flops 98304 | bytes 132608 | tf_op jit(solution)/shard_map/convert_element_type | solution.py:218
  8.9 0.1 broadcast_multiply_fusion.2
  9.0 0.1 broadcast_add_fusion
  9.1 0.1 pad_maximum_fusion.4.modes_ref
  9.3 2.6 %collective-permute-done.6 = f32[1,72,512]{2,1,0:T(8,128)S(1)} collective-permute-done((f32[1,72,512]{2,1,0:T(8,128)S(1)}, f32[1,72,512]{2,1,0:T(8,128)S(1)}, u32[]{:S(2)}, u32[]{:S(2)}) %collective-permute-start.6) | collective-permute-done | bytes 147488 | tf_op jit(solution)/shard_map/ppermute | solution.py:37
  11.9 1.8 %collective-permute-start.7 = (f32[2,72,512]{2,1,0:T(8,128)S(1)}, f32[2,72,512]{2,1,0:T(8,128)S(1)}, u32[]{:S(2)}, u32[]{:S(2)}) collective-permute-start(f32[2,72,512]{2,1,0:T(8,128)S(1)} %pad_maximum_fusion.1), channel_id=1, source_target_pairs={{0,4},{2,6},{4,0},{6,2},{1,5},{3,7},{5,1},{7,3},{8,12},{10,14},{12... | collective-permute-start | bytes 884744 | tf_op jit(solution)/shard_map/ppermute | solution.py:37
  13.7 0.8 %convert_multiply_fusion = f32[2,128,128]{2,1,0:T(8,128)} fusion(s32[2,128]{1,0:T(2,128)S(1)} %iota_add_fusion, s32[128]{0:T(128)S(1)} %iota_add_fusion.1), kind=kLoop, calls=%fused_computation.11 | loop fusion | flops 131072 | bytes 132608 | tf_op jit(solution)/shard_map/mul | solution.py:219
  14.5 6.3 %collective-permute-done.7 = f32[2,72,512]{2,1,0:T(8,128)S(1)} collective-permute-done((f32[2,72,512]{2,1,0:T(8,128)S(1)}, f32[2,72,512]{2,1,0:T(8,128)S(1)}, u32[]{:S(2)}, u32[]{:S(2)}) %collective-permute-start.7) | collective-permute-done | bytes 294944 | tf_op jit(solution)/shard_map/ppermute | solution.py:37
  20.8 0.9 %maximum_bitcast_fusion = f32[1,4,72,512]{3,2,1,0:T(8,128)S(1)} fusion(f32[2,72,512]{2,1,0:T(8,128)S(1)} %collective-permute-done.7, f32[1,72,512]{2,1,0:T(8,128)} %copy-done.2, f32[1,72,512]{2,1,0:T(8,128)S(1)} %maximum_bitcast_fusion.1), kind=kLoop, calls=%fused_computation.2 | loop fusion | flops 294912 | bytes 1179648 | tf_op jit(solution)/shard_map/broadcast_in_dim | solution.py:42
  21.8 0.1 pad_add_fusion.3.origin_ref
  21.9 0.1 tile.15
  22.0 0.1 tile.13
  22.1 0.1 add.98.spots_ref
  22.1 2.1 %negate_multiply_fusion.matrix_ref = f32[2,16,128,128]{3,2,1,0:T(8,128)S(1)} fusion(f32[2,128,128]{2,1,0:T(8,128)} %convert_multiply_fusion, f32[16]{0:T(128)S(1)} %get-tuple-element.28, f32[2,128,128]{2,1,0:T(8,128)} %abs_convert_fusion, f32[16]{0:T(128)S(1)} %get-tuple-element.16), kind=kLoop, calls=%fused_computation | loop fusion | flops 2621440 | bytes 2359424 | tf_op jit(solution)/shard_map/mul | solution.py:217
  24.3 1.2 %shard_map.104 = (f32[2048,128]{1,0:T(8,128)S(1)}, f32[2,64,128]{2,1,0:T(8,128)S(1)}) custom-call(bf16[4,16,32,128]{3,2,1,0:T(8,128)(2,1)S(1)} %copy-done, f32[1,4,16,32,128]{4,3,2,1,0:T(8,128)S(1)} %bitcast.36, f32[2,16,128,128]{3,2,1,0:T(8,128)S(1)} %negate_multiply_fusion.matrix_ref, f32[64,128]{1,0:T(8,128)S(1)} %broadcast_in_dim.30.decay_ref), custom_call_target="tpu_custom_call" | custom-call | flops 268435456 | bytes 4194304 | tf_op jit(solution)/shard_map/pallas_call | solution.py:233
  25.5 1.6 %collective-permute-start.1 = (f32[1,2,64,128]{3,2,1,0:T(8,128)S(1)}, f32[1,2,64,128]{3,2,1,0:T(8,128)S(1)}, u32[]{:S(2)}, u32[]{:S(2)}) collective-permute-start(f32[1,2,64,128]{3,2,1,0:T(8,128)S(1)} %bitcast.37), channel_id=1, source_target_pairs={{0,2},{2,0},{4,6},{6,4},{1,3},{3,1},{5,7},{7,5},{8,10},{10,8},{12,... | collective-permute-start | bytes 196616 | tf_op jit(solution)/shard_map/ppermute | solution.py:37
  27.1 0.1 pad_add_fusion.1.chunks_ref
  27.1 2.9 %collective-permute-done.1 = f32[1,2,64,128]{3,2,1,0:T(8,128)S(1)} collective-permute-done((f32[1,2,64,128]{3,2,1,0:T(8,128)S(1)}, f32[1,2,64,128]{3,2,1,0:T(8,128)S(1)}, u32[]{:S(2)}, u32[]{:S(2)}) %collective-permute-start.1) | collective-permute-done | bytes 65568 | tf_op jit(solution)/shard_map/ppermute | solution.py:37
  30.0 1.6 %collective-permute-start.2 = (f32[2,2,64,128]{3,2,1,0:T(8,128)S(1)}, f32[2,2,64,128]{3,2,1,0:T(8,128)S(1)}, u32[]{:S(2)}, u32[]{:S(2)}) collective-permute-start(f32[2,2,64,128]{3,2,1,0:T(8,128)S(1)} %pad_maximum_fusion.3), channel_id=1, source_target_pairs={{0,4},{2,6},{4,0},{6,2},{1,5},{3,7},{5,1},{7,3},{8,12},{10,14},{12... | collective-permute-start | bytes 393224 | tf_op jit(solution)/shard_map/ppermute | solution.py:37
  31.7 1.2 %pad_maximum_fusion = f32[2,4,72,512]{3,2,1,0:T(8,128)S(1)} fusion(f32[1,4,72,512]{3,2,1,0:T(8,128)} %collective-permute-done.8, f32[1,4,72,512]{3,2,1,0:T(8,128)S(1)} %maximum_bitcast_fusion), kind=kLoop, calls=%fused_computation.1 | loop fusion | flops 294912 | bytes 2359296 | tf_op jit(solution)/shard_map/concatenate | solution.py:47
  32.9 2.4 %collective-permute-done.2 = f32[2,2,64,128]{3,2,1,0:T(8,128)S(1)} collective-permute-done((f32[2,2,64,128]{3,2,1,0:T(8,128)S(1)}, f32[2,2,64,128]{3,2,1,0:T(8,128)S(1)}, u32[]{:S(2)}, u32[]{:S(2)}) %collective-permute-start.2) | collective-permute-done | bytes 131104 | tf_op jit(solution)/shard_map/ppermute | solution.py:37
  35.2 0.1 broadcast_in_dim.29.table_ref
  35.3 4.5 %shard_map.105 = (f32[512,128]{1,0:T(8,128)S(1)}, f32[512,128]{1,0:T(8,128)S(1)}, f32[512,128]{1,0:T(8,128)S(1)}, f32[512,128]{1,0:T(8,128)S(1)}) custom-call(s32[4]{0:T(128)S(1)} %get-tuple-element.15.places_ref, s32[4]{0:T(128)S(1)} %pad_add_fusion.1.chunks_ref, f32[3,64,128]{2,1,0:T(8,128)S(1)} %broadcast_in_dim.29.table_ref, ...), custom_call_target="tpu_custom_call" | custom-call | flops 402653184 | bytes 6291456 | tf_op jit(solution)/shard_map/pallas_call | solution.py:260
  39.9 1.7 %collective-permute-start.4 = (f32[512,128]{1,0:T(8,128)S(1)}, f32[512,128]{1,0:T(8,128)S(1)}, u32[]{:S(2)}, u32[]{:S(2)}) collective-permute-start(f32[512,128]{1,0:T(8,128)S(1)} %get-tuple-element.13.rest_3_), channel_id=1, source_target_pairs={{0,8},{8,0},{16,24},{24,16},{1,9},{9,1},{17,25},{25,17},{2,10},{10... | collective-permute-start | bytes 786440 | tf_op jit(solution)/shard_map/ppermute | solution.py:37
  41.6 6.8 %shard_map.106 = f32[8,512]{1,0:T(8,128)S(1)} custom-call(s32[4]{0:T(128)S(1)} %pad_add_fusion.1.chunks_ref, s32[8]{0:T(128)S(1)} %add.98.spots_ref, s32[2]{0:T(128)S(1)} %pad_add_fusion.3.origin_ref, f32[8,72,512]{2,1,0:T(8,128)S(1)} %bitcast.35, f32[512,128]{1,0:T(8,128)S(1)} %get-tuple-element.10.rest_0_, f32[512,128]{1,0:T(8,128)S(1)} %get-tuple-element.11.rest_1_, ...), custom_call_target="tpu_custom_call" | custom-call | flops 4294967296 | bytes 4194304 | tf_op jit(solution)/shard_map/pallas_call | solution.py:288
  48.4 0.7 %all_to_all.6 = f32[32,1,512]{2,1,0:T(1,128)} reshape(f32[4,8,512]{2,1,0:T(8,128)S(1)} %broadcast_in_dim.60) | data formatting | bytes 131072 | tf_op jit(solution)/shard_map/all_to_all | solution.py:298
  49.1 4.8 %all-to-all-start = ((f32[32,1,512]{2,1,0:T(1,128)}), f32[32,1,512]{2,1,0:T(1,128)S(1)}, u32[]{:S(2)}, u32[]{:S(2)}) async-start(f32[32,1,512]{2,1,0:T(1,128)} %all_to_all.6), calls=%async_computation | async-start | bytes 131072 | tf_op jit(solution)/shard_map/all_to_all | solution.py:298
  54.0 1.8 %collective-permute-start.3 = (f32[512,128]{1,0:T(8,128)S(1)}, f32[512,128]{1,0:T(8,128)S(1)}, u32[]{:S(2)}, u32[]{:S(2)}) collective-permute-start(f32[512,128]{1,0:T(8,128)S(1)} %get-tuple-element.11.rest_1_), channel_id=1, source_target_pairs={{0,8},{8,0},{16,24},{24,16},{1,9},{9,1},{17,25},{25,17},{2,10},{10... | collective-permute-start | bytes 786440 | tf_op jit(solution)/shard_map/ppermute | solution.py:37
  55.8 2.5 %collective-permute-start.5 = (f32[512,128]{1,0:T(8,128)S(1)}, f32[512,128]{1,0:T(8,128)S(1)}, u32[]{:S(2)}, u32[]{:S(2)}) collective-permute-start(f32[512,128]{1,0:T(8,128)S(1)} %add.93), channel_id=1, source_target_pairs={{0,16},{8,24},{16,0},{24,8},{1,17},{9,25},{17,1},{25,9},{2,18},{10... | collective-permute-start | bytes 786440 | tf_op jit(solution)/shard_map/ppermute | solution.py:37
  58.3 3.3 %all-to-all-done = f32[32,1,512]{2,1,0:T(1,128)S(1)} async-done(((f32[32,1,512]{2,1,0:T(1,128)}), f32[32,1,512]{2,1,0:T(1,128)S(1)}, u32[]{:S(2)}, u32[]{:S(2)}) %all-to-all-start) | async-done | bytes 65568 | tf_op jit(solution)/shard_map/all_to_all | solution.py:298
  61.7 0.6 subtract_select_fusion
  62.3 6.8 %collective-permute-done.3 = f32[512,128]{1,0:T(8,128)S(1)} collective-permute-done((f32[512,128]{1,0:T(8,128)S(1)}, f32[512,128]{1,0:T(8,128)S(1)}, u32[]{:S(2)}, u32[]{:S(2)}) %collective-permute-start.3) | collective-permute-done | bytes 262176 | tf_op jit(solution)/shard_map/ppermute | solution.py:37
  69.1 0.7 %add_add_fusion = f32[512,128]{1,0:T(8,128)} fusion(f32[512,128]{1,0:T(8,128)S(1)} %collective-permute-done.5, f32[512,128]{1,0:T(8,128)S(1)} %get-tuple-element.10.rest_0_, f32[512,128]{1,0:T(8,128)S(1)} %collective-permute-done.3), kind=kLoop, calls=%fused_computation.5 | loop fusion | flops 131072 | bytes 1048576 | tf_op jit(solution)/shard_map/add | solution.py:278
  (37 shorter events, 0.4 us)
Async XLA Ops:
  0.6 6.7 %copy-start.3 = (f32[64,16]{0,1:T(8,128)S(1)}, f32[64,16]{0,1:T(8,128)}, u32[]{:S(2)}) copy-start(f32[64,16]{0,1:T(8,128)} %param.12) | copy-start | bytes 12292
  0.6 7.4 %copy-start.5 = (f32[16]{0:T(128)S(1)}, f32[16]{0:T(128)}, u32[]{:S(2)}) copy-start(f32[16]{0:T(128)} %param.11) | copy-start | bytes 196
  1.8 22.4 %collective-permute-start = (f32[4,16,32,128]{3,2,1,0:T(8,128)S(1)}, f32[4,16,32,128]{3,2,1,0:T(8,128)S(1)}, u32[]{:S(2)}, u32[]{:S(2)}) collective-permute-start(f32[4,16,32,128]{3,2,1,0:T(8,128)S(1)} %convert_element_type.33), channel_id=1, source_target_pairs={{0,1},{1,0},{2,3},{3,2},{4,5},{5,4},{6,7},{7,6},{8,9},{9,8},{10,11... | collective-permute-start | bytes 3145736 | tf_op jit(solution)/shard_map/ppermute | solution.py:37
  4.8 7.1 %collective-permute-start.6 = (f32[1,72,512]{2,1,0:T(8,128)S(1)}, f32[1,72,512]{2,1,0:T(8,128)S(1)}, u32[]{:S(2)}, u32[]{:S(2)}) collective-permute-start(f32[1,72,512]{2,1,0:T(8,128)S(1)} %maximum_bitcast_fusion.1), channel_id=1, source_target_pairs={{0,2},{2,0},{4,6},{6,4},{1,3},{3,1},{5,7},{7,5},{8,10},{10,8},{12,... | collective-permute-start | bytes 442376 | tf_op jit(solution)/shard_map/ppermute | solution.py:37
  9.2 15.0 %copy-start = (bf16[4,16,32,128]{3,2,1,0:T(8,128)(2,1)S(1)}, bf16[4,16,32,128]{3,2,1,0:T(8,128)(2,1)}, u32[]{:S(2)}) copy-start(bf16[4,16,32,128]{3,2,1,0:T(8,128)(2,1)} %own_ref.1) | copy-start | bytes 1572868
  11.9 2.6 %copy-start.2 = (f32[1,72,512]{2,1,0:T(8,128)}, f32[1,72,512]{2,1,0:T(8,128)S(1)}, u32[]{:S(2)}) copy-start(f32[1,72,512]{2,1,0:T(8,128)S(1)} %collective-permute-done.6) | copy-start | bytes 442372
  11.9 8.9 %collective-permute-start.7 = (f32[2,72,512]{2,1,0:T(8,128)S(1)}, f32[2,72,512]{2,1,0:T(8,128)S(1)}, u32[]{:S(2)}, u32[]{:S(2)}) collective-permute-start(f32[2,72,512]{2,1,0:T(8,128)S(1)} %pad_maximum_fusion.1), channel_id=1, source_target_pairs={{0,4},{2,6},{4,0},{6,2},{1,5},{3,7},{5,1},{7,3},{8,12},{10,14},{12... | collective-permute-start | bytes 884744 | tf_op jit(solution)/shard_map/ppermute | solution.py:37
  21.7 9.9 %collective-permute-start.8 = (f32[1,4,72,512]{3,2,1,0:T(8,128)S(1)}, f32[1,4,72,512]{3,2,1,0:T(8,128)}, u32[]{:S(2)}, u32[]{:S(2)}) collective-permute-start(f32[1,4,72,512]{3,2,1,0:T(8,128)S(1)} %maximum_bitcast_fusion), channel_id=1, source_target_pairs={{0,1},{1,0},{2,3},{3,2},{4,5},{5,4},{6,7},{7,6},{8,9},{9,8},{10,11... | collective-permute-start | bytes 1769480 | tf_op jit(solution)/shard_map/ppermute | solution.py:37
  25.5 9.9 %copy-start.1 = (bf16[4,64,32,128]{3,2,1,0:T(8,128)(2,1)S(1)}, bf16[4,64,32,128]{3,2,1,0:T(8,128)(2,1)}, u32[]{:S(2)}) copy-start(bf16[4,64,32,128]{3,2,1,0:T(8,128)(2,1)} %pert_ref.1) | copy-start | bytes 6291460
  25.5 4.6 %collective-permute-start.1 = (f32[1,2,64,128]{3,2,1,0:T(8,128)S(1)}, f32[1,2,64,128]{3,2,1,0:T(8,128)S(1)}, u32[]{:S(2)}, u32[]{:S(2)}) collective-permute-start(f32[1,2,64,128]{3,2,1,0:T(8,128)S(1)} %bitcast.37), channel_id=1, source_target_pairs={{0,2},{2,0},{4,6},{6,4},{1,3},{3,1},{5,7},{7,5},{8,10},{10,8},{12,... | collective-permute-start | bytes 196616 | tf_op jit(solution)/shard_map/ppermute | solution.py:37
  30.0 5.2 %collective-permute-start.2 = (f32[2,2,64,128]{3,2,1,0:T(8,128)S(1)}, f32[2,2,64,128]{3,2,1,0:T(8,128)S(1)}, u32[]{:S(2)}, u32[]{:S(2)}) collective-permute-start(f32[2,2,64,128]{3,2,1,0:T(8,128)S(1)} %pad_maximum_fusion.3), channel_id=1, source_target_pairs={{0,4},{2,6},{4,0},{6,2},{1,5},{3,7},{5,1},{7,3},{8,12},{10,14},{12... | collective-permute-start | bytes 393224 | tf_op jit(solution)/shard_map/ppermute | solution.py:37
  39.9 15.9 %collective-permute-start.4 = (f32[512,128]{1,0:T(8,128)S(1)}, f32[512,128]{1,0:T(8,128)S(1)}, u32[]{:S(2)}, u32[]{:S(2)}) collective-permute-start(f32[512,128]{1,0:T(8,128)S(1)} %get-tuple-element.13.rest_3_), channel_id=1, source_target_pairs={{0,8},{8,0},{16,24},{24,16},{1,9},{9,1},{17,25},{25,17},{2,10},{10... | collective-permute-start | bytes 786440 | tf_op jit(solution)/shard_map/ppermute | solution.py:37
  41.6 20.1 %copy-start.4 = (f32[512]{0:T(512)S(1)}, f32[512]{0:T(512)}, u32[]{:S(2)}) copy-start(f32[512]{0:T(512)} %param.14) | copy-start | bytes 6148
  49.1 12.5 %all-to-all-start = ((f32[32,1,512]{2,1,0:T(1,128)}), f32[32,1,512]{2,1,0:T(1,128)S(1)}, u32[]{:S(2)}, u32[]{:S(2)}) async-start(f32[32,1,512]{2,1,0:T(1,128)} %all_to_all.6), calls=%async_computation | async-start | bytes 131072 | tf_op jit(solution)/shard_map/all_to_all | solution.py:298
  54.0 15.2 %collective-permute-start.3 = (f32[512,128]{1,0:T(8,128)S(1)}, f32[512,128]{1,0:T(8,128)S(1)}, u32[]{:S(2)}, u32[]{:S(2)}) collective-permute-start(f32[512,128]{1,0:T(8,128)S(1)} %get-tuple-element.11.rest_1_), channel_id=1, source_target_pairs={{0,8},{8,0},{16,24},{24,16},{1,9},{9,1},{17,25},{25,17},{2,10},{10... | collective-permute-start | bytes 786440 | tf_op jit(solution)/shard_map/ppermute | solution.py:37
  55.8 13.3 %collective-permute-start.5 = (f32[512,128]{1,0:T(8,128)S(1)}, f32[512,128]{1,0:T(8,128)S(1)}, u32[]{:S(2)}, u32[]{:S(2)}) collective-permute-start(f32[512,128]{1,0:T(8,128)S(1)} %add.93), channel_id=1, source_target_pairs={{0,16},{8,24},{16,0},{24,8},{1,17},{9,25},{17,1},{25,9},{2,18},{10... | collective-permute-start | bytes 786440 | tf_op jit(solution)/shard_map/ppermute | solution.py:37

commit v2 on v1

v2 whole, which is shorter than its diff:
```python
import functools
import math

import jax
import jax.numpy as jnp
from jax import lax
from jax.experimental import pallas as pl
from jax.experimental.pallas import tpu as pltpu
from jax.sharding import PartitionSpec as P

F32, BF16 = jnp.float32, jnp.bfloat16
VMEM = pl.BlockSpec(memory_space=pltpu.VMEM)
SMEM = pl.BlockSpec(memory_space=pltpu.SMEM)


def params(flops, moved, held):
    return dict(
        compiler_params=pltpu.CompilerParams(vmem_limit_bytes=held + 6 * 2**20),
        cost_estimate=pl.CostEstimate(flops=flops, bytes_accessed=moved, transcendentals=0),
    )


def paired(count):
    return count & (count - 1) == 0


def toward(place, step, count):
    return place ^ step if paired(count) else (place + step) % count


def source(place, step, count):
    return place ^ step if paired(count) else (place - step) % count


def send(block, axis, step):
    count = lax.axis_size(axis)
    return lax.ppermute(block, axis, [(i, toward(i, step, count)) for i in range(count)])


def collect(block, axis):
    count = lax.axis_size(axis)
    blocks = block[None]
    if not paired(count):
        return jnp.concatenate([blocks] + [send(blocks, axis, s) for s in range(1, count)])
    step = 1
    while step < count:
        blocks = jnp.concatenate([blocks, send(blocks, axis, step)])
        step *= 2
    return blocks


def halve(value):
    high = value.astype(BF16)
    return high, (value - high.astype(F32)).astype(BF16)


def matrix_kernel(starts_ref, log_ref, to_ref, from_ref, matrix_ref):
    sources, cols, modes = from_ref.shape
    across = lax.broadcasted_iota(jnp.int32, (cols, cols), 1) + starts_ref[0]
    for s in range(sources):
        down = lax.broadcasted_iota(jnp.int32, (cols, cols), 0) + starts_ref[s]
        distance = jnp.abs(across - down).astype(F32)
        for k in range(modes):
            end = jnp.where(across >= down, to_ref[k : k + 1, :], from_ref[s, :, k : k + 1])
            high, low = halve(jnp.exp(distance * log_ref[k]) * end)
            at = s * cols
            matrix_ref[k, at : at + cols, :] = jnp.concatenate([high, low], axis=1)


def columns_kernel(own_ref, other_ref, matrix_ref, table_ref, field_ref, edge_ref, first):
    members, modes, rows, cols = own_ref.shape
    sources = matrix_ref.shape[1] // cols
    lines = members * modes
    for k in range(modes):
        pieces = [jnp.concatenate([own_ref[m, k] for m in range(members)])]
        for s in range(1, sources):
            pieces.append(
                jnp.concatenate([other_ref[s - 1, m, k] for m in range(members)]).astype(BF16)
            )
        both = jnp.dot(
            jnp.concatenate(pieces, axis=1), matrix_ref[k], preferred_element_type=F32
        )
        made = both[:, :cols] + both[:, cols:]
        for m in range(members):
            field_ref[pl.ds(m * modes + k, rows, stride=lines), :] = made[m * rows : (m + 1) * rows]
    decay = jnp.broadcast_to(table_ref[:, 1:2], (lines, cols))
    state = jnp.zeros((lines, cols), F32)
    for x in range(rows):
        state = decay * state + field_ref[x * lines : (x + 1) * lines, :]
        first[x * lines : (x + 1) * lines, :] = state
    edge_ref[0] = state
    state = jnp.zeros((lines, cols), F32)
    for x in reversed(range(rows)):
        state = decay * state + first[x * lines : (x + 1) * lines, :]
    edge_ref[1] = state


def sum_kernel(
    scale, places_ref, chunks_ref, table_ref, edges_ref, field_ref, modes_ref, pert_ref, *rest
):
    chunks = len(rest) - 3
    outs, (first, second, pert) = rest[:chunks], rest[chunks:]
    members, levels, rows, cols = pert_ref.shape
    lines, kinds = table_ref.shape[0], table_ref.shape[0] // members
    share = levels // chunks
    count = edges_ref.shape[0]

    for m in range(members):
        for z in range(levels):
            at = (m * levels + z) * rows
            pert[at : at + rows, :] = pert_ref[m, z].astype(F32)

    log, decay, beta = (
        jnp.broadcast_to(table_ref[:, i : i + 1], (lines, cols)) for i in range(3)
    )

    def power(ahead):
        exponent = (rows * jnp.maximum(ahead, 0)).astype(F32)
        return jnp.where(ahead >= 0, jnp.exp(log * exponent), 0.0)

    own = places_ref[0]
    state = jnp.zeros((lines, cols), F32)
    after = jnp.zeros((lines, cols), F32)
    for s in range(count):
        there = places_ref[s]
        state = state + power(own - there - 1) * edges_ref[s, 0]
        before = jnp.zeros((lines, cols), F32)
        for t in range(count):
            before = before + power(there - places_ref[t] - 1) * edges_ref[t, 0]
        after = after + power(there - own - 1) * (edges_ref[s, 1] + beta * before)

    for x in range(rows):
        state = decay * state + field_ref[x * lines : (x + 1) * lines, :]
        first[x * lines : (x + 1) * lines, :] = state
    state = after
    for x in reversed(range(rows)):
        state = decay * state + first[x * lines : (x + 1) * lines, :]
        high, low = halve(state)
        second[:, x * cols : (x + 1) * cols] = jnp.concatenate([high, low, high])

    held = jnp.concatenate([modes_ref[pl.ds(chunks_ref[r] * share, share), :] for r in range(chunks)])
    held = jnp.concatenate([held * scale] * members, axis=1)
    member = lax.broadcasted_iota(jnp.int32, (levels, lines), 1) // kinds
    high, low = halve(
        jnp.concatenate([jnp.where(member == m, held, 0.0) for m in range(members)])
    )
    weights = jnp.concatenate([high, high, low], axis=1)

    for pair in range(0, rows, 2):
        profile = jnp.dot(
            weights,
            second[:, pair * cols : (pair + 2) * cols],
            preferred_element_type=F32,
        )
        for half in range(2):
            x = pair + half
            for r in range(chunks):
                total = None
                for m in range(members):
                    at = (m * levels + chunks_ref[r] * share) * rows + x
                    line = m * levels + r * share
                    term = (
                        profile[line : line + share, half * cols : (half + 1) * cols]
                        * pert[pl.ds(at, share, stride=rows), :]
                    )
                    total = term if total is None else total + term
                outs[r][pl.ds(x, share, stride=rows), :] = total


def observe_kernel(levels, rows, chunks_ref, origin_ref, spots_ref, *rest):
    chunks, tiles = chunks_ref.shape[0], spots_ref.shape[0]
    sums, packs, (out_ref, split) = rest[:chunks], rest[chunks:-2], rest[-2:]
    slots = out_ref.shape[1]
    step, cols = sums[0].shape
    for r in range(chunks):
        high, low = halve(sums[r][...])
        at = pl.multiple_of(chunks_ref[r] * step, step)
        split[pl.ds(at, step), :] = jnp.concatenate([high, low], axis=1)

    def spread(fine, origin, length):
        near = jnp.floor(fine * 0.5)
        far = near - 1.0 + 2.0 * (fine - 2.0 * near)
        cell = (lax.broadcasted_iota(jnp.int32, (length, slots), 0) + origin).astype(F32)
        return jnp.where(cell == near, 0.75, 0.0) + jnp.where(cell == far, 0.25, 0.0)

    group = math.gcd(levels, 16)
    before = 0
    for packed_ref in packs:

        @pl.loop(0, packed_ref.shape[0])
        def _(block, packed_ref=packed_ref, before=before):
            fine = packed_ref[block, levels : levels + 8, :]
            across = spread(fine[1:2], origin_ref[1], cols).astype(BF16)
            across = jnp.concatenate([across, across])
            down = spread(fine[0:1], origin_ref[0], rows)
            total = jnp.zeros((rows, slots), F32)
            for g in range(0, levels, group):
                seen = jnp.dot(
                    split[g * rows : (g + group) * rows, :], across, preferred_element_type=F32
                )
                weights = packed_ref[block, g : g + group, :]
                for z in range(group):
                    total = total + seen[z * rows : (z + 1) * rows] * weights[z : z + 1]
            row = jnp.sum(total * down, axis=0, keepdims=True)
            for copy in range(out_ref.shape[0] // tiles):
                out_ref[pl.ds(copy * tiles + spots_ref[before + block], 1), :] = row

        before += packed_ref.shape[0]


def finish_kernel(count_ref, innovation_ref, back_ref, *rest):
    parts, (increment_ref, departures_ref) = rest[:-2], rest[-2:]
    total = parts[0][...]
    for part in parts[1:]:
        total = total + part[...]
    increment_ref[...] = total
    equal = jnp.sum(back_ref[...], axis=0, keepdims=True)
    place = lax.broadcasted_iota(jnp.int32, equal.shape, 1)
    departures_ref[...] = jnp.where(place < count_ref[0], innovation_ref[...] - equal, 0.0)


def per_device(
    perturbation,
    control,
    filter_length,
    modes,
    obs_weights,
    innovation,
    obs_tile,
    obs_column,
    obs_count,
):
    members, levels, rows, cols = perturbation.shape
    kinds = control.shape[1]
    lines = members * kinds
    n_mem, n_lat, n_lon = (lax.axis_size(a) for a in ("mem", "lat", "lon"))
    mem, lat, lon = (lax.axis_index(a) for a in ("mem", "lat", "lon"))
    slots = innovation.shape[0]
    share = levels // n_mem
    all_cols = cols * n_lon

    rate = jnp.exp(-1.0 / filter_length)
    rest = 1.0 - rate
    log = jnp.log1p(-rest)
    beta = rate * jnp.expm1(2.0 * rows * log) / jnp.expm1(2.0 * log)
    table = jnp.tile(jnp.stack([log, rate, beta], axis=1), (members, 1))
    lons = jnp.stack([source(lon, s, n_lon) for s in range(n_lon)]).astype(jnp.int32)

    def ends(place):
        reach = (all_cols - place * cols - jnp.arange(cols)).astype(F32)
        return (rest * rest)[:, None] * -jnp.expm1(2.0 * log[:, None] * reach[None, :])

    matrix = pl.pallas_call(
        matrix_kernel,
        out_shape=jax.ShapeDtypeStruct((kinds, all_cols, 2 * cols), BF16),
        in_specs=[SMEM, SMEM, VMEM, VMEM],
        out_specs=VMEM,
        **params(8 * kinds * all_cols * cols, 4 * kinds * all_cols * cols, 5 * kinds * all_cols * cols),
    )(
        lons * cols,
        log,
        ends(lon),
        jnp.stack([ends(source(lon, s, n_lon)).T for s in range(n_lon)]),
    )

    whole = control.astype(F32)
    others = [send(whole, "lon", s) for s in range(1, n_lon)]
    others = jnp.stack(others) if others else jnp.zeros((1,) + whole.shape, F32)
    field, edge = pl.pallas_call(
        columns_kernel,
        out_shape=(
            jax.ShapeDtypeStruct((rows * lines, cols), F32),
            jax.ShapeDtypeStruct((2, lines, cols), F32),
        ),
        in_specs=[VMEM] * 4,
        out_specs=(VMEM, VMEM),
        scratch_shapes=[pltpu.VMEM((rows * lines, cols), F32)],
        **params(
            4 * lines * rows * cols * all_cols,
            4 * 2**20,
            4 * lines * rows * (2 * cols + all_cols) + 4 * kinds * all_cols * cols,
        ),
    )(control, others, matrix, table)

    obs_weights, obs_tile, obs_column, _ = lax.optimization_barrier(
        (obs_weights, obs_tile, obs_column, edge)
    )
    valid = jnp.arange(slots, dtype=jnp.int32) < obs_count[0]
    target = obs_tile[:, 0]
    fine_row = target // n_lon * (2 * rows) + obs_column // (2 * cols)
    fine_col = target % n_lon * (2 * cols) + obs_column % (2 * cols)
    weights = jnp.where(valid[:, None], obs_weights.astype(F32), 0.0).T
    places = jnp.stack([fine_row, fine_col]).astype(F32)
    packed = jnp.concatenate([weights, places, jnp.zeros((6, slots), F32)])

    edges = edge[None]
    step = 1
    while step < n_lat and paired(n_lat):
        edges = jnp.concatenate([edges, send(edges, "lat", step)])
        if step == 1:
            packed = lax.optimization_barrier((packed, edges))[0]
        step *= 2
    if not paired(n_lat):
        edges = collect(edge, "lat")
    packed = [packed] + [send(packed, "lat", s) for s in range(1, n_lat)]
    lats = jnp.stack([source(lat, s, n_lat) for s in range(n_lat)]).astype(jnp.int32)
    chunks = jnp.stack([toward(mem, r, n_mem) for r in range(n_mem)]).astype(jnp.int32)
    chunk_shape = jax.ShapeDtypeStruct((share * rows, cols), F32)
    sums = pl.pallas_call(
        functools.partial(sum_kernel, 1.0 / math.sqrt(members * n_mem - 1)),
        out_shape=(chunk_shape,) * n_mem,
        in_specs=[SMEM, SMEM] + [VMEM] * 5,
        out_specs=(VMEM,) * n_mem,
        scratch_shapes=[
            pltpu.VMEM((rows * lines, cols), F32),
            pltpu.VMEM((3 * lines, rows * cols), BF16),
            pltpu.VMEM((members * levels * rows, cols), F32),
        ],
        **params(
            6 * members * levels * lines * rows * cols,
            6 * 2**20,
            (6 * members + 4) * levels * rows * cols + 14 * lines * rows * cols,
        ),
    )(lats, chunks, table, edges, field, modes, perturbation)


    tiles = n_lat * n_lon
    packed = jnp.stack(lax.optimization_barrier((packed, sums[0]))[0])
    packs = [packed] + [send(packed, "lon", s) for s in range(1, n_lon)]
    equal = pl.pallas_call(
        functools.partial(observe_kernel, levels, rows),
        out_shape=jax.ShapeDtypeStruct((n_mem * tiles, slots), F32),
        in_specs=[SMEM] * 3 + [VMEM] * (n_mem + n_lon),
        out_specs=VMEM,
        scratch_shapes=[pltpu.VMEM((levels * rows, 2 * cols), BF16)],
        **params(
            4 * levels * rows * cols * tiles * slots,
            4 * 2**20,
            8 * levels * rows * cols + packed.size * n_lon * 4 + n_mem * tiles * slots * 4,
        ),
    )(
        chunks,
        jnp.stack([lat * rows, lon * cols]).astype(jnp.int32),
        (lats[None, :] * n_lon + lons[:, None]).reshape(-1),
        *sums,
        *packs,
    )

    held, leaving = [[chunk] for chunk in sums], equal
    if paired(n_mem):
        step = 1
        while step < n_mem:
            for r in reversed(range(step, n_mem, 2 * step)):
                part = functools.reduce(jnp.add, held[r])
                if 2 * step == n_mem:
                    leaving = lax.optimization_barrier((equal, part))[0]
                got = send(part, "mem", step)
                if r == 3:
                    got, _ = lax.optimization_barrier((got, equal))
                held[r ^ step].append(got)
            step *= 2
    else:
        for r in range(1, n_mem):
            held[0].append(send(sums[r], "mem", r))
    back = lax.all_to_all(leaving, ("mem", "lat", "lon"), 0, 0, tiled=True)
    increment, departures = pl.pallas_call(
        finish_kernel,
        out_shape=(chunk_shape, jax.ShapeDtypeStruct((1, slots), F32)),
        in_specs=[SMEM] + [VMEM] * (2 + len(held[0])),
        out_specs=(VMEM, VMEM),
        **params(
            len(held[0]) * share * rows * cols,
            8 * len(held[0]) * share * rows * cols,
            8 * (len(held[0]) + 1) * share * rows * cols + 8 * n_mem * tiles * slots,
        ),
    )(obs_count, innovation[None], back, *held[0])
    increment, departures = increment.reshape(share, rows, cols), departures[0]
    return (increment, departures)


def solution(mesh):
    placed = (
        P("mem", None, "lat", "lon"),
        P("mem", None, "lat", "lon"),
        P(),
        P(),
        P(("lat", "lon"), None),
        P(("lat", "lon")),
        P(("lat", "lon"), None),
        P(("lat", "lon")),
        P(("lat", "lon")),
    )
    return jax.shard_map(
        per_device,
        mesh=mesh,
        in_specs=placed,
        out_specs=(P("mem", "lat", "lon"), P(("lat", "lon"))),
        check_vma=False,
    )
```

time: 70.2 us -> 53.9 us (0.77)
  waiting for transfers between devices: 24.3 us -> 4.51 us
  blocking collectives: 0 us -> 15.9 us
  other arithmetic: 10.8 us -> 2.71 us
  starting transfers between devices: 19.1 us -> 13.3 us
  Pallas kernels: 12.5 us -> 14.6 us
    ppermute x9 -> x10, waiting for transfers between devices: 21 us -> 4.51 us  [send(): lax.ppermute(block, axis, [(i, toward(i, step, count)) for i in range(cou...]
    all_to_all x0 -> x1, blocking collectives: none -> 15.9 us  [per_device(): back = lax.all_to_all(leaving, ('mem', 'lat', 'lon'), 0, 0, tiled=True)]
    all_to_all x1 -> x0, starting transfers between devices: 4.84 us -> none  [per_device(): back = lax.all_to_all(spread_out, ('mem', 'lat', 'lon'), 0, 0, tiled=True)]
    all_to_all x1 -> x0, waiting for transfers between devices: 3.32 us -> none  [per_device(): back = lax.all_to_all(spread_out, ('mem', 'lat', 'lon'), 0, 0, tiled=True)]
    mul x7 -> x6, other arithmetic: 3.06 us -> 1.01 us  [the longest x1 0.66 us: ends(): rest * rest]
    pallas_call x1 -> x3, Pallas kernels: 4.53 us -> 6.57 us  [the longest x1 4.56 us: per_device(): pl.pallas_call(functools.partial(sum_kernel, 1.0 / math.sqrt(members * n_...]
    concatenate x6 -> x3, other arithmetic: 1.43 us -> 0.11 us  [the longest x1 0.08 us: per_device(): packed = jnp.concatenate([weights, places, jnp.zeros((6, slots), F32)])]
    broadcast_in_dim x2 -> x0, other arithmetic: 1.03 us -> none  [collect(): blocks = block[None]]
  transfers between devices with their start and end apart: 10 -> 10, of which waited for: 6 -> 4; matrix products, arithmetic and copies ran while one was open for 14% -> 5% of each run, Pallas kernels for 11% -> 24%
where the time goes in v2:
time: 53.9 us; the launch traced here: 53.7 us
  blocking collectives  15.9 us (29%)
  Pallas kernels  14.6 us (27%)
  starting transfers between devices  13.3 us (25%)
  waiting for transfers between devices  4.51 us (8%)
  other arithmetic  2.71 us (5%)
  between operations  1.51 us (3%)
  local copies, waits for them, and re-layouts  1.24 us (2%)
    all_to_all x1, blocking collectives, per_device(): back = lax.all_to_all(leaving, ('mem', 'lat', 'lon'), 0, 0, tiled=True)  15.9 us
    ppermute x10, starting transfers between devices, send(): lax.ppermute(block, axis, [(i, toward(i, step, count)) for i in range(cou...  13.3 us
    pallas_call x1, Pallas kernels, per_device(): pl.pallas_call(functools.partial(observe_kernel, levels, rows), out_shape...  6.85 us
    pallas_call x1, Pallas kernels, per_device(): pl.pallas_call(functools.partial(sum_kernel, 1.0 / math.sqrt(members * n_...  4.56 us
    ppermute x10, waiting for transfers between devices, send(): lax.ppermute(block, axis, [(i, toward(i, step, count)) for i in range(cou...  4.51 us
    pallas_call x1, Pallas kernels, per_device(): pl.pallas_call(matrix_kernel, out_shape=jax.ShapeDtypeStruct((kinds, all_...  1.26 us
    convert_element_type x1, other arithmetic, per_device(): whole = control.astype(F32)  1.22 us
    pallas_call x1, Pallas kernels, per_device(): pl.pallas_call(columns_kernel, out_shape=(jax.ShapeDtypeStruct((rows * li...  1.15 us
  transfers between devices with their start and end apart: 10, of which 4 were waited for; matrix products, arithmetic and copies ran while one was open for 5% of the time, Pallas kernels for 24%

profile of v2, /device:TPU:0, one launch (start us, length us, event | category | flops | bytes accessed | tf_op | source)
XLA Modules:
  0.0 53.7 jit_solution(12272185384551236627)
XLA Ops:
  0.6 1.2 %convert_element_type.24 = f32[4,16,32,128]{3,2,1,0:T(8,128)S(1)} convert(bf16[4,16,32,128]{3,2,1,0:T(8,128)(2,1)} %own_ref.1) | non-fusion elementwise | flops 262144 | bytes 1572864 | tf_op jit(solution)/shard_map/convert_element_type | solution.py:266
  1.9 0.5 collective-permute-start
  2.4 0.7 %subtract_multiply_fusion = (f32[16]{0:T(128)S(1)}, f32[16]{0:T(128)S(1)}) fusion(f32[16]{0:T(128)} %param.11), kind=kLoop, calls=%fused_computation.44 | loop fusion | flops 48 | bytes 192 | tf_op jit(solution)/shard_map/mul | solution.py:251
  3.1 0.1 negate_multiply_fusion.1
  3.2 0.1 copy.14.from_ref
  3.3 0.1 copy.13
  4.0 0.8 %copy.15.modes_ref = f32[64,16]{1,0:T(8,128)S(1)} copy(f32[64,16]{0,1:T(8,128)} %param.12) | data formatting | bytes 8192 | tf_op args[3]
  4.8 0.1 pad.6.clone
  4.9 0.1 broadcast_multiply_fusion
  5.0 0.1 negate_multiply_fusion.2.to_ref
  5.1 1.3 %shard_map.104.matrix_ref = bf16[16,256,256]{2,1,0:T(8,128)(2,1)S(1)} custom-call(s32[2]{0:T(128)S(1)} %get-tuple-element.40.starts_ref, f32[16]{0:T(128)S(1)} %get-tuple-element.51.log_ref, f32[16,128]{1,0:T(8,128)S(1)} %negate_multiply_fusion.2.to_ref, f32[2,128,16]{2,1,0:T(8,128)S(1)} %copy.14.from_ref), custom_call_target="tpu_custom_call" | custom-call | flops 4194304 | bytes 2097152 | tf_op jit(solution)/shard_map/pallas_call | solution.py:253
  6.3 0.0 copy-start.4
  6.3 0.0 copy-start.5
  6.4 0.0 copy-start.3
  6.4 0.1 pad_add_fusion.chunks_ref
  6.5 0.1 broadcast_multiply_fusion.2
  6.5 0.0 collective-permute-done
  6.6 0.0 copy-start.1
  6.6 1.1 %shard_map.105 = (f32[2048,128]{1,0:T(8,128)S(1)}, f32[2,64,128]{2,1,0:T(8,128)S(1)}) custom-call(bf16[4,16,32,128]{3,2,1,0:T(8,128)(2,1)S(1)} %copy-done, f32[1,4,16,32,128]{4,3,2,1,0:T(8,128)S(1)} %bitcast.38, bf16[16,256,256]{2,1,0:T(8,128)(2,1)S(1)} %shard_map.104.matrix_ref, f32[64,3]{1,0:T(8,128)S(1)} %bitcast.39), custom_call_target="tpu_custom_call" | custom-call | flops 268435456 | bytes 4194304 | tf_op jit(solution)/shard_map/pallas_call | solution.py:269
  7.7 2.6 %collective-permute-start.1 = (f32[1,2,64,128]{3,2,1,0:T(8,128)S(1)}, f32[1,2,64,128]{3,2,1,0:T(8,128)S(1)}, u32[]{:S(2)}, u32[]{:S(2)}) collective-permute-start(f32[1,2,64,128]{3,2,1,0:T(8,128)S(1)} %bitcast.42), channel_id=1, source_target_pairs={{0,2},{2,0},{4,6},{6,4},{1,3},{3,1},{5,7},{7,5},{8,10},{10,8},{12,... | collective-permute-start | bytes 196616 | tf_op jit(solution)/shard_map/ppermute | solution.py:37
  10.3 0.0 copy-done.4
  10.4 2.7 %collective-permute-done.1 = f32[1,2,64,128]{3,2,1,0:T(8,128)S(1)} collective-permute-done((f32[1,2,64,128]{3,2,1,0:T(8,128)S(1)}, f32[1,2,64,128]{3,2,1,0:T(8,128)S(1)}, u32[]{:S(2)}, u32[]{:S(2)}) %collective-permute-start.1) | collective-permute-done | bytes 65568 | tf_op jit(solution)/shard_map/ppermute | solution.py:37
  13.1 1.8 %collective-permute-start.2 = (f32[2,2,64,128]{3,2,1,0:T(8,128)S(1)}, f32[2,2,64,128]{3,2,1,0:T(8,128)S(1)}, u32[]{:S(2)}, u32[]{:S(2)}) collective-permute-start(f32[2,2,64,128]{3,2,1,0:T(8,128)S(1)} %pad_maximum_fusion.2), channel_id=1, source_target_pairs={{0,4},{2,6},{4,0},{6,2},{1,5},{3,7},{5,1},{7,3},{8,12},{10,14},{12... | collective-permute-start | bytes 393224 | tf_op jit(solution)/shard_map/ppermute | solution.py:37
  14.9 0.1 maximum_maximum_fusion
  15.0 1.6 %collective-permute-start.3 = (f32[72,512]{1,0:T(8,128)S(1)}, f32[72,512]{1,0:T(8,128)S(1)}, u32[]{:S(2)}, u32[]{:S(2)}) collective-permute-start(f32[72,512]{1,0:T(8,128)S(1)} %maximum_maximum_fusion), channel_id=1, source_target_pairs={{0,2},{2,0},{4,6},{6,4},{1,3},{3,1},{5,7},{7,5},{8,10},{10,8},{12,... | collective-permute-start | bytes 442376 | tf_op jit(solution)/shard_map/ppermute | solution.py:37
  16.5 0.5 collective-permute-start.4
  17.0 1.5 %collective-permute-start.5 = (f32[72,512]{1,0:T(8,128)S(1)}, f32[72,512]{1,0:T(8,128)S(1)}, u32[]{:S(2)}, u32[]{:S(2)}) collective-permute-start(f32[72,512]{1,0:T(8,128)S(1)} %maximum_maximum_fusion), channel_id=1, source_target_pairs={{0,6},{2,4},{4,2},{6,0},{1,7},{3,5},{5,3},{7,1},{8,14},{10,12},{12... | collective-permute-start | bytes 442376 | tf_op jit(solution)/shard_map/ppermute | solution.py:37
  18.5 0.1 collective-permute-done.2
  18.7 0.0 copy-done.1
  18.7 4.6 %shard_map.106 = (f32[512,128]{1,0:T(8,128)S(1)}, f32[512,128]{1,0:T(8,128)S(1)}, f32[512,128]{1,0:T(8,128)S(1)}, f32[512,128]{1,0:T(8,128)S(1)}) custom-call(s32[4]{0:T(128)S(1)} %get-tuple-element.43.places_ref, s32[4]{0:T(128)S(1)} %pad_add_fusion.chunks_ref, f32[64,3]{1,0:T(8,128)S(1)} %bitcast.40, f32[4,2,64,128]{3,2,1,0:T(8,128)S(1)} %pad_maximum_fusion.1.edges_ref, ...), custom_call_target="tpu_custom_call" | custom-call | flops 402653184 | bytes 6291456 | tf_op jit(solution)/shard_map/pallas_call | solution.py:309
  23.2 0.0 collective-permute-done.3
  23.2 1.5 %collective-permute-done.4 = f32[72,512]{1,0:T(8,128)S(1)} collective-permute-done((f32[72,512]{1,0:T(8,128)S(1)}, f32[72,512]{1,0:T(8,128)S(1)}, u32[]{:S(2)}, u32[]{:S(2)}) %collective-permute-start.4) | collective-permute-done | bytes 147488 | tf_op jit(solution)/shard_map/ppermute | solution.py:37
  24.8 0.0 collective-permute-done.5
  24.8 0.1 collective-permute-start.6
  24.9 0.1 broadcast_add_fusion
  25.0 0.1 add.41.spots_ref
  25.0 0.1 pad_add_fusion.1.origin_ref
  25.1 1.6 %collective-permute-start.7 = (f32[512,128]{1,0:T(8,128)S(1)}, f32[512,128]{1,0:T(8,128)S(1)}, u32[]{:S(2)}, u32[]{:S(2)}) collective-permute-start(f32[512,128]{1,0:T(8,128)S(1)} %get-tuple-element.25.rest_3_), channel_id=1, source_target_pairs={{0,8},{8,0},{16,24},{24,16},{1,9},{9,1},{17,25},{25,17},{2,10},{10... | collective-permute-start | bytes 786440 | tf_op jit(solution)/shard_map/ppermute | solution.py:37
  26.7 0.4 collective-permute-start.8
  27.1 0.0 collective-permute-done.6.rest_5_
  27.1 6.9 %shard_map.107 = f32[32,512]{1,0:T(8,128)S(1)} custom-call(s32[4]{0:T(128)S(1)} %pad_add_fusion.chunks_ref, s32[2]{0:T(128)S(1)} %pad_add_fusion.1.origin_ref, s32[8]{0:T(128)S(1)} %add.41.spots_ref, f32[512,128]{1,0:T(8,128)S(1)} %get-tuple-element.22.rest_0_, f32[512,128]{1,0:T(8,128)S(1)} %get-tuple-element.23.rest_1_, ...), custom_call_target="tpu_custom_call" | custom-call | flops 4294967296 | bytes 4194304 | tf_op jit(solution)/shard_map/pallas_call | solution.py:330
  34.0 0.2 collective-permute-done.7
  34.3 2.7 %collective-permute-start.9 = (f32[512,128]{1,0:T(8,128)S(1)}, f32[512,128]{1,0:T(8,128)S(1)}, u32[]{:S(2)}, u32[]{:S(2)}) collective-permute-start(f32[512,128]{1,0:T(8,128)S(1)} %add.46), channel_id=1, source_target_pairs={{0,16},{8,24},{16,0},{24,8},{1,17},{9,25},{17,1},{25,9},{2,18},{10... | collective-permute-start | bytes 786440 | tf_op jit(solution)/shard_map/ppermute | solution.py:37
  37.0 0.1 copy.16
  37.0 15.9 %all_to_all.11 = f32[32,1,512]{2,1,0:T(1,128)S(1)} all-to-all(f32[32,1,512]{2,1,0:T(1,128)S(1)} %copy.16), channel_id=1, replica_groups=mesh['mem'=4,'lat'=4,'lon'=2] {'mem','lat','lon'}, dimensions={0} | all-to-all | bytes 131072 | tf_op jit(solution)/shard_map/all_to_all | solution.py:365
  52.9 0.0 collective-permute-done.8.rest_1_
  52.9 0.0 collective-permute-done.9.rest_2_
  52.9 0.8 %shard_map.108 = (f32[512,128]{1,0:T(8,128)}, f32[1,512]{1,0:T(1,128)}) custom-call(s32[1]{0:T(128)} %copy.20.count_ref, f32[1,512]{1,0:T(1,128)S(1)} %bitcast.46, f32[32,512]{1,0:T(8,128)S(1)} %bitcast.41, f32[512,128]{1,0:T(8,128)S(1)} %get-tuple-element.22.rest_0_, f32[512,128]{1,0:T(8,128)S(1)} %collective-permute-done.8.rest_1_, ...), custom_call_target="tpu_custom_call" | custom-call | flops 196608 | bytes 1572864 | tf_op jit(solution)/shard_map/pallas_call | solution.py:366
  (21 shorter events, 0.2 us)
Async XLA Ops:
  0.6 5.9 %copy-start = (bf16[4,16,32,128]{3,2,1,0:T(8,128)(2,1)S(1)}, bf16[4,16,32,128]{3,2,1,0:T(8,128)(2,1)}, u32[]{:S(2)}) copy-start(bf16[4,16,32,128]{3,2,1,0:T(8,128)(2,1)} %own_ref.1) | copy-start | bytes 1572868
  1.9 4.7 %collective-permute-start = (f32[4,16,32,128]{3,2,1,0:T(8,128)S(1)}, f32[4,16,32,128]{3,2,1,0:T(8,128)S(1)}, u32[]{:S(2)}, u32[]{:S(2)}) collective-permute-start(f32[4,16,32,128]{3,2,1,0:T(8,128)S(1)} %convert_element_type.24), channel_id=1, source_target_pairs={{0,1},{1,0},{2,3},{3,2},{4,5},{5,4},{6,7},{7,6},{8,9},{9,8},{10,11... | collective-permute-start | bytes 3145736 | tf_op jit(solution)/shard_map/ppermute | solution.py:37
  6.3 4.0 %copy-start.4 = (s32[512,1]{0,1:T(1,128)S(1)}, s32[512,1]{0,1:T(1,128)}, u32[]{:S(2)}) copy-start(s32[512,1]{0,1:T(1,128)} %param.15) | copy-start | bytes 6148
  6.3 4.0 %copy-start.5 = (s32[512]{0:T(512)S(1)}, s32[512]{0:T(512)}, u32[]{:S(2)}) copy-start(s32[512]{0:T(512)} %param.16) | copy-start | bytes 6148
  6.4 4.0 %copy-start.3 = (bf16[512,64]{0,1:T(8,128)(2,1)S(1)}, bf16[512,64]{0,1:T(8,128)(2,1)}, u32[]{:S(2)}) copy-start(bf16[512,64]{0,1:T(8,128)(2,1)} %param.13) | copy-start | bytes 196612
  6.6 12.1 %copy-start.1 = (bf16[4,64,32,128]{3,2,1,0:T(8,128)(2,1)S(1)}, bf16[4,64,32,128]{3,2,1,0:T(8,128)(2,1)}, u32[]{:S(2)}) copy-start(bf16[4,64,32,128]{3,2,1,0:T(8,128)(2,1)} %pert_ref.1) | copy-start | bytes 6291460
  7.7 5.3 %collective-permute-start.1 = (f32[1,2,64,128]{3,2,1,0:T(8,128)S(1)}, f32[1,2,64,128]{3,2,1,0:T(8,128)S(1)}, u32[]{:S(2)}, u32[]{:S(2)}) collective-permute-start(f32[1,2,64,128]{3,2,1,0:T(8,128)S(1)} %bitcast.42), channel_id=1, source_target_pairs={{0,2},{2,0},{4,6},{6,4},{1,3},{3,1},{5,7},{7,5},{8,10},{10,8},{12,... | collective-permute-start | bytes 196616 | tf_op jit(solution)/shard_map/ppermute | solution.py:37
  13.1 5.6 %collective-permute-start.2 = (f32[2,2,64,128]{3,2,1,0:T(8,128)S(1)}, f32[2,2,64,128]{3,2,1,0:T(8,128)S(1)}, u32[]{:S(2)}, u32[]{:S(2)}) collective-permute-start(f32[2,2,64,128]{3,2,1,0:T(8,128)S(1)} %pad_maximum_fusion.2), channel_id=1, source_target_pairs={{0,4},{2,6},{4,0},{6,2},{1,5},{3,7},{5,1},{7,3},{8,12},{10,14},{12... | collective-permute-start | bytes 393224 | tf_op jit(solution)/shard_map/ppermute | solution.py:37
  15.0 8.3 %collective-permute-start.3 = (f32[72,512]{1,0:T(8,128)S(1)}, f32[72,512]{1,0:T(8,128)S(1)}, u32[]{:S(2)}, u32[]{:S(2)}) collective-permute-start(f32[72,512]{1,0:T(8,128)S(1)} %maximum_maximum_fusion), channel_id=1, source_target_pairs={{0,2},{2,0},{4,6},{6,4},{1,3},{3,1},{5,7},{7,5},{8,10},{10,8},{12,... | collective-permute-start | bytes 442376 | tf_op jit(solution)/shard_map/ppermute | solution.py:37
  16.5 8.2 %collective-permute-start.4 = (f32[72,512]{1,0:T(8,128)S(1)}, f32[72,512]{1,0:T(8,128)S(1)}, u32[]{:S(2)}, u32[]{:S(2)}) collective-permute-start(f32[72,512]{1,0:T(8,128)S(1)} %maximum_maximum_fusion), channel_id=1, source_target_pairs={{0,4},{2,6},{4,0},{6,2},{1,5},{3,7},{5,1},{7,3},{8,12},{10,14},{12... | collective-permute-start | bytes 442376 | tf_op jit(solution)/shard_map/ppermute | solution.py:37
  17.0 7.7 %collective-permute-start.5 = (f32[72,512]{1,0:T(8,128)S(1)}, f32[72,512]{1,0:T(8,128)S(1)}, u32[]{:S(2)}, u32[]{:S(2)}) collective-permute-start(f32[72,512]{1,0:T(8,128)S(1)} %maximum_maximum_fusion), channel_id=1, source_target_pairs={{0,6},{2,4},{4,2},{6,0},{1,7},{3,5},{5,3},{7,1},{8,14},{10,12},{12... | collective-permute-start | bytes 442376 | tf_op jit(solution)/shard_map/ppermute | solution.py:37
  24.8 2.3 %collective-permute-start.6 = (f32[4,72,512]{2,1,0:T(8,128)S(1)}, f32[4,72,512]{2,1,0:T(8,128)S(1)}, u32[]{:S(2)}, u32[]{:S(2)}) collective-permute-start(f32[4,72,512]{2,1,0:T(8,128)S(1)} %pad_maximum_fusion.rest_4_), channel_id=1, source_target_pairs={{0,1},{1,0},{2,3},{3,2},{4,5},{5,4},{6,7},{7,6},{8,9},{9,8},{10,11... | collective-permute-start | bytes 1769480 | tf_op jit(solution)/shard_map/ppermute | solution.py:37
  25.1 9.1 %collective-permute-start.7 = (f32[512,128]{1,0:T(8,128)S(1)}, f32[512,128]{1,0:T(8,128)S(1)}, u32[]{:S(2)}, u32[]{:S(2)}) collective-permute-start(f32[512,128]{1,0:T(8,128)S(1)} %get-tuple-element.25.rest_3_), channel_id=1, source_target_pairs={{0,8},{8,0},{16,24},{24,16},{1,9},{9,1},{17,25},{25,17},{2,10},{10... | collective-permute-start | bytes 786440 | tf_op jit(solution)/shard_map/ppermute | solution.py:37
  26.7 26.2 %collective-permute-start.8 = (f32[512,128]{1,0:T(8,128)S(1)}, f32[512,128]{1,0:T(8,128)S(1)}, u32[]{:S(2)}, u32[]{:S(2)}) collective-permute-start(f32[512,128]{1,0:T(8,128)S(1)} %get-tuple-element.23.rest_1_), channel_id=1, source_target_pairs={{0,8},{8,0},{16,24},{24,16},{1,9},{9,1},{17,25},{25,17},{2,10},{10... | collective-permute-start | bytes 786440 | tf_op jit(solution)/shard_map/ppermute | solution.py:37
  27.1 25.8 %copy-start.2 = (f32[512]{0:T(512)S(1)}, f32[512]{0:T(512)}, u32[]{:S(2)}) copy-start(f32[512]{0:T(512)} %param.14) | copy-start | bytes 6148
  34.3 18.7 %collective-permute-start.9 = (f32[512,128]{1,0:T(8,128)S(1)}, f32[512,128]{1,0:T(8,128)S(1)}, u32[]{:S(2)}, u32[]{:S(2)}) collective-permute-start(f32[512,128]{1,0:T(8,128)S(1)} %add.46), channel_id=1, source_target_pairs={{0,16},{8,24},{16,0},{24,8},{1,17},{9,25},{17,1},{25,9},{2,18},{10... | collective-permute-start | bytes 786440 | tf_op jit(solution)/shard_map/ppermute | solution.py:37

commit v3 on v2

--- a/solution.py
+++ b/solution.py
@@ -15,7 +15,7 @@
 
 def params(flops, moved, held):
     return dict(
-        compiler_params=pltpu.CompilerParams(vmem_limit_bytes=held + 6 * 2**20),
+        compiler_params=pltpu.CompilerParams(vmem_limit_bytes=held + 2 * 2**20),
         cost_estimate=pl.CostEstimate(flops=flops, bytes_accessed=moved, transcendentals=0),
     )
 
@@ -71,6 +71,7 @@
     members, modes, rows, cols = own_ref.shape
     sources = matrix_ref.shape[1] // cols
     lines = members * modes
+    pitch = field_ref.shape[0] // rows
     for k in range(modes):
         pieces = [jnp.concatenate([own_ref[m, k] for m in range(members)])]
         for s in range(1, sources):
@@ -82,11 +83,11 @@
         )
         made = both[:, :cols] + both[:, cols:]
         for m in range(members):
-            field_ref[pl.ds(m * modes + k, rows, stride=lines), :] = made[m * rows : (m + 1) * rows]
+            field_ref[pl.ds(m * modes + k, rows, stride=pitch), :] = made[m * rows : (m + 1) * rows]
     decay = jnp.broadcast_to(table_ref[:, 1:2], (lines, cols))
     state = jnp.zeros((lines, cols), F32)
     for x in range(rows):
-        state = decay * state + field_ref[x * lines : (x + 1) * lines, :]
+        state = decay * state + field_ref[x * pitch : x * pitch + lines, :]
         first[x * lines : (x + 1) * lines, :] = state
     edge_ref[0] = state
     state = jnp.zeros((lines, cols), F32)
@@ -98,16 +99,18 @@
 def sum_kernel(
     scale, places_ref, chunks_ref, table_ref, edges_ref, field_ref, modes_ref, pert_ref, *rest
 ):
-    chunks = len(rest) - 3
-    outs, (first, second, pert) = rest[:chunks], rest[chunks:]
+    chunks = len(rest) - 4
+    outs, (first, second, pert, turned) = rest[:chunks], rest[chunks:]
     members, levels, rows, cols = pert_ref.shape
     lines, kinds = table_ref.shape[0], table_ref.shape[0] // members
     share = levels // chunks
     count = edges_ref.shape[0]
+    pitch = pert.shape[0] // (members * levels)
+    field_pitch = field_ref.shape[0] // rows
 
     for m in range(members):
         for z in range(levels):
-            at = (m * levels + z) * rows
+            at = (m * levels + z) * pitch
             pert[at : at + rows, :] = pert_ref[m, z].astype(F32)
 
     log, decay, beta = (
@@ -130,7 +133,7 @@
         after = after + power(there - own - 1) * (edges_ref[s, 1] + beta * before)
 
     for x in range(rows):
-        state = decay * state + field_ref[x * lines : (x + 1) * lines, :]
+        state = decay * state + field_ref[x * field_pitch : x * field_pitch + lines, :]
         first[x * lines : (x + 1) * lines, :] = state
     state = after
     for x in reversed(range(rows)):
@@ -138,8 +141,9 @@
         high, low = halve(state)
         second[:, x * cols : (x + 1) * cols] = jnp.concatenate([high, low, high])
 
-    held = jnp.concatenate([modes_ref[pl.ds(chunks_ref[r] * share, share), :] for r in range(chunks)])
-    held = jnp.concatenate([held * scale] * members, axis=1)
+    turned[...] = (modes_ref[...] * scale).T
+    held = jnp.concatenate([turned[pl.ds(chunks_ref[r] * share, share), :] for r in range(chunks)])
+    held = jnp.concatenate([held] * members, axis=1)
     member = lax.broadcasted_iota(jnp.int32, (levels, lines), 1) // kinds
     high, low = halve(
         jnp.concatenate([jnp.where(member == m, held, 0.0) for m in range(members)])
@@ -157,11 +161,11 @@
             for r in range(chunks):
                 total = None
                 for m in range(members):
-                    at = (m * levels + chunks_ref[r] * share) * rows + x
+                    at = (m * levels + chunks_ref[r] * share) * pitch + x
                     line = m * levels + r * share
                     term = (
                         profile[line : line + share, half * cols : (half + 1) * cols]
-                        * pert[pl.ds(at, share, stride=rows), :]
+                        * pert[pl.ds(at, share, stride=pitch), :]
                     )
                     total = term if total is None else total + term
                 outs[r][pl.ds(x, share, stride=rows), :] = total
@@ -269,7 +273,7 @@
     field, edge = pl.pallas_call(
         columns_kernel,
         out_shape=(
-            jax.ShapeDtypeStruct((rows * lines, cols), F32),
+            jax.ShapeDtypeStruct((rows * (lines + 8), cols), F32),
             jax.ShapeDtypeStruct((2, lines, cols), F32),
         ),
         in_specs=[VMEM] * 4,
@@ -314,14 +318,15 @@
         scratch_shapes=[
             pltpu.VMEM((rows * lines, cols), F32),
             pltpu.VMEM((3 * lines, rows * cols), BF16),
-            pltpu.VMEM((members * levels * rows, cols), F32),
+            pltpu.VMEM((members * levels * (rows + 4), cols), F32),
+            pltpu.VMEM((levels, kinds), F32),
         ],
         **params(
             6 * members * levels * lines * rows * cols,
             6 * 2**20,
-            (6 * members + 4) * levels * rows * cols + 14 * lines * rows * cols,
+            (7 * members + 4) * levels * rows * cols + 14 * lines * rows * cols,
         ),
-    )(lats, chunks, table, edges, field, modes, perturbation)
+    )(lats, chunks, table, edges, field, modes.T, perturbation)
 
 
     tiles = n_lat * n_lon

time: 53.9 us -> 51.7 us (0.959)
  Pallas kernels: 14.6 us -> 12.1 us
  waiting for transfers between devices: 4.51 us -> 6.45 us
  blocking collectives: 15.9 us -> 15 us
  local copies, waits for them, and re-layouts: 1.24 us -> 0.46 us
    pallas_call x1, Pallas kernels: 4.56 us -> 2.6 us  [per_device(): pl.pallas_call(functools.partial(sum_kernel, 1.0 / math.sqrt(members * n_...]
    ppermute x10, waiting for transfers between devices: 4.51 us -> 6.45 us  [send(): lax.ppermute(block, axis, [(i, toward(i, step, count)) for i in range(cou...]
    all_to_all x1, blocking collectives: 15.9 us -> 15 us  [per_device(): back = lax.all_to_all(leaving, ('mem', 'lat', 'lon'), 0, 0, tiled=True)]
    unnamed x14 -> x15, local copies, waits for them, and re-layouts: 0.82 us -> 0.04 us
  transfers between devices with their start and end apart: 10 -> 10, of which waited for: 4 -> 4; matrix products, arithmetic and copies ran while one was open for 5% -> 4% of each run, Pallas kernels for 24% -> 21%
where the time goes in v3:
time: 51.7 us; the launch traced here: 51.6 us
  blocking collectives  15 us (29%)
  starting transfers between devices  13.3 us (26%)
  Pallas kernels  12.1 us (23%)
  waiting for transfers between devices  6.45 us (12%)
  other arithmetic  2.71 us (5%)
  between operations  1.53 us (3%)
    all_to_all x1, blocking collectives, per_device(): back = lax.all_to_all(leaving, ('mem', 'lat', 'lon'), 0, 0, tiled=True)  15 us
    ppermute x10, starting transfers between devices, send(): lax.ppermute(block, axis, [(i, toward(i, step, count)) for i in range(cou...  13.3 us
    pallas_call x1, Pallas kernels, per_device(): pl.pallas_call(functools.partial(observe_kernel, levels, rows), out_shape...  6.85 us
    ppermute x10, waiting for transfers between devices, send(): lax.ppermute(block, axis, [(i, toward(i, step, count)) for i in range(cou...  6.45 us
    pallas_call x1, Pallas kernels, per_device(): pl.pallas_call(functools.partial(sum_kernel, 1.0 / math.sqrt(members * n_...  2.6 us
    pallas_call x1, Pallas kernels, per_device(): pl.pallas_call(matrix_kernel, out_shape=jax.ShapeDtypeStruct((kinds, all_...  1.26 us
    convert_element_type x1, other arithmetic, per_device(): whole = control.astype(F32)  1.22 us
  transfers between devices with their start and end apart: 10, of which 4 were waited for; matrix products, arithmetic and copies ran while one was open for 4% of the time, Pallas kernels for 21%

profile of v3, /device:TPU:0, one launch (start us, length us, event | category | flops | bytes accessed | tf_op | source)
XLA Modules:
  0.0 51.6 jit_solution(12188333745176319915)
XLA Ops:
  0.6 1.2 %convert_element_type.24 = f32[4,16,32,128]{3,2,1,0:T(8,128)S(1)} convert(bf16[4,16,32,128]{3,2,1,0:T(8,128)(2,1)} %own_ref.1) | non-fusion elementwise | flops 262144 | bytes 1572864 | tf_op jit(solution)/shard_map/convert_element_type | solution.py:270
  1.9 0.5 %collective-permute-start = (f32[4,16,32,128]{3,2,1,0:T(8,128)S(1)}, f32[4,16,32,128]{3,2,1,0:T(8,128)S(1)}, u32[]{:S(2)}, u32[]{:S(2)}) collective-permute-start(f32[4,16,32,128]{3,2,1,0:T(8,128)S(1)} %convert_element_type.24), channel_id=1, source_target_pairs={{0,1},{1,0},{2,3},{3,2},{4,5},{5,4},{6,7},{7,6},{8,9},{9,8},{10,11... | collective-permute-start | bytes 3145736 | tf_op jit(solution)/shard_map/ppermute | solution.py:37
  2.4 0.7 %subtract_multiply_fusion = (f32[16]{0:T(128)S(1)}, f32[16]{0:T(128)S(1)}) fusion(f32[16]{0:T(128)} %param.11), kind=kLoop, calls=%fused_computation.44 | loop fusion | flops 48 | bytes 192 | tf_op jit(solution)/shard_map/mul | solution.py:255
  3.1 0.1 negate_multiply_fusion.1
  3.2 0.1 copy.13.from_ref
  3.3 0.1 copy.12
  4.1 0.1 pad.6.clone
  4.1 0.1 broadcast_multiply_fusion
  4.2 0.1 negate_multiply_fusion.2.to_ref
  4.3 1.3 %shard_map.104.matrix_ref = bf16[16,256,256]{2,1,0:T(8,128)(2,1)S(1)} custom-call(s32[2]{0:T(128)S(1)} %get-tuple-element.40.starts_ref, f32[16]{0:T(128)S(1)} %get-tuple-element.51.log_ref, f32[16,128]{1,0:T(8,128)S(1)} %negate_multiply_fusion.2.to_ref, f32[2,128,16]{2,1,0:T(8,128)S(1)} %copy.13.from_ref), custom_call_target="tpu_custom_call" | custom-call | flops 4194304 | bytes 2097152 | tf_op jit(solution)/shard_map/pallas_call | solution.py:257
  5.6 0.0 copy-start.5
  5.6 0.0 copy-start.6
  5.6 0.0 copy-start.4
  5.6 0.1 pad_add_fusion.chunks_ref
  5.7 0.1 broadcast_multiply_fusion.2
  5.8 0.0 collective-permute-done
  5.8 0.0 copy-start.1
  5.8 0.0 copy-start.2
  5.8 0.6 %shard_map.105 = (f32[2304,128]{1,0:T(8,128)S(1)}, f32[2,64,128]{2,1,0:T(8,128)S(1)}) custom-call(bf16[4,16,32,128]{3,2,1,0:T(8,128)(2,1)S(1)} %copy-done, f32[1,4,16,32,128]{4,3,2,1,0:T(8,128)S(1)} %bitcast.39, bf16[16,256,256]{2,1,0:T(8,128)(2,1)S(1)} %shard_map.104.matrix_ref, f32[64,3]{1,0:T(8,128)S(1)} %bitcast.40), custom_call_target="tpu_custom_call" | custom-call | flops 268435456 | bytes 4194304 | tf_op jit(solution)/shard_map/pallas_call | solution.py:273
  6.4 2.6 %collective-permute-start.1 = (f32[1,2,64,128]{3,2,1,0:T(8,128)S(1)}, f32[1,2,64,128]{3,2,1,0:T(8,128)S(1)}, u32[]{:S(2)}, u32[]{:S(2)}) collective-permute-start(f32[1,2,64,128]{3,2,1,0:T(8,128)S(1)} %bitcast.43), channel_id=1, source_target_pairs={{0,2},{2,0},{4,6},{6,4},{1,3},{3,1},{5,7},{7,5},{8,10},{10,8},{12,... | collective-permute-start | bytes 196616 | tf_op jit(solution)/shard_map/ppermute | solution.py:37
  9.0 0.0 copy-done.6
  9.1 2.7 %collective-permute-done.1 = f32[1,2,64,128]{3,2,1,0:T(8,128)S(1)} collective-permute-done((f32[1,2,64,128]{3,2,1,0:T(8,128)S(1)}, f32[1,2,64,128]{3,2,1,0:T(8,128)S(1)}, u32[]{:S(2)}, u32[]{:S(2)}) %collective-permute-start.1) | collective-permute-done | bytes 65568 | tf_op jit(solution)/shard_map/ppermute | solution.py:37
  11.8 1.8 %collective-permute-start.2 = (f32[2,2,64,128]{3,2,1,0:T(8,128)S(1)}, f32[2,2,64,128]{3,2,1,0:T(8,128)S(1)}, u32[]{:S(2)}, u32[]{:S(2)}) collective-permute-start(f32[2,2,64,128]{3,2,1,0:T(8,128)S(1)} %pad_maximum_fusion.2), channel_id=1, source_target_pairs={{0,4},{2,6},{4,0},{6,2},{1,5},{3,7},{5,1},{7,3},{8,12},{10,14},{12... | collective-permute-start | bytes 393224 | tf_op jit(solution)/shard_map/ppermute | solution.py:37
  13.6 0.1 maximum_maximum_fusion
  13.7 1.6 %collective-permute-start.3 = (f32[72,512]{1,0:T(8,128)S(1)}, f32[72,512]{1,0:T(8,128)S(1)}, u32[]{:S(2)}, u32[]{:S(2)}) collective-permute-start(f32[72,512]{1,0:T(8,128)S(1)} %maximum_maximum_fusion), channel_id=1, source_target_pairs={{0,2},{2,0},{4,6},{6,4},{1,3},{3,1},{5,7},{7,5},{8,10},{10,8},{12,... | collective-permute-start | bytes 442376 | tf_op jit(solution)/shard_map/ppermute | solution.py:37
  15.2 0.5 collective-permute-start.4
  15.7 1.5 %collective-permute-start.5 = (f32[72,512]{1,0:T(8,128)S(1)}, f32[72,512]{1,0:T(8,128)S(1)}, u32[]{:S(2)}, u32[]{:S(2)}) collective-permute-start(f32[72,512]{1,0:T(8,128)S(1)} %maximum_maximum_fusion), channel_id=1, source_target_pairs={{0,6},{2,4},{4,2},{6,0},{1,7},{3,5},{5,3},{7,1},{8,14},{10,12},{12... | collective-permute-start | bytes 442376 | tf_op jit(solution)/shard_map/ppermute | solution.py:37
  17.2 0.1 collective-permute-done.2
  17.4 0.0 copy-done.2
  17.4 2.6 %shard_map.106 = (f32[512,128]{1,0:T(8,128)S(1)}, f32[512,128]{1,0:T(8,128)S(1)}, f32[512,128]{1,0:T(8,128)S(1)}, f32[512,128]{1,0:T(8,128)S(1)}) custom-call(s32[4]{0:T(128)S(1)} %get-tuple-element.43.places_ref, s32[4]{0:T(128)S(1)} %pad_add_fusion.chunks_ref, f32[64,3]{1,0:T(8,128)S(1)} %bitcast.41, f32[4,2,64,128]{3,2,1,0:T(8,128)S(1)} %pad_maximum_fusion.1.edges_ref, ...), custom_call_target="tpu_custom_call" | custom-call | flops 402653184 | bytes 6291456 | tf_op jit(solution)/shard_map/pallas_call | solution.py:313
  20.0 0.0 collective-permute-done.3
  20.0 3.4 %collective-permute-done.4 = f32[72,512]{1,0:T(8,128)S(1)} collective-permute-done((f32[72,512]{1,0:T(8,128)S(1)}, f32[72,512]{1,0:T(8,128)S(1)}, u32[]{:S(2)}, u32[]{:S(2)}) %collective-permute-start.4) | collective-permute-done | bytes 147488 | tf_op jit(solution)/shard_map/ppermute | solution.py:37
  23.5 0.0 collective-permute-done.5
  23.5 0.1 collective-permute-start.6
  23.6 0.1 broadcast_add_fusion
  23.7 0.1 add.41.spots_ref
  23.7 0.1 pad_add_fusion.1.origin_ref
  23.8 1.6 %collective-permute-start.7 = (f32[512,128]{1,0:T(8,128)S(1)}, f32[512,128]{1,0:T(8,128)S(1)}, u32[]{:S(2)}, u32[]{:S(2)}) collective-permute-start(f32[512,128]{1,0:T(8,128)S(1)} %get-tuple-element.25.rest_3_), channel_id=1, source_target_pairs={{0,8},{8,0},{16,24},{24,16},{1,9},{9,1},{17,25},{25,17},{2,10},{10... | collective-permute-start | bytes 786440 | tf_op jit(solution)/shard_map/ppermute | solution.py:37
  25.4 0.4 collective-permute-start.8
  25.8 0.0 collective-permute-done.6.rest_5_
  25.9 6.9 %shard_map.107 = f32[32,512]{1,0:T(8,128)S(1)} custom-call(s32[4]{0:T(128)S(1)} %pad_add_fusion.chunks_ref, s32[2]{0:T(128)S(1)} %pad_add_fusion.1.origin_ref, s32[8]{0:T(128)S(1)} %add.41.spots_ref, f32[512,128]{1,0:T(8,128)S(1)} %get-tuple-element.22.rest_0_, f32[512,128]{1,0:T(8,128)S(1)} %get-tuple-element.23.rest_1_, ...), custom_call_target="tpu_custom_call" | custom-call | flops 4294967296 | bytes 4194304 | tf_op jit(solution)/shard_map/pallas_call | solution.py:335
  32.7 0.2 collective-permute-done.7
  33.0 2.7 %collective-permute-start.9 = (f32[512,128]{1,0:T(8,128)S(1)}, f32[512,128]{1,0:T(8,128)S(1)}, u32[]{:S(2)}, u32[]{:S(2)}) collective-permute-start(f32[512,128]{1,0:T(8,128)S(1)} %add.46), channel_id=1, source_target_pairs={{0,16},{8,24},{16,0},{24,8},{1,17},{9,25},{17,1},{25,9},{2,18},{10... | collective-permute-start | bytes 786440 | tf_op jit(solution)/shard_map/ppermute | solution.py:37
  35.7 0.1 copy.14
  35.7 15.0 %all_to_all.11 = f32[32,1,512]{2,1,0:T(1,128)S(1)} all-to-all(f32[32,1,512]{2,1,0:T(1,128)S(1)} %copy.14), channel_id=1, replica_groups=mesh['mem'=4,'lat'=4,'lon'=2] {'mem','lat','lon'}, dimensions={0} | all-to-all | bytes 131072 | tf_op jit(solution)/shard_map/all_to_all | solution.py:370
  50.8 0.0 collective-permute-done.8.rest_1_
  50.8 0.0 collective-permute-done.9.rest_2_
  50.8 0.8 %shard_map.108 = (f32[512,128]{1,0:T(8,128)}, f32[1,512]{1,0:T(1,128)}) custom-call(s32[1]{0:T(128)} %copy.18.count_ref, f32[1,512]{1,0:T(1,128)S(1)} %bitcast.48, f32[32,512]{1,0:T(8,128)S(1)} %bitcast.42, f32[512,128]{1,0:T(8,128)S(1)} %get-tuple-element.22.rest_0_, f32[512,128]{1,0:T(8,128)S(1)} %collective-permute-done.8.rest_1_, ...), custom_call_target="tpu_custom_call" | custom-call | flops 196608 | bytes 1572864 | tf_op jit(solution)/shard_map/pallas_call | solution.py:371
  (22 shorter events, 0.2 us)
Async XLA Ops:
  0.6 5.2 %copy-start = (bf16[4,16,32,128]{3,2,1,0:T(8,128)(2,1)S(1)}, bf16[4,16,32,128]{3,2,1,0:T(8,128)(2,1)}, u32[]{:S(2)}) copy-start(bf16[4,16,32,128]{3,2,1,0:T(8,128)(2,1)} %own_ref.1) | copy-start | bytes 1572868
  1.9 3.9 %collective-permute-start = (f32[4,16,32,128]{3,2,1,0:T(8,128)S(1)}, f32[4,16,32,128]{3,2,1,0:T(8,128)S(1)}, u32[]{:S(2)}, u32[]{:S(2)}) collective-permute-start(f32[4,16,32,128]{3,2,1,0:T(8,128)S(1)} %convert_element_type.24), channel_id=1, source_target_pairs={{0,1},{1,0},{2,3},{3,2},{4,5},{5,4},{6,7},{7,6},{8,9},{9,8},{10,11... | collective-permute-start | bytes 3145736 | tf_op jit(solution)/shard_map/ppermute | solution.py:37
  5.6 3.5 %copy-start.5 = (s32[512,1]{0,1:T(1,128)S(1)}, s32[512,1]{0,1:T(1,128)}, u32[]{:S(2)}) copy-start(s32[512,1]{0,1:T(1,128)} %param.15) | copy-start | bytes 6148
  5.6 3.4 %copy-start.6 = (s32[512]{0:T(512)S(1)}, s32[512]{0:T(512)}, u32[]{:S(2)}) copy-start(s32[512]{0:T(512)} %param.16) | copy-start | bytes 6148
  5.6 3.5 %copy-start.4 = (bf16[512,64]{0,1:T(8,128)(2,1)S(1)}, bf16[512,64]{0,1:T(8,128)(2,1)}, u32[]{:S(2)}) copy-start(bf16[512,64]{0,1:T(8,128)(2,1)} %param.13) | copy-start | bytes 196612
  5.8 11.6 %copy-start.1 = (bf16[4,64,32,128]{3,2,1,0:T(8,128)(2,1)S(1)}, bf16[4,64,32,128]{3,2,1,0:T(8,128)(2,1)}, u32[]{:S(2)}) copy-start(bf16[4,64,32,128]{3,2,1,0:T(8,128)(2,1)} %pert_ref.1) | copy-start | bytes 6291460
  5.8 11.6 %copy-start.2 = (f32[64,16]{0,1:T(8,128)S(1)}, f32[64,16]{0,1:T(8,128)}, u32[]{:S(2)}) copy-start(f32[64,16]{0,1:T(8,128)} %param.12) | copy-start | bytes 12292
  6.4 5.3 %collective-permute-start.1 = (f32[1,2,64,128]{3,2,1,0:T(8,128)S(1)}, f32[1,2,64,128]{3,2,1,0:T(8,128)S(1)}, u32[]{:S(2)}, u32[]{:S(2)}) collective-permute-start(f32[1,2,64,128]{3,2,1,0:T(8,128)S(1)} %bitcast.43), channel_id=1, source_target_pairs={{0,2},{2,0},{4,6},{6,4},{1,3},{3,1},{5,7},{7,5},{8,10},{10,8},{12,... | collective-permute-start | bytes 196616 | tf_op jit(solution)/shard_map/ppermute | solution.py:37
  11.8 5.6 %collective-permute-start.2 = (f32[2,2,64,128]{3,2,1,0:T(8,128)S(1)}, f32[2,2,64,128]{3,2,1,0:T(8,128)S(1)}, u32[]{:S(2)}, u32[]{:S(2)}) collective-permute-start(f32[2,2,64,128]{3,2,1,0:T(8,128)S(1)} %pad_maximum_fusion.2), channel_id=1, source_target_pairs={{0,4},{2,6},{4,0},{6,2},{1,5},{3,7},{5,1},{7,3},{8,12},{10,14},{12... | collective-permute-start | bytes 393224 | tf_op jit(solution)/shard_map/ppermute | solution.py:37
  13.7 6.3 %collective-permute-start.3 = (f32[72,512]{1,0:T(8,128)S(1)}, f32[72,512]{1,0:T(8,128)S(1)}, u32[]{:S(2)}, u32[]{:S(2)}) collective-permute-start(f32[72,512]{1,0:T(8,128)S(1)} %maximum_maximum_fusion), channel_id=1, source_target_pairs={{0,2},{2,0},{4,6},{6,4},{1,3},{3,1},{5,7},{7,5},{8,10},{10,8},{12,... | collective-permute-start | bytes 442376 | tf_op jit(solution)/shard_map/ppermute | solution.py:37
  15.2 8.2 %collective-permute-start.4 = (f32[72,512]{1,0:T(8,128)S(1)}, f32[72,512]{1,0:T(8,128)S(1)}, u32[]{:S(2)}, u32[]{:S(2)}) collective-permute-start(f32[72,512]{1,0:T(8,128)S(1)} %maximum_maximum_fusion), channel_id=1, source_target_pairs={{0,4},{2,6},{4,0},{6,2},{1,5},{3,7},{5,1},{7,3},{8,12},{10,14},{12... | collective-permute-start | bytes 442376 | tf_op jit(solution)/shard_map/ppermute | solution.py:37
  15.7 7.7 %collective-permute-start.5 = (f32[72,512]{1,0:T(8,128)S(1)}, f32[72,512]{1,0:T(8,128)S(1)}, u32[]{:S(2)}, u32[]{:S(2)}) collective-permute-start(f32[72,512]{1,0:T(8,128)S(1)} %maximum_maximum_fusion), channel_id=1, source_target_pairs={{0,6},{2,4},{4,2},{6,0},{1,7},{3,5},{5,3},{7,1},{8,14},{10,12},{12... | collective-permute-start | bytes 442376 | tf_op jit(solution)/shard_map/ppermute | solution.py:37
  23.5 2.3 %collective-permute-start.6 = (f32[4,72,512]{2,1,0:T(8,128)S(1)}, f32[4,72,512]{2,1,0:T(8,128)S(1)}, u32[]{:S(2)}, u32[]{:S(2)}) collective-permute-start(f32[4,72,512]{2,1,0:T(8,128)S(1)} %pad_maximum_fusion.rest_4_), channel_id=1, source_target_pairs={{0,1},{1,0},{2,3},{3,2},{4,5},{5,4},{6,7},{7,6},{8,9},{9,8},{10,11... | collective-permute-start | bytes 1769480 | tf_op jit(solution)/shard_map/ppermute | solution.py:37
  23.8 9.1 %collective-permute-start.7 = (f32[512,128]{1,0:T(8,128)S(1)}, f32[512,128]{1,0:T(8,128)S(1)}, u32[]{:S(2)}, u32[]{:S(2)}) collective-permute-start(f32[512,128]{1,0:T(8,128)S(1)} %get-tuple-element.25.rest_3_), channel_id=1, source_target_pairs={{0,8},{8,0},{16,24},{24,16},{1,9},{9,1},{17,25},{25,17},{2,10},{10... | collective-permute-start | bytes 786440 | tf_op jit(solution)/shard_map/ppermute | solution.py:37
  25.4 25.3 %collective-permute-start.8 = (f32[512,128]{1,0:T(8,128)S(1)}, f32[512,128]{1,0:T(8,128)S(1)}, u32[]{:S(2)}, u32[]{:S(2)}) collective-permute-start(f32[512,128]{1,0:T(8,128)S(1)} %get-tuple-element.23.rest_1_), channel_id=1, source_target_pairs={{0,8},{8,0},{16,24},{24,16},{1,9},{9,1},{17,25},{25,17},{2,10},{10... | collective-permute-start | bytes 786440 | tf_op jit(solution)/shard_map/ppermute | solution.py:37
  25.9 24.9 %copy-start.3 = (f32[512]{0:T(512)S(1)}, f32[512]{0:T(512)}, u32[]{:S(2)}) copy-start(f32[512]{0:T(512)} %param.14) | copy-start | bytes 6148
  33.0 17.8 %collective-permute-start.9 = (f32[512,128]{1,0:T(8,128)S(1)}, f32[512,128]{1,0:T(8,128)S(1)}, u32[]{:S(2)}, u32[]{:S(2)}) collective-permute-start(f32[512,128]{1,0:T(8,128)S(1)} %add.46), channel_id=1, source_target_pairs={{0,16},{8,24},{16,0},{24,8},{1,17},{9,25},{17,1},{25,9},{2,18},{10... | collective-permute-start | bytes 786440 | tf_op jit(solution)/shard_map/ppermute | solution.py:37

commit v4 on v3

--- a/solution.py
+++ b/solution.py
@@ -62,7 +62,7 @@
         distance = jnp.abs(across - down).astype(F32)
         for k in range(modes):
             end = jnp.where(across >= down, to_ref[k : k + 1, :], from_ref[s, :, k : k + 1])
-            high, low = halve(jnp.exp(distance * log_ref[k]) * end)
+            high, low = halve(jnp.exp(distance * log_ref[k : k + 1, :1]) * end)
             at = s * cols
             matrix_ref[k, at : at + cols, :] = jnp.concatenate([high, low], axis=1)
 
@@ -171,15 +171,8 @@
                 outs[r][pl.ds(x, share, stride=rows), :] = total
 
 
-def observe_kernel(levels, rows, chunks_ref, origin_ref, spots_ref, *rest):
-    chunks, tiles = chunks_ref.shape[0], spots_ref.shape[0]
-    sums, packs, (out_ref, split) = rest[:chunks], rest[chunks:-2], rest[-2:]
-    slots = out_ref.shape[1]
-    step, cols = sums[0].shape
-    for r in range(chunks):
-        high, low = halve(sums[r][...])
-        at = pl.multiple_of(chunks_ref[r] * step, step)
-        split[pl.ds(at, step), :] = jnp.concatenate([high, low], axis=1)
+def observed(levels, rows, origin_ref, packed_ref, block, split):
+    slots, cols = packed_ref.shape[2], split.shape[1] // 2
 
     def spread(fine, origin, length):
         near = jnp.floor(fine * 0.5)
@@ -188,26 +181,49 @@
         return jnp.where(cell == near, 0.75, 0.0) + jnp.where(cell == far, 0.25, 0.0)
 
     group = math.gcd(levels, 16)
-    before = 0
+    fine = packed_ref[block, levels : levels + 8, :]
+    across = spread(fine[1:2], origin_ref[1], cols).astype(BF16)
+    across = jnp.concatenate([across, across])
+    down = spread(fine[0:1], origin_ref[0], rows)
+    total = jnp.zeros((rows, slots), F32)
+    for g in range(0, levels, group):
+        seen = jnp.dot(
+            split[g * rows : (g + group) * rows, :], across, preferred_element_type=F32
+        )
+        weights = packed_ref[block, g : g + group, :]
+        for z in range(group):
+            total = total + seen[z * rows : (z + 1) * rows] * weights[z : z + 1]
+    return jnp.sum(total * down, axis=0, keepdims=True)
+
+
+def near_kernel(levels, rows, chunks_ref, origin_ref, *rest):
+    chunks = chunks_ref.shape[0]
+    sums, packs, (out_ref, split) = rest[:chunks], rest[chunks:-2], rest[-2:]
+    step = sums[0].shape[0]
+    for r in range(chunks):
+        high, low = halve(sums[r][...])
+        at = pl.multiple_of(chunks_ref[r] * step, step)
+        split[pl.ds(at, step), :] = jnp.concatenate([high, low], axis=1)
+    for i, packed_ref in enumerate(packs):
+        out_ref[i : i + 1, :] = observed(levels, rows, origin_ref, packed_ref, 0, split)
+
+
+def far_kernel(levels, rows, origin_ref, spots_ref, split, near_ref, *rest):
+    packs, out_ref = rest[:-1], rest[-1]
+    tiles = spots_ref.shape[0]
+
+    def put(place, row):
+        for copy in range(out_ref.shape[0] // tiles):
+            out_ref[pl.ds(copy * tiles + spots_ref[place], 1), :] = row
+
+    before = near_ref.shape[0]
+    for i in range(before):
+        put(i, near_ref[i : i + 1, :])
     for packed_ref in packs:
 
         @pl.loop(0, packed_ref.shape[0])
         def _(block, packed_ref=packed_ref, before=before):
-            fine = packed_ref[block, levels : levels + 8, :]
-            across = spread(fine[1:2], origin_ref[1], cols).astype(BF16)
-            across = jnp.concatenate([across, across])
-            down = spread(fine[0:1], origin_ref[0], rows)
-            total = jnp.zeros((rows, slots), F32)
-            for g in range(0, levels, group):
-                seen = jnp.dot(
-                    split[g * rows : (g + group) * rows, :], across, preferred_element_type=F32
-                )
-                weights = packed_ref[block, g : g + group, :]
-                for z in range(group):
-                    total = total + seen[z * rows : (z + 1) * rows] * weights[z : z + 1]
-            row = jnp.sum(total * down, axis=0, keepdims=True)
-            for copy in range(out_ref.shape[0] // tiles):
-                out_ref[pl.ds(copy * tiles + spots_ref[before + block], 1), :] = row
+            put(before + block, observed(levels, rows, origin_ref, packed_ref, block, split))
 
         before += packed_ref.shape[0]
 
@@ -257,12 +273,12 @@
     matrix = pl.pallas_call(
         matrix_kernel,
         out_shape=jax.ShapeDtypeStruct((kinds, all_cols, 2 * cols), BF16),
-        in_specs=[SMEM, SMEM, VMEM, VMEM],
+        in_specs=[SMEM, VMEM, VMEM, VMEM],
         out_specs=VMEM,
         **params(8 * kinds * all_cols * cols, 4 * kinds * all_cols * cols, 5 * kinds * all_cols * cols),
     )(
         lons * cols,
-        log,
+        log[:, None],
         ends(lon),
         jnp.stack([ends(source(lon, s, n_lon)).T for s in range(n_lon)]),
     )
@@ -297,16 +313,10 @@
     places = jnp.stack([fine_row, fine_col]).astype(F32)
     packed = jnp.concatenate([weights, places, jnp.zeros((6, slots), F32)])
 
-    edges = edge[None]
-    step = 1
-    while step < n_lat and paired(n_lat):
-        edges = jnp.concatenate([edges, send(edges, "lat", step)])
-        if step == 1:
-            packed = lax.optimization_barrier((packed, edges))[0]
-        step *= 2
-    if not paired(n_lat):
-        edges = collect(edge, "lat")
-    packed = [packed] + [send(packed, "lat", s) for s in range(1, n_lat)]
+    edges = [edge] + [send(edge, "lat", s) for s in range(1, n_lat)]
+    near = [packed[None]] + [send(packed[None], "lon", s) for s in range(1, n_lon)]
+    edges = jnp.stack(edges)
+    packed = [send(packed, "lat", s) for s in range(1, n_lat)]
     lats = jnp.stack([source(lat, s, n_lat) for s in range(n_lat)]).astype(jnp.int32)
     chunks = jnp.stack([toward(mem, r, n_mem) for r in range(n_mem)]).astype(jnp.int32)
     chunk_shape = jax.ShapeDtypeStruct((share * rows, cols), F32)
@@ -330,24 +340,41 @@
 
 
     tiles = n_lat * n_lon
-    packed = jnp.stack(lax.optimization_barrier((packed, sums[0]))[0])
-    packs = [packed] + [send(packed, "lon", s) for s in range(1, n_lon)]
+    origin = jnp.stack([lat * rows, lon * cols]).astype(jnp.int32)
+    block_flops, block_size = 2 * levels * rows * cols * slots, 4 * (levels + 8) * slots
+    equal, split = pl.pallas_call(
+        functools.partial(near_kernel, levels, rows),
+        out_shape=(
+            jax.ShapeDtypeStruct((n_lon, slots), F32),
+            jax.ShapeDtypeStruct((levels * rows, 2 * cols), BF16),
+        ),
+        in_specs=[SMEM] * 2 + [VMEM] * (n_mem + n_lon),
+        out_specs=(VMEM, VMEM),
+        **params(
+            n_lon * block_flops, 2**20, 8 * levels * rows * cols + n_lon * block_size
+        ),
+    )(chunks, origin, *sums, *near)
+    packs = []
+    if n_lat > 1:
+        packed = jnp.stack(lax.optimization_barrier((packed, equal))[0])
+        packs = [packed] + [send(packed, "lon", s) for s in range(1, n_lon)]
     equal = pl.pallas_call(
-        functools.partial(observe_kernel, levels, rows),
+        functools.partial(far_kernel, levels, rows),
         out_shape=jax.ShapeDtypeStruct((n_mem * tiles, slots), F32),
-        in_specs=[SMEM] * 3 + [VMEM] * (n_mem + n_lon),
+        in_specs=[SMEM] * 2 + [VMEM] * (2 + len(packs)),
         out_specs=VMEM,
-        scratch_shapes=[pltpu.VMEM((levels * rows, 2 * cols), BF16)],
         **params(
-            4 * levels * rows * cols * tiles * slots,
+            (tiles - n_lon) * block_flops,
             4 * 2**20,
-            8 * levels * rows * cols + packed.size * n_lon * 4 + n_mem * tiles * slots * 4,
+            4 * levels * rows * cols + tiles * block_size + n_mem * tiles * slots * 4,
         ),
     )(
-        chunks,
-        jnp.stack([lat * rows, lon * cols]).astype(jnp.int32),
-        (lats[None, :] * n_lon + lons[:, None]).reshape(-1),
-        *sums,
+        origin,
+        jnp.concatenate(
+            [lats[0] * n_lon + lons, (lats[None, 1:] * n_lon + lons[:, None]).reshape(-1)]
+        ),
+        split,
+        equal,
         *packs,
     )
 

time: 51.7 us -> 48.4 us (0.936)
  waiting for transfers between devices: 6.45 us -> 4.3 us
  blocking collectives: 15 us -> 13.2 us
    ppermute x10 -> x12, waiting for transfers between devices: 6.45 us -> 4.3 us  [send(): lax.ppermute(block, axis, [(i, toward(i, step, count)) for i in range(cou...]
    all_to_all x1, blocking collectives: 15 us -> 13.2 us  [per_device(): back = lax.all_to_all(leaving, ('mem', 'lat', 'lon'), 0, 0, tiled=True)]
    pallas_call x1 -> x2, Pallas kernels: 6.85 us -> 7.27 us  [the longest x1 5.2 us: per_device(): pl.pallas_call(functools.partial(far_kernel, levels, rows), out_shape=jax...]
    ppermute x10 -> x12, starting transfers between devices: 13.3 us -> 13.1 us  [send(): lax.ppermute(block, axis, [(i, toward(i, step, count)) for i in range(cou...]
  transfers between devices with their start and end apart: 10 -> 12, of which waited for: 4 -> 3; matrix products, arithmetic and copies ran while one was open for 4% -> 4% of each run, Pallas kernels for 21% -> 23%
where the time goes in v4:
time: 48.4 us; the launch traced here: 48.2 us
  blocking collectives  13.2 us (27%)
  starting transfers between devices  13.1 us (27%)
  Pallas kernels  12.6 us (26%)
  waiting for transfers between devices  4.3 us (9%)
  other arithmetic  2.84 us (6%)
  between operations  1.56 us (3%)
  local copies, waits for them, and re-layouts  0.54 us (1%)
    all_to_all x1, blocking collectives, per_device(): back = lax.all_to_all(leaving, ('mem', 'lat', 'lon'), 0, 0, tiled=True)  13.2 us
    ppermute x12, starting transfers between devices, send(): lax.ppermute(block, axis, [(i, toward(i, step, count)) for i in range(cou...  13.1 us
    pallas_call x1, Pallas kernels, per_device(): pl.pallas_call(functools.partial(far_kernel, levels, rows), out_shape=jax...  5.2 us
    ppermute x12, waiting for transfers between devices, send(): lax.ppermute(block, axis, [(i, toward(i, step, count)) for i in range(cou...  4.3 us
    pallas_call x1, Pallas kernels, per_device(): pl.pallas_call(functools.partial(sum_kernel, 1.0 / math.sqrt(members * n_...  2.61 us
    pallas_call x1, Pallas kernels, per_device(): pl.pallas_call(functools.partial(near_kernel, levels, rows), out_shape=(j...  2.06 us
    pallas_call x1, Pallas kernels, per_device(): pl.pallas_call(matrix_kernel, out_shape=jax.ShapeDtypeStruct((kinds, all_...  1.37 us
    convert_element_type x1, other arithmetic, per_device(): whole = control.astype(F32)  1.22 us
  transfers between devices with their start and end apart: 12, of which 3 were waited for; matrix products, arithmetic and copies ran while one was open for 4% of the time, Pallas kernels for 23%

profile of v4, /device:TPU:0, one launch (start us, length us, event | category | flops | bytes accessed | tf_op | source)
XLA Modules:
  0.0 48.2 jit_solution(6795815556524467116)
XLA Ops:
  0.6 1.2 %convert_element_type.24 = f32[4,16,32,128]{3,2,1,0:T(8,128)S(1)} convert(bf16[4,16,32,128]{3,2,1,0:T(8,128)(2,1)} %own_ref.1) | non-fusion elementwise | flops 262144 | bytes 1572864 | tf_op jit(solution)/shard_map/convert_element_type | solution.py:286
  1.9 0.5 %collective-permute-start = (f32[4,16,32,128]{3,2,1,0:T(8,128)S(1)}, f32[4,16,32,128]{3,2,1,0:T(8,128)S(1)}, u32[]{:S(2)}, u32[]{:S(2)}) collective-permute-start(f32[4,16,32,128]{3,2,1,0:T(8,128)S(1)} %convert_element_type.24), channel_id=1, source_target_pairs={{0,1},{1,0},{2,3},{3,2},{4,5},{5,4},{6,7},{7,6},{8,9},{9,8},{10,11... | collective-permute-start | bytes 3145736 | tf_op jit(solution)/shard_map/ppermute | solution.py:37
  2.4 0.7 %subtract_multiply_fusion = (f32[16]{0:T(128)S(1)}, f32[16]{0:T(128)S(1)}) fusion(f32[16]{0:T(128)} %param.11), kind=kLoop, calls=%fused_computation.45 | loop fusion | flops 48 | bytes 192 | tf_op jit(solution)/shard_map/mul | solution.py:271
  3.1 0.1 negate_multiply_fusion.1
  3.2 0.1 copy.15.from_ref
  3.3 0.1 copy.14.log_ref
  3.4 0.1 copy.13
  4.1 0.1 pad.5.clone
  4.2 0.1 broadcast_multiply_fusion
  4.3 0.1 negate_multiply_fusion.2.to_ref
  4.4 1.4 %shard_map.104.matrix_ref = bf16[16,256,256]{2,1,0:T(8,128)(2,1)S(1)} custom-call(s32[2]{0:T(128)S(1)} %get-tuple-element.40.starts_ref, f32[16,1]{1,0:T(8,128)S(1)} %copy.14.log_ref, f32[16,128]{1,0:T(8,128)S(1)} %negate_multiply_fusion.2.to_ref, f32[2,128,16]{2,1,0:T(8,128)S(1)} %copy.15.from_ref), custom_call_target="tpu_custom_call" | custom-call | flops 4194304 | bytes 2097152 | tf_op jit(solution)/shard_map/pallas_call | solution.py:273
  5.8 0.0 copy-start.5
  5.8 0.0 copy-start.6
  5.8 0.0 copy-start.4
  5.8 0.1 add_multiply_fusion
  5.9 0.1 pad_add_fusion.4.places_ref
  6.0 0.1 pad_add_fusion.origin_ref
  6.0 0.1 pad_add_fusion.3.chunks_ref
  6.1 0.0 copy-start.1
  6.2 0.0 copy-start.2
  6.2 0.6 %shard_map.105 = (f32[2304,128]{1,0:T(8,128)S(1)}, f32[2,64,128]{2,1,0:T(8,128)S(1)}) custom-call(bf16[4,16,32,128]{3,2,1,0:T(8,128)(2,1)S(1)} %copy-done, f32[1,4,16,32,128]{4,3,2,1,0:T(8,128)S(1)} %bitcast.43, bf16[16,256,256]{2,1,0:T(8,128)(2,1)S(1)} %shard_map.104.matrix_ref, f32[64,3]{1,0:T(8,128)S(1)} %bitcast.44), custom_call_target="tpu_custom_call" | custom-call | flops 268435456 | bytes 4194304 | tf_op jit(solution)/shard_map/pallas_call | solution.py:289
  6.8 2.6 %collective-permute-start.1 = (f32[2,64,128]{2,1,0:T(8,128)S(1)}, f32[2,64,128]{2,1,0:T(8,128)S(1)}, u32[]{:S(2)}, u32[]{:S(2)}) collective-permute-start(f32[2,64,128]{2,1,0:T(8,128)S(1)} %get-tuple-element.20), channel_id=1, source_target_pairs={{0,2},{2,0},{4,6},{6,4},{1,3},{3,1},{5,7},{7,5},{8,10},{10,8},{12,... | collective-permute-start | bytes 196616 | tf_op jit(solution)/shard_map/ppermute | solution.py:37
  9.4 1.5 %collective-permute-start.2 = (f32[2,64,128]{2,1,0:T(8,128)S(1)}, f32[2,64,128]{2,1,0:T(8,128)S(1)}, u32[]{:S(2)}, u32[]{:S(2)}) collective-permute-start(f32[2,64,128]{2,1,0:T(8,128)S(1)} %get-tuple-element.20), channel_id=1, source_target_pairs={{0,4},{2,6},{4,0},{6,2},{1,5},{3,7},{5,1},{7,3},{8,12},{10,14},{12... | collective-permute-start | bytes 196616 | tf_op jit(solution)/shard_map/ppermute | solution.py:37
  10.9 0.0 collective-permute-start.3
  11.0 0.1 maximum_maximum_fusion
  11.1 2.0 %collective-permute-start.5 = (f32[72,512]{1,0:T(8,128)S(1)}, f32[72,512]{1,0:T(8,128)S(1)}, u32[]{:S(2)}, u32[]{:S(2)}) collective-permute-start(f32[72,512]{1,0:T(8,128)S(1)} %get-tuple-element.42), channel_id=1, source_target_pairs={{0,2},{2,0},{4,6},{6,4},{1,3},{3,1},{5,7},{7,5},{8,10},{10,8},{12,... | collective-permute-start | bytes 442376 | tf_op jit(solution)/shard_map/ppermute | solution.py:37
  13.1 1.5 %collective-permute-start.6 = (f32[72,512]{1,0:T(8,128)S(1)}, f32[72,512]{1,0:T(8,128)S(1)}, u32[]{:S(2)}, u32[]{:S(2)}) collective-permute-start(f32[72,512]{1,0:T(8,128)S(1)} %get-tuple-element.42), channel_id=1, source_target_pairs={{0,4},{2,6},{4,0},{6,2},{1,5},{3,7},{5,1},{7,3},{8,12},{10,14},{12... | collective-permute-start | bytes 442376 | tf_op jit(solution)/shard_map/ppermute | solution.py:37
  14.6 0.0 collective-permute-done.1
  14.6 0.2 collective-permute-start.7
  14.8 0.0 collective-permute-start.4
  14.8 1.9 %collective-permute-done.3 = f32[2,64,128]{2,1,0:T(8,128)S(1)} collective-permute-done((f32[2,64,128]{2,1,0:T(8,128)S(1)}, f32[2,64,128]{2,1,0:T(8,128)S(1)}, u32[]{:S(2)}, u32[]{:S(2)}) %collective-permute-start.3) | collective-permute-done | bytes 65568 | tf_op jit(solution)/shard_map/ppermute | solution.py:37
  16.8 2.6 %shard_map.106 = (f32[512,128]{1,0:T(8,128)S(1)}, f32[512,128]{1,0:T(8,128)S(1)}, f32[512,128]{1,0:T(8,128)S(1)}, f32[512,128]{1,0:T(8,128)S(1)}) custom-call(s32[4]{0:T(128)S(1)} %pad_add_fusion.4.places_ref, s32[4]{0:T(128)S(1)} %pad_add_fusion.3.chunks_ref, f32[64,3]{1,0:T(8,128)S(1)} %bitcast.45, f32[4,2,64,128]{3,2,1,0:T(8,128)S(1)} %pad_maximum_fusion.1.edges_ref, ...), custom_call_target="tpu_custom_call" | custom-call | flops 402653184 | bytes 6291456 | tf_op jit(solution)/shard_map/pallas_call | solution.py:323
  19.4 0.0 collective-permute-done.4.rest_5_
  19.4 2.1 %shard_map.107 = (f32[2,512]{1,0:T(2,128)S(1)}, bf16[2048,256]{1,0:T(8,128)(2,1)S(1)}) custom-call(s32[4]{0:T(128)S(1)} %pad_add_fusion.3.chunks_ref, s32[2]{0:T(128)S(1)} %pad_add_fusion.origin_ref, f32[512,128]{1,0:T(8,128)S(1)} %get-tuple-element.22.rest_0_, f32[512,128]{1,0:T(8,128)S(1)} %get-tuple-element.23.rest_1_, ...), custom_call_target="tpu_custom_call" | custom-call | flops 536870912 | bytes 1048576 | tf_op jit(solution)/shard_map/pallas_call | solution.py:345
  21.5 0.0 collective-permute-done.6
  21.5 0.6 %collective-permute-done.7 = f32[72,512]{1,0:T(8,128)S(1)} collective-permute-done((f32[72,512]{1,0:T(8,128)S(1)}, f32[72,512]{1,0:T(8,128)S(1)}, u32[]{:S(2)}, u32[]{:S(2)}) %collective-permute-start.7) | collective-permute-done | bytes 147488 | tf_op jit(solution)/shard_map/ppermute | solution.py:37
  22.1 0.1 collective-permute-start.8
  22.2 0.1 broadcast_add_fusion
  22.2 0.1 add.49
  22.3 1.6 %collective-permute-start.9 = (f32[512,128]{1,0:T(8,128)S(1)}, f32[512,128]{1,0:T(8,128)S(1)}, u32[]{:S(2)}, u32[]{:S(2)}) collective-permute-start(f32[512,128]{1,0:T(8,128)S(1)} %get-tuple-element.25.rest_3_), channel_id=1, source_target_pairs={{0,8},{8,0},{16,24},{24,16},{1,9},{9,1},{17,25},{25,17},{2,10},{10... | collective-permute-start | bytes 786440 | tf_op jit(solution)/shard_map/ppermute | solution.py:37
  23.9 0.1 pad_add_fusion.2.spots_ref
  24.0 0.4 collective-permute-start.10
  24.4 5.2 %shard_map.108 = f32[32,512]{1,0:T(8,128)S(1)} custom-call(s32[2]{0:T(128)S(1)} %pad_add_fusion.origin_ref, s32[8]{0:T(128)S(1)} %pad_add_fusion.2.spots_ref, bf16[2048,256]{1,0:T(8,128)(2,1)S(1)} %get-tuple-element.29.split, f32[2,512]{1,0:T(2,128)S(1)} %get-tuple-element.30.near_ref, f32[3,72,512]{2,1,0:T(8,128)S(1)} %pad_maximum_fusion.rest_0_, ...), custom_call_target="tpu_custom_call" | custom-call | flops 1610612736 | bytes 4194304 | tf_op jit(solution)/shard_map/pallas_call | solution.py:361
  29.6 1.8 %collective-permute-done.9 = f32[512,128]{1,0:T(8,128)S(1)} collective-permute-done((f32[512,128]{1,0:T(8,128)S(1)}, f32[512,128]{1,0:T(8,128)S(1)}, u32[]{:S(2)}, u32[]{:S(2)}) %collective-permute-start.9) | collective-permute-done | bytes 262176 | tf_op jit(solution)/shard_map/ppermute | solution.py:37
  31.5 2.7 %collective-permute-start.11 = (f32[512,128]{1,0:T(8,128)S(1)}, f32[512,128]{1,0:T(8,128)S(1)}, u32[]{:S(2)}, u32[]{:S(2)}) collective-permute-start(f32[512,128]{1,0:T(8,128)S(1)} %add.54), channel_id=1, source_target_pairs={{0,16},{8,24},{16,0},{24,8},{1,17},{9,25},{17,1},{25,9},{2,18},{10... | collective-permute-start | bytes 786440 | tf_op jit(solution)/shard_map/ppermute | solution.py:37
  34.1 0.1 copy.16
  34.2 13.2 %all_to_all.11 = f32[32,1,512]{2,1,0:T(1,128)S(1)} all-to-all(f32[32,1,512]{2,1,0:T(1,128)S(1)} %copy.16), channel_id=1, replica_groups=mesh['mem'=4,'lat'=4,'lon'=2] {'mem','lat','lon'}, dimensions={0} | all-to-all | bytes 131072 | tf_op jit(solution)/shard_map/all_to_all | solution.py:397
  47.5 0.8 %shard_map.109 = (f32[512,128]{1,0:T(8,128)}, f32[1,512]{1,0:T(1,128)}) custom-call(s32[1]{0:T(128)} %copy.20.count_ref, f32[1,512]{1,0:T(1,128)S(1)} %bitcast.50, f32[32,512]{1,0:T(8,128)S(1)} %bitcast.46, f32[512,128]{1,0:T(8,128)S(1)} %get-tuple-element.22.rest_0_, f32[512,128]{1,0:T(8,128)S(1)} %collective-permute-done.10.rest_1_, ...), custom_call_target="tpu_custom_call" | custom-call | flops 196608 | bytes 1572864 | tf_op jit(solution)/shard_map/pallas_call | solution.py:398
  (30 shorter events, 0.2 us)
Async XLA Ops:
  0.6 5.5 %copy-start = (bf16[4,16,32,128]{3,2,1,0:T(8,128)(2,1)S(1)}, bf16[4,16,32,128]{3,2,1,0:T(8,128)(2,1)}, u32[]{:S(2)}) copy-start(bf16[4,16,32,128]{3,2,1,0:T(8,128)(2,1)} %own_ref.1) | copy-start | bytes 1572868
  1.9 4.3 %collective-permute-start = (f32[4,16,32,128]{3,2,1,0:T(8,128)S(1)}, f32[4,16,32,128]{3,2,1,0:T(8,128)S(1)}, u32[]{:S(2)}, u32[]{:S(2)}) collective-permute-start(f32[4,16,32,128]{3,2,1,0:T(8,128)S(1)} %convert_element_type.24), channel_id=1, source_target_pairs={{0,1},{1,0},{2,3},{3,2},{4,5},{5,4},{6,7},{7,6},{8,9},{9,8},{10,11... | collective-permute-start | bytes 3145736 | tf_op jit(solution)/shard_map/ppermute | solution.py:37
  5.8 5.1 %copy-start.5 = (s32[512,1]{0,1:T(1,128)S(1)}, s32[512,1]{0,1:T(1,128)}, u32[]{:S(2)}) copy-start(s32[512,1]{0,1:T(1,128)} %param.15) | copy-start | bytes 6148
  5.8 5.1 %copy-start.6 = (s32[512]{0:T(512)S(1)}, s32[512]{0:T(512)}, u32[]{:S(2)}) copy-start(s32[512]{0:T(512)} %param.16) | copy-start | bytes 6148
  5.8 5.2 %copy-start.4 = (bf16[512,64]{0,1:T(8,128)(2,1)S(1)}, bf16[512,64]{0,1:T(8,128)(2,1)}, u32[]{:S(2)}) copy-start(bf16[512,64]{0,1:T(8,128)(2,1)} %param.13) | copy-start | bytes 196612
  6.1 10.6 %copy-start.1 = (bf16[4,64,32,128]{3,2,1,0:T(8,128)(2,1)S(1)}, bf16[4,64,32,128]{3,2,1,0:T(8,128)(2,1)}, u32[]{:S(2)}) copy-start(bf16[4,64,32,128]{3,2,1,0:T(8,128)(2,1)} %pert_ref.1) | copy-start | bytes 6291460
  6.2 10.6 %copy-start.2 = (f32[64,16]{0,1:T(8,128)S(1)}, f32[64,16]{0,1:T(8,128)}, u32[]{:S(2)}) copy-start(f32[64,16]{0,1:T(8,128)} %param.12) | copy-start | bytes 12292
  6.8 7.8 %collective-permute-start.1 = (f32[2,64,128]{2,1,0:T(8,128)S(1)}, f32[2,64,128]{2,1,0:T(8,128)S(1)}, u32[]{:S(2)}, u32[]{:S(2)}) collective-permute-start(f32[2,64,128]{2,1,0:T(8,128)S(1)} %get-tuple-element.20), channel_id=1, source_target_pairs={{0,2},{2,0},{4,6},{6,4},{1,3},{3,1},{5,7},{7,5},{8,10},{10,8},{12,... | collective-permute-start | bytes 196616 | tf_op jit(solution)/shard_map/ppermute | solution.py:37
  9.4 5.4 %collective-permute-start.2 = (f32[2,64,128]{2,1,0:T(8,128)S(1)}, f32[2,64,128]{2,1,0:T(8,128)S(1)}, u32[]{:S(2)}, u32[]{:S(2)}) collective-permute-start(f32[2,64,128]{2,1,0:T(8,128)S(1)} %get-tuple-element.20), channel_id=1, source_target_pairs={{0,4},{2,6},{4,0},{6,2},{1,5},{3,7},{5,1},{7,3},{8,12},{10,14},{12... | collective-permute-start | bytes 196616 | tf_op jit(solution)/shard_map/ppermute | solution.py:37
  10.9 5.9 %collective-permute-start.3 = (f32[2,64,128]{2,1,0:T(8,128)S(1)}, f32[2,64,128]{2,1,0:T(8,128)S(1)}, u32[]{:S(2)}, u32[]{:S(2)}) collective-permute-start(f32[2,64,128]{2,1,0:T(8,128)S(1)} %get-tuple-element.20), channel_id=1, source_target_pairs={{0,6},{2,4},{4,2},{6,0},{1,7},{3,5},{5,3},{7,1},{8,14},{10,12},{12... | collective-permute-start | bytes 196616 | tf_op jit(solution)/shard_map/ppermute | solution.py:37
  11.1 10.4 %collective-permute-start.5 = (f32[72,512]{1,0:T(8,128)S(1)}, f32[72,512]{1,0:T(8,128)S(1)}, u32[]{:S(2)}, u32[]{:S(2)}) collective-permute-start(f32[72,512]{1,0:T(8,128)S(1)} %get-tuple-element.42), channel_id=1, source_target_pairs={{0,2},{2,0},{4,6},{6,4},{1,3},{3,1},{5,7},{7,5},{8,10},{10,8},{12,... | collective-permute-start | bytes 442376 | tf_op jit(solution)/shard_map/ppermute | solution.py:37
  13.1 8.4 %collective-permute-start.6 = (f32[72,512]{1,0:T(8,128)S(1)}, f32[72,512]{1,0:T(8,128)S(1)}, u32[]{:S(2)}, u32[]{:S(2)}) collective-permute-start(f32[72,512]{1,0:T(8,128)S(1)} %get-tuple-element.42), channel_id=1, source_target_pairs={{0,4},{2,6},{4,0},{6,2},{1,5},{3,7},{5,1},{7,3},{8,12},{10,14},{12... | collective-permute-start | bytes 442376 | tf_op jit(solution)/shard_map/ppermute | solution.py:37
  14.6 7.5 %collective-permute-start.7 = (f32[72,512]{1,0:T(8,128)S(1)}, f32[72,512]{1,0:T(8,128)S(1)}, u32[]{:S(2)}, u32[]{:S(2)}) collective-permute-start(f32[72,512]{1,0:T(8,128)S(1)} %get-tuple-element.42), channel_id=1, source_target_pairs={{0,6},{2,4},{4,2},{6,0},{1,7},{3,5},{5,3},{7,1},{8,14},{10,12},{12... | collective-permute-start | bytes 442376 | tf_op jit(solution)/shard_map/ppermute | solution.py:37
  14.8 4.6 %collective-permute-start.4 = (f32[1,72,512]{2,1,0:T(8,128)S(1)}, f32[1,72,512]{2,1,0:T(8,128)S(1)}, u32[]{:S(2)}, u32[]{:S(2)}) collective-permute-start(f32[1,72,512]{2,1,0:T(8,128)S(1)} %get-tuple-element.43.rest_4_), channel_id=1, source_target_pairs={{0,1},{1,0},{2,3},{3,2},{4,5},{5,4},{6,7},{7,6},{8,9},{9,8},{10,11... | collective-permute-start | bytes 442376 | tf_op jit(solution)/shard_map/ppermute | solution.py:37
  22.1 2.3 %collective-permute-start.8 = (f32[3,72,512]{2,1,0:T(8,128)S(1)}, f32[3,72,512]{2,1,0:T(8,128)S(1)}, u32[]{:S(2)}, u32[]{:S(2)}) collective-permute-start(f32[3,72,512]{2,1,0:T(8,128)S(1)} %pad_maximum_fusion.rest_0_), channel_id=1, source_target_pairs={{0,1},{1,0},{2,3},{3,2},{4,5},{5,4},{6,7},{7,6},{8,9},{9,8},{10,11... | collective-permute-start | bytes 1327112 | tf_op jit(solution)/shard_map/ppermute | solution.py:37
  22.3 9.1 %collective-permute-start.9 = (f32[512,128]{1,0:T(8,128)S(1)}, f32[512,128]{1,0:T(8,128)S(1)}, u32[]{:S(2)}, u32[]{:S(2)}) collective-permute-start(f32[512,128]{1,0:T(8,128)S(1)} %get-tuple-element.25.rest_3_), channel_id=1, source_target_pairs={{0,8},{8,0},{16,24},{24,16},{1,9},{9,1},{17,25},{25,17},{2,10},{10... | collective-permute-start | bytes 786440 | tf_op jit(solution)/shard_map/ppermute | solution.py:37
  24.0 23.5 %collective-permute-start.10 = (f32[512,128]{1,0:T(8,128)S(1)}, f32[512,128]{1,0:T(8,128)S(1)}, u32[]{:S(2)}, u32[]{:S(2)}) collective-permute-start(f32[512,128]{1,0:T(8,128)S(1)} %get-tuple-element.23.rest_1_), channel_id=1, source_target_pairs={{0,8},{8,0},{16,24},{24,16},{1,9},{9,1},{17,25},{25,17},{2,10},{10... | collective-permute-start | bytes 786440 | tf_op jit(solution)/shard_map/ppermute | solution.py:37
  24.4 23.0 %copy-start.3 = (f32[512]{0:T(512)S(1)}, f32[512]{0:T(512)}, u32[]{:S(2)}) copy-start(f32[512]{0:T(512)} %param.14) | copy-start | bytes 6148
  31.5 16.0 %collective-permute-start.11 = (f32[512,128]{1,0:T(8,128)S(1)}, f32[512,128]{1,0:T(8,128)S(1)}, u32[]{:S(2)}, u32[]{:S(2)}) collective-permute-start(f32[512,128]{1,0:T(8,128)S(1)} %add.54), channel_id=1, source_target_pairs={{0,16},{8,24},{16,0},{24,8},{1,17},{9,25},{17,1},{25,9},{2,18},{10... | collective-permute-start | bytes 786440 | tf_op jit(solution)/shard_map/ppermute | solution.py:37

commit v5 on v4

--- a/solution.py
+++ b/solution.py
@@ -54,17 +54,32 @@
     return high, (value - high.astype(F32)).astype(BF16)
 
 
-def matrix_kernel(starts_ref, log_ref, to_ref, from_ref, matrix_ref):
+def matrix_kernel(starts_ref, log_ref, log_row_ref, to_ref, from_ref, matrix_ref):
     sources, cols, modes = from_ref.shape
-    across = lax.broadcasted_iota(jnp.int32, (cols, cols), 1) + starts_ref[0]
-    for s in range(sources):
-        down = lax.broadcasted_iota(jnp.int32, (cols, cols), 0) + starts_ref[s]
-        distance = jnp.abs(across - down).astype(F32)
+    own = starts_ref[0]
+
+    def put(s, k, value):
+        high, low = halve(value)
+        matrix_ref[k, s * cols : (s + 1) * cols, :] = jnp.concatenate([high, low], axis=1)
+
+    across = lax.broadcasted_iota(jnp.int32, (cols, cols), 1)
+    down = lax.broadcasted_iota(jnp.int32, (cols, cols), 0)
+    distance = jnp.abs(across - down).astype(F32)
+    for k in range(modes):
+        end = jnp.where(across >= down, to_ref[k : k + 1, :], from_ref[0, :, k : k + 1])
+        put(0, k, jnp.exp(distance * log_ref[k : k + 1, :1]) * end)
+    for s in range(1, sources):
+        there = starts_ref[s]
+        between = jnp.maximum(own, there)
+        before = there < own
+        row = own + lax.broadcasted_iota(jnp.int32, (modes, cols), 1) - between
+        row = jnp.exp(jnp.abs(row).astype(F32) * log_ref[...])
+        row = row * jnp.where(before, to_ref[...], 1.0)
+        column = there + lax.broadcasted_iota(jnp.int32, (cols, modes), 0) - between
+        column = jnp.exp(jnp.abs(column).astype(F32) * log_row_ref[...])
+        column = column * jnp.where(before, 1.0, from_ref[s])
         for k in range(modes):
-            end = jnp.where(across >= down, to_ref[k : k + 1, :], from_ref[s, :, k : k + 1])
-            high, low = halve(jnp.exp(distance * log_ref[k : k + 1, :1]) * end)
-            at = s * cols
-            matrix_ref[k, at : at + cols, :] = jnp.concatenate([high, low], axis=1)
+            put(s, k, column[:, k : k + 1] * row[k : k + 1, :])
 
 
 def columns_kernel(own_ref, other_ref, matrix_ref, table_ref, field_ref, edge_ref, first):
@@ -228,15 +243,14 @@
         before += packed_ref.shape[0]
 
 
-def finish_kernel(count_ref, innovation_ref, back_ref, *rest):
+def finish_kernel(valid_ref, innovation_ref, back_ref, *rest):
     parts, (increment_ref, departures_ref) = rest[:-2], rest[-2:]
     total = parts[0][...]
     for part in parts[1:]:
         total = total + part[...]
     increment_ref[...] = total
     equal = jnp.sum(back_ref[...], axis=0, keepdims=True)
-    place = lax.broadcasted_iota(jnp.int32, equal.shape, 1)
-    departures_ref[...] = jnp.where(place < count_ref[0], innovation_ref[...] - equal, 0.0)
+    departures_ref[...] = jnp.where(valid_ref[...] > 0.0, innovation_ref[...] - equal, 0.0)
 
 
 def per_device(
@@ -273,12 +287,13 @@
     matrix = pl.pallas_call(
         matrix_kernel,
         out_shape=jax.ShapeDtypeStruct((kinds, all_cols, 2 * cols), BF16),
-        in_specs=[SMEM, VMEM, VMEM, VMEM],
+        in_specs=[SMEM] + [VMEM] * 4,
         out_specs=VMEM,
         **params(8 * kinds * all_cols * cols, 4 * kinds * all_cols * cols, 5 * kinds * all_cols * cols),
     )(
         lons * cols,
         log[:, None],
+        log[None],
         ends(lon),
         jnp.stack([ends(source(lon, s, n_lon)).T for s in range(n_lon)]),
     )
@@ -302,14 +317,13 @@
         ),
     )(control, others, matrix, table)
 
-    obs_weights, obs_tile, obs_column, _ = lax.optimization_barrier(
-        (obs_weights, obs_tile, obs_column, edge)
-    )
-    valid = jnp.arange(slots, dtype=jnp.int32) < obs_count[0]
+    obs_weights, obs_tile, obs_column, slot, _ = lax.optimization_barrier(
+        (obs_weights, obs_tile, obs_column, jnp.arange(slots, dtype=jnp.int32), edge)
+    )
     target = obs_tile[:, 0]
     fine_row = target // n_lon * (2 * rows) + obs_column // (2 * cols)
     fine_col = target % n_lon * (2 * cols) + obs_column % (2 * cols)
-    weights = jnp.where(valid[:, None], obs_weights.astype(F32), 0.0).T
+    weights = obs_weights.astype(F32).T
     places = jnp.stack([fine_row, fine_col]).astype(F32)
     packed = jnp.concatenate([weights, places, jnp.zeros((6, slots), F32)])
 
@@ -398,14 +412,14 @@
     increment, departures = pl.pallas_call(
         finish_kernel,
         out_shape=(chunk_shape, jax.ShapeDtypeStruct((1, slots), F32)),
-        in_specs=[SMEM] + [VMEM] * (2 + len(held[0])),
+        in_specs=[VMEM] * (3 + len(held[0])),
         out_specs=(VMEM, VMEM),
         **params(
             len(held[0]) * share * rows * cols,
             8 * len(held[0]) * share * rows * cols,
             8 * (len(held[0]) + 1) * share * rows * cols + 8 * n_mem * tiles * slots,
         ),
-    )(obs_count, innovation[None], back, *held[0])
+    )((slot < obs_count[0]).astype(F32)[None], innovation[None], back, *held[0])
     increment, departures = increment.reshape(share, rows, cols), departures[0]
     return (increment, departures)
 

time: 48.4 us -> 47.7 us (0.986)
  blocking collectives: 13.2 us -> 0 us
  waiting for transfers between devices: 4.3 us -> 13.7 us
  starting transfers between devices: 13.1 us -> 15.7 us
  local copies, waits for them, and re-layouts: 0.54 us -> 1.18 us
    all_to_all x1 -> x0, blocking collectives: 13.2 us -> none  [per_device(): back = lax.all_to_all(leaving, ('mem', 'lat', 'lon'), 0, 0, tiled=True)]
    all_to_all x0 -> x1, waiting for transfers between devices: none -> 9.37 us  [per_device(): back = lax.all_to_all(leaving, ('mem', 'lat', 'lon'), 0, 0, tiled=True)]
    all_to_all x0 -> x1, starting transfers between devices: none -> 2.57 us  [per_device(): back = lax.all_to_all(leaving, ('mem', 'lat', 'lon'), 0, 0, tiled=True)]
    another operation x1 -> x2, other arithmetic: 0.01 us -> 0.69 us  [per_device(): table = jnp.tile(jnp.stack([log, rate, beta], axis=1), (members, 1))]
    mul x1, other arithmetic: 0.66 us -> 0.01 us  [ends(): rest * rest]
    all_to_all x1, local copies, waits for them, and re-layouts: 0.07 us -> 0.7 us  [per_device(): back = lax.all_to_all(leaving, ('mem', 'lat', 'lon'), 0, 0, tiled=True)]
  transfers between devices with their start and end apart: 12 -> 13, of which waited for: 3 -> 4; matrix products, arithmetic and copies ran while one was open for 4% -> 6% of each run, Pallas kernels for 23% -> 23%
where the time goes in v5:
time: 47.7 us; the launch traced here: 47.5 us
  starting transfers between devices  15.7 us (33%)
  waiting for transfers between devices  13.7 us (29%)
  Pallas kernels  12.5 us (26%)
  other arithmetic  2.86 us (6%)
  between operations  1.57 us (3%)
  local copies, waits for them, and re-layouts  1.18 us (2%)
    ppermute x12, starting transfers between devices, send(): lax.ppermute(block, axis, [(i, toward(i, step, count)) for i in range(cou...  13.1 us
    all_to_all x1, waiting for transfers between devices, per_device(): back = lax.all_to_all(leaving, ('mem', 'lat', 'lon'), 0, 0, tiled=True)  9.37 us
    pallas_call x1, Pallas kernels, per_device(): pl.pallas_call(functools.partial(far_kernel, levels, rows), out_shape=jax...  5.2 us
    ppermute x12, waiting for transfers between devices, send(): lax.ppermute(block, axis, [(i, toward(i, step, count)) for i in range(cou...  4.3 us
    pallas_call x1, Pallas kernels, per_device(): pl.pallas_call(functools.partial(sum_kernel, 1.0 / math.sqrt(members * n_...  2.61 us
    all_to_all x1, starting transfers between devices, per_device(): back = lax.all_to_all(leaving, ('mem', 'lat', 'lon'), 0, 0, tiled=True)  2.57 us
    pallas_call x1, Pallas kernels, per_device(): pl.pallas_call(functools.partial(near_kernel, levels, rows), out_shape=(j...  2.08 us
    pallas_call x1, Pallas kernels, per_device(): pl.pallas_call(matrix_kernel, out_shape=jax.ShapeDtypeStruct((kinds, all_...  1.26 us
  transfers between devices with their start and end apart: 13, of which 4 were waited for; matrix products, arithmetic and copies ran while one was open for 6% of the time, Pallas kernels for 23%

profile of v5, /device:TPU:0, one launch (start us, length us, event | category | flops | bytes accessed | tf_op | source)
XLA Modules:
  0.0 47.5 jit_solution(1180950215510695790)
XLA Ops:
  0.6 1.2 %convert_element_type.23 = f32[4,16,32,128]{3,2,1,0:T(8,128)S(1)} convert(bf16[4,16,32,128]{3,2,1,0:T(8,128)(2,1)} %own_ref.1) | non-fusion elementwise | flops 262144 | bytes 1572864 | tf_op jit(solution)/shard_map/convert_element_type | solution.py:301
  1.9 0.5 %collective-permute-start = (f32[4,16,32,128]{3,2,1,0:T(8,128)S(1)}, f32[4,16,32,128]{3,2,1,0:T(8,128)S(1)}, u32[]{:S(2)}, u32[]{:S(2)}) collective-permute-start(f32[4,16,32,128]{3,2,1,0:T(8,128)S(1)} %convert_element_type.23), channel_id=1, source_target_pairs={{0,1},{1,0},{2,3},{3,2},{4,5},{5,4},{6,7},{7,6},{8,9},{9,8},{10,11... | collective-permute-start | bytes 3145736 | tf_op jit(solution)/shard_map/ppermute | solution.py:37
  2.4 0.7 %fusion.6 = (f32[16,1]{0,1:T(1,128)S(1)}, f32[16]{0:T(128)S(1)}) fusion(f32[16]{0:T(128)} %param.11), kind=kLoop, calls=%fused_computation.44 | loop fusion | flops 112 | bytes 192 | tf_op jit(solution)/shard_map/stack | solution.py:280
  3.1 0.1 negate_multiply_fusion.1
  3.2 0.1 copy.14.from_ref
  3.3 0.1 copy.13.log_ref
  3.4 0.1 copy.15
  3.5 0.1 pad.5.clone
  3.6 0.1 broadcast_add_fusion.1
  3.7 0.1 negate_multiply_fusion.2.to_ref
  3.7 1.3 %shard_map.104.matrix_ref = bf16[16,256,256]{2,1,0:T(8,128)(2,1)S(1)} custom-call(s32[2]{0:T(128)S(1)} %broadcast_multiply_fusion.1.starts_ref, f32[16,1]{1,0:T(8,128)S(1)} %copy.13.log_ref, f32[1,16]{1,0:T(1,128)S(1)} %get-tuple-element.52.log_row_ref, f32[16,128]{1,0:T(8,128)S(1)} %negate_multiply_fusion.2.to_ref, f32[2,128,16]{2,1,0:T(8,128)S(1)} %copy.14.from_ref), custom_call_target="tpu_custom_call" | custom-call | flops 4194304 | bytes 2097152 | tf_op jit(solution)/shard_map/pallas_call | solution.py:287
  5.0 0.0 copy-start.4
  5.0 0.0 copy-start.5
  5.0 0.0 copy-start.6
  5.0 0.1 pad_add_fusion.1.origin_ref
  5.1 0.1 pad_add_fusion.4.places_ref
  5.2 0.1 pad_add_fusion.3.chunks_ref
  5.3 0.0 copy-start.1
  5.3 0.0 copy-start.2
  5.3 0.6 %shard_map.105 = (f32[2304,128]{1,0:T(8,128)S(1)}, f32[2,64,128]{2,1,0:T(8,128)S(1)}) custom-call(bf16[4,16,32,128]{3,2,1,0:T(8,128)(2,1)S(1)} %copy-done, f32[1,4,16,32,128]{4,3,2,1,0:T(8,128)S(1)} %bitcast.46, bf16[16,256,256]{2,1,0:T(8,128)(2,1)S(1)} %shard_map.104.matrix_ref, f32[64,3]{1,0:T(8,128)S(1)} %bitcast.47), custom_call_target="tpu_custom_call" | custom-call | flops 268435456 | bytes 4194304 | tf_op jit(solution)/shard_map/pallas_call | solution.py:304
  5.9 2.6 %collective-permute-start.1 = (f32[2,64,128]{2,1,0:T(8,128)S(1)}, f32[2,64,128]{2,1,0:T(8,128)S(1)}, u32[]{:S(2)}, u32[]{:S(2)}) collective-permute-start(f32[2,64,128]{2,1,0:T(8,128)S(1)} %get-tuple-element.21), channel_id=1, source_target_pairs={{0,2},{2,0},{4,6},{6,4},{1,3},{3,1},{5,7},{7,5},{8,10},{10,8},{12,... | collective-permute-start | bytes 196616 | tf_op jit(solution)/shard_map/ppermute | solution.py:37
  8.5 1.5 %collective-permute-start.2 = (f32[2,64,128]{2,1,0:T(8,128)S(1)}, f32[2,64,128]{2,1,0:T(8,128)S(1)}, u32[]{:S(2)}, u32[]{:S(2)}) collective-permute-start(f32[2,64,128]{2,1,0:T(8,128)S(1)} %get-tuple-element.21), channel_id=1, source_target_pairs={{0,4},{2,6},{4,0},{6,2},{1,5},{3,7},{5,1},{7,3},{8,12},{10,14},{12... | collective-permute-start | bytes 196616 | tf_op jit(solution)/shard_map/ppermute | solution.py:37
  10.0 0.0 collective-permute-start.3
  10.1 0.1 maximum_maximum_fusion
  10.2 2.0 %collective-permute-start.5 = (f32[72,512]{1,0:T(8,128)S(1)}, f32[72,512]{1,0:T(8,128)S(1)}, u32[]{:S(2)}, u32[]{:S(2)}) collective-permute-start(f32[72,512]{1,0:T(8,128)S(1)} %get-tuple-element.44), channel_id=1, source_target_pairs={{0,2},{2,0},{4,6},{6,4},{1,3},{3,1},{5,7},{7,5},{8,10},{10,8},{12,... | collective-permute-start | bytes 442376 | tf_op jit(solution)/shard_map/ppermute | solution.py:37
  12.2 1.5 %collective-permute-start.6 = (f32[72,512]{1,0:T(8,128)S(1)}, f32[72,512]{1,0:T(8,128)S(1)}, u32[]{:S(2)}, u32[]{:S(2)}) collective-permute-start(f32[72,512]{1,0:T(8,128)S(1)} %get-tuple-element.44), channel_id=1, source_target_pairs={{0,4},{2,6},{4,0},{6,2},{1,5},{3,7},{5,1},{7,3},{8,12},{10,14},{12... | collective-permute-start | bytes 442376 | tf_op jit(solution)/shard_map/ppermute | solution.py:37
  13.8 0.2 collective-permute-start.7
  14.0 1.9 %collective-permute-done.3 = f32[2,64,128]{2,1,0:T(8,128)S(1)} collective-permute-done((f32[2,64,128]{2,1,0:T(8,128)S(1)}, f32[2,64,128]{2,1,0:T(8,128)S(1)}, u32[]{:S(2)}, u32[]{:S(2)}) %collective-permute-start.3) | collective-permute-done | bytes 65568 | tf_op jit(solution)/shard_map/ppermute | solution.py:37
  16.0 2.6 %shard_map.106 = (f32[512,128]{1,0:T(8,128)S(1)}, f32[512,128]{1,0:T(8,128)S(1)}, f32[512,128]{1,0:T(8,128)S(1)}, f32[512,128]{1,0:T(8,128)S(1)}) custom-call(s32[4]{0:T(128)S(1)} %pad_add_fusion.4.places_ref, s32[4]{0:T(128)S(1)} %pad_add_fusion.3.chunks_ref, f32[64,3]{1,0:T(8,128)S(1)} %bitcast.48, f32[4,2,64,128]{3,2,1,0:T(8,128)S(1)} %pad_maximum_fusion.1.edges_ref, ...), custom_call_target="tpu_custom_call" | custom-call | flops 402653184 | bytes 6291456 | tf_op jit(solution)/shard_map/pallas_call | solution.py:337
  18.6 2.1 %shard_map.107 = (f32[2,512]{1,0:T(2,128)S(1)}, bf16[2048,256]{1,0:T(8,128)(2,1)S(1)}) custom-call(s32[4]{0:T(128)S(1)} %pad_add_fusion.3.chunks_ref, s32[2]{0:T(128)S(1)} %pad_add_fusion.1.origin_ref, f32[512,128]{1,0:T(8,128)S(1)} %get-tuple-element.24.rest_0_, f32[512,128]{1,0:T(8,128)S(1)} %get-tuple-element.25.rest_1_, ...), custom_call_target="tpu_custom_call" | custom-call | flops 536870912 | bytes 1048576 | tf_op jit(solution)/shard_map/pallas_call | solution.py:359
  20.7 0.0 collective-permute-done.5
  20.7 0.0 collective-permute-done.6
  20.7 0.5 %collective-permute-done.7 = f32[72,512]{1,0:T(8,128)S(1)} collective-permute-done((f32[72,512]{1,0:T(8,128)S(1)}, f32[72,512]{1,0:T(8,128)S(1)}, u32[]{:S(2)}, u32[]{:S(2)}) %collective-permute-start.7) | collective-permute-done | bytes 147488 | tf_op jit(solution)/shard_map/ppermute | solution.py:37
  21.3 0.1 collective-permute-start.8
  21.3 0.1 add_multiply_fusion
  21.4 0.1 broadcast_add_fusion
  21.5 0.1 add.49
  21.6 1.6 %collective-permute-start.9 = (f32[512,128]{1,0:T(8,128)S(1)}, f32[512,128]{1,0:T(8,128)S(1)}, u32[]{:S(2)}, u32[]{:S(2)}) collective-permute-start(f32[512,128]{1,0:T(8,128)S(1)} %get-tuple-element.27.rest_3_), channel_id=1, source_target_pairs={{0,8},{8,0},{16,24},{24,16},{1,9},{9,1},{17,25},{25,17},{2,10},{10... | collective-permute-start | bytes 786440 | tf_op jit(solution)/shard_map/ppermute | solution.py:37
  23.2 0.1 pad_add_fusion.2.spots_ref
  23.2 0.4 collective-permute-start.10
  23.7 0.0 collective-permute-done.8.rest_1_
  23.7 5.2 %shard_map.108 = f32[32,512]{1,0:T(8,128)S(1)} custom-call(s32[2]{0:T(128)S(1)} %pad_add_fusion.1.origin_ref, s32[8]{0:T(128)S(1)} %pad_add_fusion.2.spots_ref, bf16[2048,256]{1,0:T(8,128)(2,1)S(1)} %get-tuple-element.31.split, f32[2,512]{1,0:T(2,128)S(1)} %get-tuple-element.32.near_ref, f32[3,72,512]{2,1,0:T(8,128)S(1)} %pad_maximum_fusion.rest_0_, ...), custom_call_target="tpu_custom_call" | custom-call | flops 1610612736 | bytes 4194304 | tf_op jit(solution)/shard_map/pallas_call | solution.py:375
  28.9 1.8 %collective-permute-done.9 = f32[512,128]{1,0:T(8,128)S(1)} collective-permute-done((f32[512,128]{1,0:T(8,128)S(1)}, f32[512,128]{1,0:T(8,128)S(1)}, u32[]{:S(2)}, u32[]{:S(2)}) %collective-permute-start.9) | collective-permute-done | bytes 262176 | tf_op jit(solution)/shard_map/ppermute | solution.py:37
  30.7 2.7 %collective-permute-start.11 = (f32[512,128]{1,0:T(8,128)S(1)}, f32[512,128]{1,0:T(8,128)S(1)}, u32[]{:S(2)}, u32[]{:S(2)}) collective-permute-start(f32[512,128]{1,0:T(8,128)S(1)} %add.54), channel_id=1, source_target_pairs={{0,16},{8,24},{16,0},{24,8},{1,17},{9,25},{17,1},{25,9},{2,18},{10... | collective-permute-start | bytes 786440 | tf_op jit(solution)/shard_map/ppermute | solution.py:37
  34.0 0.7 %copy.16 = f32[32,1,512]{2,1,0:T(1,128)} copy(f32[32,1,512]{2,0,1:T(8,128)S(1)} %bitcast.50) | data formatting | bytes 131072 | tf_op jit(solution)/shard_map/all_to_all | solution.py:411
  34.7 2.6 %all-to-all-start = ((f32[32,1,512]{2,1,0:T(1,128)}), f32[32,1,512]{2,1,0:T(1,128)S(1)}, u32[]{:S(2)}, u32[]{:S(2)}) async-start(f32[32,1,512]{2,1,0:T(1,128)} %copy.16), calls=%async_computation | async-start | bytes 131072 | tf_op jit(solution)/shard_map/all_to_all | solution.py:411
  37.3 9.4 %all-to-all-done = f32[32,1,512]{2,1,0:T(1,128)S(1)} async-done(((f32[32,1,512]{2,1,0:T(1,128)}), f32[32,1,512]{2,1,0:T(1,128)S(1)}, u32[]{:S(2)}, u32[]{:S(2)}) %all-to-all-start) | async-done | bytes 65568 | tf_op jit(solution)/shard_map/all_to_all | solution.py:411
  46.7 0.7 %shard_map.109 = (f32[512,128]{1,0:T(8,128)}, f32[1,512]{1,0:T(1,128)}) custom-call(f32[1,512]{1,0:T(1,128)S(1)} %bitcast.53, f32[1,512]{1,0:T(1,128)S(1)} %bitcast.54, f32[32,512]{1,0:T(8,128)S(1)} %bitcast.49, f32[512,128]{1,0:T(8,128)S(1)} %get-tuple-element.24.rest_0_, f32[512,128]{1,0:T(8,128)S(1)} %collective-permute-done.10.rest_1_, ...), custom_call_target="tpu_custom_call" | custom-call | flops 196608 | bytes 1572864 | tf_op jit(solution)/shard_map/pallas_call | solution.py:412
  (32 shorter events, 0.2 us)
Async XLA Ops:
  0.6 4.7 %copy-start = (bf16[4,16,32,128]{3,2,1,0:T(8,128)(2,1)S(1)}, bf16[4,16,32,128]{3,2,1,0:T(8,128)(2,1)}, u32[]{:S(2)}) copy-start(bf16[4,16,32,128]{3,2,1,0:T(8,128)(2,1)} %own_ref.1) | copy-start | bytes 1572868
  1.9 3.4 %collective-permute-start = (f32[4,16,32,128]{3,2,1,0:T(8,128)S(1)}, f32[4,16,32,128]{3,2,1,0:T(8,128)S(1)}, u32[]{:S(2)}, u32[]{:S(2)}) collective-permute-start(f32[4,16,32,128]{3,2,1,0:T(8,128)S(1)} %convert_element_type.23), channel_id=1, source_target_pairs={{0,1},{1,0},{2,3},{3,2},{4,5},{5,4},{6,7},{7,6},{8,9},{9,8},{10,11... | collective-permute-start | bytes 3145736 | tf_op jit(solution)/shard_map/ppermute | solution.py:37
  5.0 5.1 %copy-start.4 = (bf16[512,64]{0,1:T(8,128)(2,1)S(1)}, bf16[512,64]{0,1:T(8,128)(2,1)}, u32[]{:S(2)}) copy-start(bf16[512,64]{0,1:T(8,128)(2,1)} %param.13) | copy-start | bytes 196612
  5.0 5.1 %copy-start.5 = (s32[512,1]{0,1:T(1,128)S(1)}, s32[512,1]{0,1:T(1,128)}, u32[]{:S(2)}) copy-start(s32[512,1]{0,1:T(1,128)} %param.15) | copy-start | bytes 6148
  5.0 5.1 %copy-start.6 = (s32[512]{0:T(512)S(1)}, s32[512]{0:T(512)}, u32[]{:S(2)}) copy-start(s32[512]{0:T(512)} %param.16) | copy-start | bytes 6148
  5.3 10.6 %copy-start.1 = (bf16[4,64,32,128]{3,2,1,0:T(8,128)(2,1)S(1)}, bf16[4,64,32,128]{3,2,1,0:T(8,128)(2,1)}, u32[]{:S(2)}) copy-start(bf16[4,64,32,128]{3,2,1,0:T(8,128)(2,1)} %pert_ref.1) | copy-start | bytes 6291460
  5.3 10.6 %copy-start.2 = (f32[64,16]{0,1:T(8,128)S(1)}, f32[64,16]{0,1:T(8,128)}, u32[]{:S(2)}) copy-start(f32[64,16]{0,1:T(8,128)} %param.12) | copy-start | bytes 12292
  5.9 7.8 %collective-permute-start.1 = (f32[2,64,128]{2,1,0:T(8,128)S(1)}, f32[2,64,128]{2,1,0:T(8,128)S(1)}, u32[]{:S(2)}, u32[]{:S(2)}) collective-permute-start(f32[2,64,128]{2,1,0:T(8,128)S(1)} %get-tuple-element.21), channel_id=1, source_target_pairs={{0,2},{2,0},{4,6},{6,4},{1,3},{3,1},{5,7},{7,5},{8,10},{10,8},{12,... | collective-permute-start | bytes 196616 | tf_op jit(solution)/shard_map/ppermute | solution.py:37
  8.5 5.4 %collective-permute-start.2 = (f32[2,64,128]{2,1,0:T(8,128)S(1)}, f32[2,64,128]{2,1,0:T(8,128)S(1)}, u32[]{:S(2)}, u32[]{:S(2)}) collective-permute-start(f32[2,64,128]{2,1,0:T(8,128)S(1)} %get-tuple-element.21), channel_id=1, source_target_pairs={{0,4},{2,6},{4,0},{6,2},{1,5},{3,7},{5,1},{7,3},{8,12},{10,14},{12... | collective-permute-start | bytes 196616 | tf_op jit(solution)/shard_map/ppermute | solution.py:37
  10.0 5.9 %collective-permute-start.3 = (f32[2,64,128]{2,1,0:T(8,128)S(1)}, f32[2,64,128]{2,1,0:T(8,128)S(1)}, u32[]{:S(2)}, u32[]{:S(2)}) collective-permute-start(f32[2,64,128]{2,1,0:T(8,128)S(1)} %get-tuple-element.21), channel_id=1, source_target_pairs={{0,6},{2,4},{4,2},{6,0},{1,7},{3,5},{5,3},{7,1},{8,14},{10,12},{12... | collective-permute-start | bytes 196616 | tf_op jit(solution)/shard_map/ppermute | solution.py:37
  10.2 10.4 %collective-permute-start.5 = (f32[72,512]{1,0:T(8,128)S(1)}, f32[72,512]{1,0:T(8,128)S(1)}, u32[]{:S(2)}, u32[]{:S(2)}) collective-permute-start(f32[72,512]{1,0:T(8,128)S(1)} %get-tuple-element.44), channel_id=1, source_target_pairs={{0,2},{2,0},{4,6},{6,4},{1,3},{3,1},{5,7},{7,5},{8,10},{10,8},{12,... | collective-permute-start | bytes 442376 | tf_op jit(solution)/shard_map/ppermute | solution.py:37
  12.2 8.4 %collective-permute-start.6 = (f32[72,512]{1,0:T(8,128)S(1)}, f32[72,512]{1,0:T(8,128)S(1)}, u32[]{:S(2)}, u32[]{:S(2)}) collective-permute-start(f32[72,512]{1,0:T(8,128)S(1)} %get-tuple-element.44), channel_id=1, source_target_pairs={{0,4},{2,6},{4,0},{6,2},{1,5},{3,7},{5,1},{7,3},{8,12},{10,14},{12... | collective-permute-start | bytes 442376 | tf_op jit(solution)/shard_map/ppermute | solution.py:37
  13.8 7.5 %collective-permute-start.7 = (f32[72,512]{1,0:T(8,128)S(1)}, f32[72,512]{1,0:T(8,128)S(1)}, u32[]{:S(2)}, u32[]{:S(2)}) collective-permute-start(f32[72,512]{1,0:T(8,128)S(1)} %get-tuple-element.44), channel_id=1, source_target_pairs={{0,6},{2,4},{4,2},{6,0},{1,7},{3,5},{5,3},{7,1},{8,14},{10,12},{12... | collective-permute-start | bytes 442376 | tf_op jit(solution)/shard_map/ppermute | solution.py:37
  14.0 4.6 %collective-permute-start.4 = (f32[1,72,512]{2,1,0:T(8,128)S(1)}, f32[1,72,512]{2,1,0:T(8,128)S(1)}, u32[]{:S(2)}, u32[]{:S(2)}) collective-permute-start(f32[1,72,512]{2,1,0:T(8,128)S(1)} %get-tuple-element.45.rest_4_), channel_id=1, source_target_pairs={{0,1},{1,0},{2,3},{3,2},{4,5},{5,4},{6,7},{7,6},{8,9},{9,8},{10,11... | collective-permute-start | bytes 442376 | tf_op jit(solution)/shard_map/ppermute | solution.py:37
  21.3 2.4 %collective-permute-start.8 = (f32[3,72,512]{2,1,0:T(8,128)S(1)}, f32[3,72,512]{2,1,0:T(8,128)S(1)}, u32[]{:S(2)}, u32[]{:S(2)}) collective-permute-start(f32[3,72,512]{2,1,0:T(8,128)S(1)} %pad_maximum_fusion.rest_0_), channel_id=1, source_target_pairs={{0,1},{1,0},{2,3},{3,2},{4,5},{5,4},{6,7},{7,6},{8,9},{9,8},{10,11... | collective-permute-start | bytes 1327112 | tf_op jit(solution)/shard_map/ppermute | solution.py:37
  21.6 9.1 %collective-permute-start.9 = (f32[512,128]{1,0:T(8,128)S(1)}, f32[512,128]{1,0:T(8,128)S(1)}, u32[]{:S(2)}, u32[]{:S(2)}) collective-permute-start(f32[512,128]{1,0:T(8,128)S(1)} %get-tuple-element.27.rest_3_), channel_id=1, source_target_pairs={{0,8},{8,0},{16,24},{24,16},{1,9},{9,1},{17,25},{25,17},{2,10},{10... | collective-permute-start | bytes 786440 | tf_op jit(solution)/shard_map/ppermute | solution.py:37
  23.2 23.5 %collective-permute-start.10 = (f32[512,128]{1,0:T(8,128)S(1)}, f32[512,128]{1,0:T(8,128)S(1)}, u32[]{:S(2)}, u32[]{:S(2)}) collective-permute-start(f32[512,128]{1,0:T(8,128)S(1)} %get-tuple-element.25.rest_1_), channel_id=1, source_target_pairs={{0,8},{8,0},{16,24},{24,16},{1,9},{9,1},{17,25},{25,17},{2,10},{10... | collective-permute-start | bytes 786440 | tf_op jit(solution)/shard_map/ppermute | solution.py:37
  23.7 23.0 %copy-start.3 = (f32[512]{0:T(512)S(1)}, f32[512]{0:T(512)}, u32[]{:S(2)}) copy-start(f32[512]{0:T(512)} %param.14) | copy-start | bytes 6148
  30.7 16.0 %collective-permute-start.11 = (f32[512,128]{1,0:T(8,128)S(1)}, f32[512,128]{1,0:T(8,128)S(1)}, u32[]{:S(2)}, u32[]{:S(2)}) collective-permute-start(f32[512,128]{1,0:T(8,128)S(1)} %add.54), channel_id=1, source_target_pairs={{0,16},{8,24},{16,0},{24,8},{1,17},{9,25},{17,1},{25,9},{2,18},{10... | collective-permute-start | bytes 786440 | tf_op jit(solution)/shard_map/ppermute | solution.py:37
  34.7 12.0 %all-to-all-start = ((f32[32,1,512]{2,1,0:T(1,128)}), f32[32,1,512]{2,1,0:T(1,128)S(1)}, u32[]{:S(2)}, u32[]{:S(2)}) async-start(f32[32,1,512]{2,1,0:T(1,128)} %copy.16), calls=%async_computation | async-start | bytes 131072 | tf_op jit(solution)/shard_map/all_to_all | solution.py:411

commit v6 on v5

--- a/solution.py
+++ b/solution.py
@@ -236,7 +236,7 @@
         put(i, near_ref[i : i + 1, :])
     for packed_ref in packs:
 
-        @pl.loop(0, packed_ref.shape[0])
+        @pl.loop(0, packed_ref.shape[0], unroll=True)
         def _(block, packed_ref=packed_ref, before=before):
             put(before + block, observed(levels, rows, origin_ref, packed_ref, block, split))
 

time: 47.7 us -> 47.7 us (level)
  waiting for transfers between devices: 13.7 us -> 14.8 us
  Pallas kernels: 12.5 us -> 11.4 us
    ppermute x12, waiting for transfers between devices: 4.3 us -> 5.41 us  [send(): lax.ppermute(block, axis, [(i, toward(i, step, count)) for i in range(cou...]
    pallas_call x1, Pallas kernels: 5.2 us -> 4.09 us  [per_device(): pl.pallas_call(functools.partial(far_kernel, levels, rows), out_shape=jax...]
  transfers between devices with their start and end apart: 13 -> 13, of which waited for: 4 -> 4; matrix products, arithmetic and copies ran while one was open for 6% -> 6% of each run, Pallas kernels for 23% -> 21%
where the time goes in v6:
time: 47.7 us; the launch traced here: 47.5 us
  starting transfers between devices  15.7 us (33%)
  waiting for transfers between devices  14.8 us (31%)
  Pallas kernels  11.4 us (24%)
  other arithmetic  2.86 us (6%)
  between operations  1.57 us (3%)
  local copies, waits for them, and re-layouts  1.18 us (2%)
    ppermute x12, starting transfers between devices, send(): lax.ppermute(block, axis, [(i, toward(i, step, count)) for i in range(cou...  13.1 us
    all_to_all x1, waiting for transfers between devices, per_device(): back = lax.all_to_all(leaving, ('mem', 'lat', 'lon'), 0, 0, tiled=True)  9.37 us
    ppermute x12, waiting for transfers between devices, send(): lax.ppermute(block, axis, [(i, toward(i, step, count)) for i in range(cou...  5.41 us
    pallas_call x1, Pallas kernels, per_device(): pl.pallas_call(functools.partial(far_kernel, levels, rows), out_shape=jax...  4.09 us
    pallas_call x1, Pallas kernels, per_device(): pl.pallas_call(functools.partial(sum_kernel, 1.0 / math.sqrt(members * n_...  2.61 us
    all_to_all x1, starting transfers between devices, per_device(): back = lax.all_to_all(leaving, ('mem', 'lat', 'lon'), 0, 0, tiled=True)  2.57 us
    pallas_call x1, Pallas kernels, per_device(): pl.pallas_call(functools.partial(near_kernel, levels, rows), out_shape=(j...  2.08 us
    pallas_call x1, Pallas kernels, per_device(): pl.pallas_call(matrix_kernel, out_shape=jax.ShapeDtypeStruct((kinds, all_...  1.26 us
  transfers between devices with their start and end apart: 13, of which 4 were waited for; matrix products, arithmetic and copies ran while one was open for 6% of the time, Pallas kernels for 21%

profile of v6, /device:TPU:0, one launch (start us, length us, event | category | flops | bytes accessed | tf_op | source)
XLA Modules:
  0.0 47.5 jit_solution(6569959469076128005)
XLA Ops:
  0.6 1.2 %convert_element_type.23 = f32[4,16,32,128]{3,2,1,0:T(8,128)S(1)} convert(bf16[4,16,32,128]{3,2,1,0:T(8,128)(2,1)} %own_ref.1) | non-fusion elementwise | flops 262144 | bytes 1572864 | tf_op jit(solution)/shard_map/convert_element_type | solution.py:301
  1.9 0.5 %collective-permute-start = (f32[4,16,32,128]{3,2,1,0:T(8,128)S(1)}, f32[4,16,32,128]{3,2,1,0:T(8,128)S(1)}, u32[]{:S(2)}, u32[]{:S(2)}) collective-permute-start(f32[4,16,32,128]{3,2,1,0:T(8,128)S(1)} %convert_element_type.23), channel_id=1, source_target_pairs={{0,1},{1,0},{2,3},{3,2},{4,5},{5,4},{6,7},{7,6},{8,9},{9,8},{10,11... | collective-permute-start | bytes 3145736 | tf_op jit(solution)/shard_map/ppermute | solution.py:37
  2.4 0.7 %fusion.6 = (f32[16,1]{0,1:T(1,128)S(1)}, f32[16]{0:T(128)S(1)}) fusion(f32[16]{0:T(128)} %param.11), kind=kLoop, calls=%fused_computation.44 | loop fusion | flops 112 | bytes 192 | tf_op jit(solution)/shard_map/stack | solution.py:280
  3.1 0.1 negate_multiply_fusion.1
  3.2 0.1 copy.14.from_ref
  3.3 0.1 copy.13.log_ref
  3.4 0.1 copy.15
  3.5 0.1 pad.5.clone
  3.6 0.1 broadcast_add_fusion.1
  3.7 0.1 negate_multiply_fusion.2.to_ref
  3.7 1.3 %shard_map.104.matrix_ref = bf16[16,256,256]{2,1,0:T(8,128)(2,1)S(1)} custom-call(s32[2]{0:T(128)S(1)} %broadcast_multiply_fusion.1.starts_ref, f32[16,1]{1,0:T(8,128)S(1)} %copy.13.log_ref, f32[1,16]{1,0:T(1,128)S(1)} %get-tuple-element.52.log_row_ref, f32[16,128]{1,0:T(8,128)S(1)} %negate_multiply_fusion.2.to_ref, f32[2,128,16]{2,1,0:T(8,128)S(1)} %copy.14.from_ref), custom_call_target="tpu_custom_call" | custom-call | flops 4194304 | bytes 2097152 | tf_op jit(solution)/shard_map/pallas_call | solution.py:287
  5.0 0.0 copy-start.4
  5.0 0.0 copy-start.5
  5.0 0.0 copy-start.6
  5.0 0.1 pad_add_fusion.1.origin_ref
  5.1 0.1 pad_add_fusion.4.places_ref
  5.2 0.1 pad_add_fusion.3.chunks_ref
  5.3 0.0 copy-start.1
  5.3 0.0 copy-start.2
  5.3 0.6 %shard_map.105 = (f32[2304,128]{1,0:T(8,128)S(1)}, f32[2,64,128]{2,1,0:T(8,128)S(1)}) custom-call(bf16[4,16,32,128]{3,2,1,0:T(8,128)(2,1)S(1)} %copy-done, f32[1,4,16,32,128]{4,3,2,1,0:T(8,128)S(1)} %bitcast.46, bf16[16,256,256]{2,1,0:T(8,128)(2,1)S(1)} %shard_map.104.matrix_ref, f32[64,3]{1,0:T(8,128)S(1)} %bitcast.47), custom_call_target="tpu_custom_call" | custom-call | flops 268435456 | bytes 4194304 | tf_op jit(solution)/shard_map/pallas_call | solution.py:304
  5.9 2.6 %collective-permute-start.1 = (f32[2,64,128]{2,1,0:T(8,128)S(1)}, f32[2,64,128]{2,1,0:T(8,128)S(1)}, u32[]{:S(2)}, u32[]{:S(2)}) collective-permute-start(f32[2,64,128]{2,1,0:T(8,128)S(1)} %get-tuple-element.21), channel_id=1, source_target_pairs={{0,2},{2,0},{4,6},{6,4},{1,3},{3,1},{5,7},{7,5},{8,10},{10,8},{12,... | collective-permute-start | bytes 196616 | tf_op jit(solution)/shard_map/ppermute | solution.py:37
  8.5 1.5 %collective-permute-start.2 = (f32[2,64,128]{2,1,0:T(8,128)S(1)}, f32[2,64,128]{2,1,0:T(8,128)S(1)}, u32[]{:S(2)}, u32[]{:S(2)}) collective-permute-start(f32[2,64,128]{2,1,0:T(8,128)S(1)} %get-tuple-element.21), channel_id=1, source_target_pairs={{0,4},{2,6},{4,0},{6,2},{1,5},{3,7},{5,1},{7,3},{8,12},{10,14},{12... | collective-permute-start | bytes 196616 | tf_op jit(solution)/shard_map/ppermute | solution.py:37
  10.0 0.0 collective-permute-start.3
  10.1 0.1 maximum_maximum_fusion
  10.2 2.0 %collective-permute-start.5 = (f32[72,512]{1,0:T(8,128)S(1)}, f32[72,512]{1,0:T(8,128)S(1)}, u32[]{:S(2)}, u32[]{:S(2)}) collective-permute-start(f32[72,512]{1,0:T(8,128)S(1)} %get-tuple-element.44), channel_id=1, source_target_pairs={{0,2},{2,0},{4,6},{6,4},{1,3},{3,1},{5,7},{7,5},{8,10},{10,8},{12,... | collective-permute-start | bytes 442376 | tf_op jit(solution)/shard_map/ppermute | solution.py:37
  12.2 1.5 %collective-permute-start.6 = (f32[72,512]{1,0:T(8,128)S(1)}, f32[72,512]{1,0:T(8,128)S(1)}, u32[]{:S(2)}, u32[]{:S(2)}) collective-permute-start(f32[72,512]{1,0:T(8,128)S(1)} %get-tuple-element.44), channel_id=1, source_target_pairs={{0,4},{2,6},{4,0},{6,2},{1,5},{3,7},{5,1},{7,3},{8,12},{10,14},{12... | collective-permute-start | bytes 442376 | tf_op jit(solution)/shard_map/ppermute | solution.py:37
  13.8 0.2 collective-permute-start.7
  14.0 1.9 %collective-permute-done.3 = f32[2,64,128]{2,1,0:T(8,128)S(1)} collective-permute-done((f32[2,64,128]{2,1,0:T(8,128)S(1)}, f32[2,64,128]{2,1,0:T(8,128)S(1)}, u32[]{:S(2)}, u32[]{:S(2)}) %collective-permute-start.3) | collective-permute-done | bytes 65568 | tf_op jit(solution)/shard_map/ppermute | solution.py:37
  16.0 2.6 %shard_map.106 = (f32[512,128]{1,0:T(8,128)S(1)}, f32[512,128]{1,0:T(8,128)S(1)}, f32[512,128]{1,0:T(8,128)S(1)}, f32[512,128]{1,0:T(8,128)S(1)}) custom-call(s32[4]{0:T(128)S(1)} %pad_add_fusion.4.places_ref, s32[4]{0:T(128)S(1)} %pad_add_fusion.3.chunks_ref, f32[64,3]{1,0:T(8,128)S(1)} %bitcast.48, f32[4,2,64,128]{3,2,1,0:T(8,128)S(1)} %pad_maximum_fusion.1.edges_ref, ...), custom_call_target="tpu_custom_call" | custom-call | flops 402653184 | bytes 6291456 | tf_op jit(solution)/shard_map/pallas_call | solution.py:337
  18.6 2.1 %shard_map.107 = (f32[2,512]{1,0:T(2,128)S(1)}, bf16[2048,256]{1,0:T(8,128)(2,1)S(1)}) custom-call(s32[4]{0:T(128)S(1)} %pad_add_fusion.3.chunks_ref, s32[2]{0:T(128)S(1)} %pad_add_fusion.1.origin_ref, f32[512,128]{1,0:T(8,128)S(1)} %get-tuple-element.24.rest_0_, f32[512,128]{1,0:T(8,128)S(1)} %get-tuple-element.25.rest_1_, ...), custom_call_target="tpu_custom_call" | custom-call | flops 536870912 | bytes 1048576 | tf_op jit(solution)/shard_map/pallas_call | solution.py:359
  20.7 0.0 collective-permute-done.5
  20.7 0.0 collective-permute-done.6
  20.7 0.5 %collective-permute-done.7 = f32[72,512]{1,0:T(8,128)S(1)} collective-permute-done((f32[72,512]{1,0:T(8,128)S(1)}, f32[72,512]{1,0:T(8,128)S(1)}, u32[]{:S(2)}, u32[]{:S(2)}) %collective-permute-start.7) | collective-permute-done | bytes 147488 | tf_op jit(solution)/shard_map/ppermute | solution.py:37
  21.3 0.1 collective-permute-start.8
  21.3 0.1 add_multiply_fusion
  21.4 0.1 broadcast_add_fusion
  21.5 0.1 add.49
  21.6 1.6 %collective-permute-start.9 = (f32[512,128]{1,0:T(8,128)S(1)}, f32[512,128]{1,0:T(8,128)S(1)}, u32[]{:S(2)}, u32[]{:S(2)}) collective-permute-start(f32[512,128]{1,0:T(8,128)S(1)} %get-tuple-element.27.rest_3_), channel_id=1, source_target_pairs={{0,8},{8,0},{16,24},{24,16},{1,9},{9,1},{17,25},{25,17},{2,10},{10... | collective-permute-start | bytes 786440 | tf_op jit(solution)/shard_map/ppermute | solution.py:37
  23.2 0.1 pad_add_fusion.2.spots_ref
  23.2 0.4 collective-permute-start.10
  23.7 0.0 collective-permute-done.8.rest_1_
  23.7 4.1 %shard_map.108 = f32[32,512]{1,0:T(8,128)S(1)} custom-call(s32[2]{0:T(128)S(1)} %pad_add_fusion.1.origin_ref, s32[8]{0:T(128)S(1)} %pad_add_fusion.2.spots_ref, bf16[2048,256]{1,0:T(8,128)(2,1)S(1)} %get-tuple-element.31.split, f32[2,512]{1,0:T(2,128)S(1)} %get-tuple-element.32.near_ref, f32[3,72,512]{2,1,0:T(8,128)S(1)} %pad_maximum_fusion.rest_0_, ...), custom_call_target="tpu_custom_call" | custom-call | flops 1610612736 | bytes 4194304 | tf_op jit(solution)/shard_map/pallas_call | solution.py:375
  27.8 2.9 %collective-permute-done.9 = f32[512,128]{1,0:T(8,128)S(1)} collective-permute-done((f32[512,128]{1,0:T(8,128)S(1)}, f32[512,128]{1,0:T(8,128)S(1)}, u32[]{:S(2)}, u32[]{:S(2)}) %collective-permute-start.9) | collective-permute-done | bytes 262176 | tf_op jit(solution)/shard_map/ppermute | solution.py:37
  30.7 2.7 %collective-permute-start.11 = (f32[512,128]{1,0:T(8,128)S(1)}, f32[512,128]{1,0:T(8,128)S(1)}, u32[]{:S(2)}, u32[]{:S(2)}) collective-permute-start(f32[512,128]{1,0:T(8,128)S(1)} %add.54), channel_id=1, source_target_pairs={{0,16},{8,24},{16,0},{24,8},{1,17},{9,25},{17,1},{25,9},{2,18},{10... | collective-permute-start | bytes 786440 | tf_op jit(solution)/shard_map/ppermute | solution.py:37
  34.0 0.7 %copy.16 = f32[32,1,512]{2,1,0:T(1,128)} copy(f32[32,1,512]{2,0,1:T(8,128)S(1)} %bitcast.50) | data formatting | bytes 131072 | tf_op jit(solution)/shard_map/all_to_all | solution.py:411
  34.7 2.6 %all-to-all-start = ((f32[32,1,512]{2,1,0:T(1,128)}), f32[32,1,512]{2,1,0:T(1,128)S(1)}, u32[]{:S(2)}, u32[]{:S(2)}) async-start(f32[32,1,512]{2,1,0:T(1,128)} %copy.16), calls=%async_computation | async-start | bytes 131072 | tf_op jit(solution)/shard_map/all_to_all | solution.py:411
  37.3 9.4 %all-to-all-done = f32[32,1,512]{2,1,0:T(1,128)S(1)} async-done(((f32[32,1,512]{2,1,0:T(1,128)}), f32[32,1,512]{2,1,0:T(1,128)S(1)}, u32[]{:S(2)}, u32[]{:S(2)}) %all-to-all-start) | async-done | bytes 65568 | tf_op jit(solution)/shard_map/all_to_all | solution.py:411
  46.7 0.7 %shard_map.109 = (f32[512,128]{1,0:T(8,128)}, f32[1,512]{1,0:T(1,128)}) custom-call(f32[1,512]{1,0:T(1,128)S(1)} %bitcast.53, f32[1,512]{1,0:T(1,128)S(1)} %bitcast.54, f32[32,512]{1,0:T(8,128)S(1)} %bitcast.49, f32[512,128]{1,0:T(8,128)S(1)} %get-tuple-element.24.rest_0_, f32[512,128]{1,0:T(8,128)S(1)} %collective-permute-done.10.rest_1_, ...), custom_call_target="tpu_custom_call" | custom-call | flops 196608 | bytes 1572864 | tf_op jit(solution)/shard_map/pallas_call | solution.py:412
  (32 shorter events, 0.2 us)
Async XLA Ops:
  0.6 4.7 %copy-start = (bf16[4,16,32,128]{3,2,1,0:T(8,128)(2,1)S(1)}, bf16[4,16,32,128]{3,2,1,0:T(8,128)(2,1)}, u32[]{:S(2)}) copy-start(bf16[4,16,32,128]{3,2,1,0:T(8,128)(2,1)} %own_ref.1) | copy-start | bytes 1572868
  1.9 3.4 %collective-permute-start = (f32[4,16,32,128]{3,2,1,0:T(8,128)S(1)}, f32[4,16,32,128]{3,2,1,0:T(8,128)S(1)}, u32[]{:S(2)}, u32[]{:S(2)}) collective-permute-start(f32[4,16,32,128]{3,2,1,0:T(8,128)S(1)} %convert_element_type.23), channel_id=1, source_target_pairs={{0,1},{1,0},{2,3},{3,2},{4,5},{5,4},{6,7},{7,6},{8,9},{9,8},{10,11... | collective-permute-start | bytes 3145736 | tf_op jit(solution)/shard_map/ppermute | solution.py:37
  5.0 5.1 %copy-start.4 = (bf16[512,64]{0,1:T(8,128)(2,1)S(1)}, bf16[512,64]{0,1:T(8,128)(2,1)}, u32[]{:S(2)}) copy-start(bf16[512,64]{0,1:T(8,128)(2,1)} %param.13) | copy-start | bytes 196612
  5.0 5.1 %copy-start.5 = (s32[512,1]{0,1:T(1,128)S(1)}, s32[512,1]{0,1:T(1,128)}, u32[]{:S(2)}) copy-start(s32[512,1]{0,1:T(1,128)} %param.15) | copy-start | bytes 6148
  5.0 5.1 %copy-start.6 = (s32[512]{0:T(512)S(1)}, s32[512]{0:T(512)}, u32[]{:S(2)}) copy-start(s32[512]{0:T(512)} %param.16) | copy-start | bytes 6148
  5.3 10.6 %copy-start.1 = (bf16[4,64,32,128]{3,2,1,0:T(8,128)(2,1)S(1)}, bf16[4,64,32,128]{3,2,1,0:T(8,128)(2,1)}, u32[]{:S(2)}) copy-start(bf16[4,64,32,128]{3,2,1,0:T(8,128)(2,1)} %pert_ref.1) | copy-start | bytes 6291460
  5.3 10.6 %copy-start.2 = (f32[64,16]{0,1:T(8,128)S(1)}, f32[64,16]{0,1:T(8,128)}, u32[]{:S(2)}) copy-start(f32[64,16]{0,1:T(8,128)} %param.12) | copy-start | bytes 12292
  5.9 7.8 %collective-permute-start.1 = (f32[2,64,128]{2,1,0:T(8,128)S(1)}, f32[2,64,128]{2,1,0:T(8,128)S(1)}, u32[]{:S(2)}, u32[]{:S(2)}) collective-permute-start(f32[2,64,128]{2,1,0:T(8,128)S(1)} %get-tuple-element.21), channel_id=1, source_target_pairs={{0,2},{2,0},{4,6},{6,4},{1,3},{3,1},{5,7},{7,5},{8,10},{10,8},{12,... | collective-permute-start | bytes 196616 | tf_op jit(solution)/shard_map/ppermute | solution.py:37
  8.5 5.4 %collective-permute-start.2 = (f32[2,64,128]{2,1,0:T(8,128)S(1)}, f32[2,64,128]{2,1,0:T(8,128)S(1)}, u32[]{:S(2)}, u32[]{:S(2)}) collective-permute-start(f32[2,64,128]{2,1,0:T(8,128)S(1)} %get-tuple-element.21), channel_id=1, source_target_pairs={{0,4},{2,6},{4,0},{6,2},{1,5},{3,7},{5,1},{7,3},{8,12},{10,14},{12... | collective-permute-start | bytes 196616 | tf_op jit(solution)/shard_map/ppermute | solution.py:37
  10.0 5.9 %collective-permute-start.3 = (f32[2,64,128]{2,1,0:T(8,128)S(1)}, f32[2,64,128]{2,1,0:T(8,128)S(1)}, u32[]{:S(2)}, u32[]{:S(2)}) collective-permute-start(f32[2,64,128]{2,1,0:T(8,128)S(1)} %get-tuple-element.21), channel_id=1, source_target_pairs={{0,6},{2,4},{4,2},{6,0},{1,7},{3,5},{5,3},{7,1},{8,14},{10,12},{12... | collective-permute-start | bytes 196616 | tf_op jit(solution)/shard_map/ppermute | solution.py:37
  10.2 10.4 %collective-permute-start.5 = (f32[72,512]{1,0:T(8,128)S(1)}, f32[72,512]{1,0:T(8,128)S(1)}, u32[]{:S(2)}, u32[]{:S(2)}) collective-permute-start(f32[72,512]{1,0:T(8,128)S(1)} %get-tuple-element.44), channel_id=1, source_target_pairs={{0,2},{2,0},{4,6},{6,4},{1,3},{3,1},{5,7},{7,5},{8,10},{10,8},{12,... | collective-permute-start | bytes 442376 | tf_op jit(solution)/shard_map/ppermute | solution.py:37
  12.2 8.4 %collective-permute-start.6 = (f32[72,512]{1,0:T(8,128)S(1)}, f32[72,512]{1,0:T(8,128)S(1)}, u32[]{:S(2)}, u32[]{:S(2)}) collective-permute-start(f32[72,512]{1,0:T(8,128)S(1)} %get-tuple-element.44), channel_id=1, source_target_pairs={{0,4},{2,6},{4,0},{6,2},{1,5},{3,7},{5,1},{7,3},{8,12},{10,14},{12... | collective-permute-start | bytes 442376 | tf_op jit(solution)/shard_map/ppermute | solution.py:37
  13.8 7.5 %collective-permute-start.7 = (f32[72,512]{1,0:T(8,128)S(1)}, f32[72,512]{1,0:T(8,128)S(1)}, u32[]{:S(2)}, u32[]{:S(2)}) collective-permute-start(f32[72,512]{1,0:T(8,128)S(1)} %get-tuple-element.44), channel_id=1, source_target_pairs={{0,6},{2,4},{4,2},{6,0},{1,7},{3,5},{5,3},{7,1},{8,14},{10,12},{12... | collective-permute-start | bytes 442376 | tf_op jit(solution)/shard_map/ppermute | solution.py:37
  14.0 4.6 %collective-permute-start.4 = (f32[1,72,512]{2,1,0:T(8,128)S(1)}, f32[1,72,512]{2,1,0:T(8,128)S(1)}, u32[]{:S(2)}, u32[]{:S(2)}) collective-permute-start(f32[1,72,512]{2,1,0:T(8,128)S(1)} %get-tuple-element.45.rest_4_), channel_id=1, source_target_pairs={{0,1},{1,0},{2,3},{3,2},{4,5},{5,4},{6,7},{7,6},{8,9},{9,8},{10,11... | collective-permute-start | bytes 442376 | tf_op jit(solution)/shard_map/ppermute | solution.py:37
  21.3 2.4 %collective-permute-start.8 = (f32[3,72,512]{2,1,0:T(8,128)S(1)}, f32[3,72,512]{2,1,0:T(8,128)S(1)}, u32[]{:S(2)}, u32[]{:S(2)}) collective-permute-start(f32[3,72,512]{2,1,0:T(8,128)S(1)} %pad_maximum_fusion.rest_0_), channel_id=1, source_target_pairs={{0,1},{1,0},{2,3},{3,2},{4,5},{5,4},{6,7},{7,6},{8,9},{9,8},{10,11... | collective-permute-start | bytes 1327112 | tf_op jit(solution)/shard_map/ppermute | solution.py:37
  21.6 9.1 %collective-permute-start.9 = (f32[512,128]{1,0:T(8,128)S(1)}, f32[512,128]{1,0:T(8,128)S(1)}, u32[]{:S(2)}, u32[]{:S(2)}) collective-permute-start(f32[512,128]{1,0:T(8,128)S(1)} %get-tuple-element.27.rest_3_), channel_id=1, source_target_pairs={{0,8},{8,0},{16,24},{24,16},{1,9},{9,1},{17,25},{25,17},{2,10},{10... | collective-permute-start | bytes 786440 | tf_op jit(solution)/shard_map/ppermute | solution.py:37
  23.2 23.5 %collective-permute-start.10 = (f32[512,128]{1,0:T(8,128)S(1)}, f32[512,128]{1,0:T(8,128)S(1)}, u32[]{:S(2)}, u32[]{:S(2)}) collective-permute-start(f32[512,128]{1,0:T(8,128)S(1)} %get-tuple-element.25.rest_1_), channel_id=1, source_target_pairs={{0,8},{8,0},{16,24},{24,16},{1,9},{9,1},{17,25},{25,17},{2,10},{10... | collective-permute-start | bytes 786440 | tf_op jit(solution)/shard_map/ppermute | solution.py:37
  23.7 23.0 %copy-start.3 = (f32[512]{0:T(512)S(1)}, f32[512]{0:T(512)}, u32[]{:S(2)}) copy-start(f32[512]{0:T(512)} %param.14) | copy-start | bytes 6148
  30.7 16.0 %collective-permute-start.11 = (f32[512,128]{1,0:T(8,128)S(1)}, f32[512,128]{1,0:T(8,128)S(1)}, u32[]{:S(2)}, u32[]{:S(2)}) collective-permute-start(f32[512,128]{1,0:T(8,128)S(1)} %add.54), channel_id=1, source_target_pairs={{0,16},{8,24},{16,0},{24,8},{1,17},{9,25},{17,1},{25,9},{2,18},{10... | collective-permute-start | bytes 786440 | tf_op jit(solution)/shard_map/ppermute | solution.py:37
  34.7 12.0 %all-to-all-start = ((f32[32,1,512]{2,1,0:T(1,128)}), f32[32,1,512]{2,1,0:T(1,128)S(1)}, u32[]{:S(2)}, u32[]{:S(2)}) async-start(f32[32,1,512]{2,1,0:T(1,128)} %copy.16), calls=%async_computation | async-start | bytes 131072 | tf_op jit(solution)/shard_map/all_to_all | solution.py:411
